TPU v7x, 32 devices: a whole 2x2x4 slice. The times are simulated.
32 devices in a mesh: brow: 4 (over y, x), bcol: 8 (over z, core).
Axes of the slice: x: 2, y: 2, z: 4, core: 2. Of those that a mesh axis runs over, the one named last changes fastest.
Arguments:
- panel_points: bfloat16 [3, 6144], P(None, ('brow', 'bcol')), may hold values from 0 to 1
- panel_map: int32 [3, 6144], replicated, may hold values from 0 to 2047, as said below
- element_nodes: int32 [125, 1024], P(None, ('brow', 'bcol')), may hold values from 0 to 2047
- element_coef: float32 [1024], P(('brow', 'bcol')), may hold values from 0.1 to 1
- element_matrix: float32 [125, 125], replicated, as said below
- node_mass: float32 [65536], P(('brow', 'bcol')), may hold values from 2 to 4
- forcing: float32 [64, 65536], P(None, ('brow', 'bcol')), may hold values from -6 to 6
- field_start: float32 [64, 65536], P(None, ('brow', 'bcol')), may hold values from -6 to 6
- potential_start: float32 [64, 6144], P(None, ('brow', 'bcol')), may hold values from -6 to 6
Outputs:
- fem_field: float32 [64, 65536], P(None, ('brow', 'bcol'))
- potential: float32 [64, 6144], P(None, ('brow', 'bcol'))
Inputs may be any that keep to these rules, and one draw needn't show every extreme that they name: `panel_map`: row 0 is an index over brow+bcol (brow slowest), row 2 a local node below 2048. In each aligned block of 192 panels every group owns either no panel or exactly 12 of them, whose row 1 values are 0 to 11, each once. `element_nodes`: local node numbers within the element's own group. `element_matrix`: Symmetric.
All inputs are finite; a program needn't handle non-finite values.
Results may differ from a plain program's by a relative error of at most 0.0015.
The roundings to bfloat16 on the way count: a program that leaves them out, or rounds other values in their place, can miss the bound.
Values may be sent and summed in bfloat16 or wider, within the bound.
No kernel may reach another device: no remote copies, remote signals or barrier semaphores. Data moves between devices by JAX's collectives and lax.ppermute only.
A program may use at most 128 MiB of HBM per device.

v0:
```python
import functools
import math

import jax
import jax.numpy as jnp
from jax import lax
from jax.experimental import pallas as pl
from jax.experimental.pallas import tpu as pltpu
from jax.sharding import PartitionSpec as P

RIM = 128
SWEEPS = 3
LANES = 128
LOAD_ROWS = 8
POINT_ROWS = 8
HALVES = 2
GROUP = 4
BLOCKS = 4

wave_number = 20.0
penalty = 0.5

AXES = ("brow", "bcol")
F32 = jnp.float32
BF16 = jnp.bfloat16

SIN_POLY = (3.14159264, -5.16771008, 2.55007752, -0.59829129, 0.07765766)
COS_POLY = (0.99999995, -4.93479283, 4.05841135, -1.33187657, 0.21968961)

MIB = 1024 * 1024


def weight_of(sweep):
    return 1.0 / (1.25 + 0.75 * math.cos(math.pi * (2 * sweep + 1) / (2.0 * SWEEPS)))


def call(kernel, out_shape, cost, limit=16, **more):
    return pl.pallas_call(
        kernel,
        out_shape=out_shape,
        compiler_params=pltpu.CompilerParams(vmem_limit_bytes=limit * MIB),
        cost_estimate=pl.CostEstimate(flops=cost, bytes_accessed=1 << 20, transcendentals=0),
        **more,
    )


def shape_of(shape, dtype):
    return jax.ShapeDtypeStruct(shape, dtype)


def dot(a, b):
    return jnp.dot(a, b, preferred_element_type=F32)


def dot_nt(a, b):
    return lax.dot_general(a, b, (((1,), (1,)), ((), ())), preferred_element_type=F32)


def split_two(value):
    high = value.astype(BF16)
    return high, (value - high.astype(F32)).astype(BF16)


def low_part(value, size):
    return value & (size - 1) if size & (size - 1) == 0 else value % size


def high_part(value, size):
    return value >> (size.bit_length() - 1) if size & (size - 1) == 0 else value // size


def stack_parts(value, parts):
    width = value.shape[1] // parts
    return jnp.concatenate([value[:, i * width : (i + 1) * width] for i in range(parts)], axis=0)


def one_hot_rows(key, rows):
    seen = lax.broadcasted_iota(jnp.int32, (rows, key.shape[1]), 0)
    return jnp.where(seen == key, 1.0, 0.0).astype(BF16)


def pick_part(stacked, part, parts):
    rows = stacked.shape[0] // parts
    picked = stacked[(parts - 1) * rows :]
    for i in reversed(range(parts - 1)):
        picked = jnp.where(part == i, stacked[i * rows : (i + 1) * rows], picked)
    return picked


def gather_nodes(field, nodes, parts):
    width = field.shape[1] // parts
    hot = one_hot_rows(jnp.where(nodes < 0, -1, low_part(nodes, width)), width)
    found = dot(stack_parts(field.astype(BF16), parts), hot)
    return pick_part(found, high_part(nodes, width), parts)


def scatter_nodes(values, nodes, parts, count):
    width = count // parts
    hot = one_hot_rows(jnp.where(nodes < 0, -1, low_part(nodes, width)), width)
    masked = jnp.concatenate(
        [jnp.where(high_part(nodes, width) == i, values, 0.0) for i in range(parts)], axis=0
    ).astype(BF16)
    added = dot_nt(masked, hot)
    rows = values.shape[0]
    return jnp.concatenate([added[i * rows : (i + 1) * rows] for i in range(parts)], axis=1)


def halves_of(slot, rows):
    half = jnp.where(slot >= rows, 1, 0)
    return half, slot - half * rows


def trace_rows(field, nodes, parts, brow, used):
    turned = jnp.transpose(gather_nodes(field, nodes, parts))
    span = turned.shape[0] // brow
    return [
        jnp.concatenate(
            [turned[r * span : r * span + used], turned[r * span + used : r * span + 2 * used]], axis=1
        )
        for r in range(brow)
    ]


def own_panels(map_ref, rank, panel_dev):
    first = rank * panel_dev
    base = (first >> 7) << 7
    window = -(-panel_dev // LANES) * LANES
    near = map_ref[:, pl.ds(pl.multiple_of(base, LANES), window)]
    return jnp.where(first == base, near[:, :panel_dev], near[:, window - panel_dev :])


def load_rows(potential, own_map, devices, slot_rows):
    owner, slot = own_map[0:1], own_map[1:2]
    half, low = halves_of(slot, slot_rows)
    rows = devices * LOAD_ROWS
    key = half * rows + owner * LOAD_ROWS + low
    found = dot_nt(one_hot_rows(key, HALVES * rows), potential.astype(BF16))
    return jnp.concatenate([found[:rows], found[rows:]], axis=1).reshape(devices, LOAD_ROWS, LANES)


def node_tables(map_ref, rank, brow, bcol, panel_dev, slot_rows, stride):
    row_panels = bcol * panel_dev
    row_slots = -(-HALVES * bcol * stride // LANES) * LANES
    lane = lax.broadcasted_iota(jnp.int32, (1, row_panels), 1).astype(F32)
    block = jnp.floor((lane + 0.5) * (1.0 / panel_dev)).astype(jnp.int32)
    row_id = lax.broadcasted_iota(jnp.int32, (8, row_panels), 0)
    tables = []
    for r in range(brow):
        span = slice(r * row_panels, (r + 1) * row_panels)
        owner, slot, node = map_ref[0:1, span], map_ref[1:2, span], map_ref[2:3, span]
        half, low = halves_of(slot, slot_rows)
        key = jnp.where(owner == rank, half * (bcol * stride) + block * stride + low, -1)
        values = jnp.where(
            row_id == 0, high_part(node, 256), jnp.where(row_id == 1, low_part(node, 256), 1)
        ).astype(F32).astype(BF16)
        found = dot_nt(values, one_hot_rows(key, row_slots))
        table = jnp.where(found[2:3] > 0.5, found[0:1] * 256.0 + found[1:2], -1.0)
        tables.append(table.astype(jnp.int32))
    return jnp.concatenate(tables, axis=1)


def point_rows(points):
    row_id = lax.broadcasted_iota(jnp.int32, (POINT_ROWS, LANES), 0)
    each = POINT_ROWS // 3
    width = points.shape[1]
    value = jnp.zeros((POINT_ROWS, LANES), F32)
    for axis in range(3):
        for part in range(-(-width // LANES)):
            piece = points[axis : axis + 1, part * LANES : (part + 1) * LANES]
            short = LANES - piece.shape[1]
            if short:
                piece = jnp.concatenate([piece, jnp.zeros((1, short), F32)], axis=1)
            value = jnp.where(row_id == axis * each + part, piece, value)
    return value


def write_chunks(chunk_ref, pieces, loads, bcol, points=None):
    used = pieces[0].shape[0]
    for r, piece in enumerate(pieces):
        for c in range(bcol):
            device = r * bcol + c
            rows = [piece, loads[device]] + ([] if points is None else [points])
            left = chunk_ref.shape[1] - used - LOAD_ROWS - (0 if points is None else POINT_ROWS)
            if left:
                rows.append(jnp.zeros((left, LANES), F32))
            chunk_ref[device] = jnp.concatenate(rows, axis=0).astype(BF16)


def write_rims(field, even, first_ref, second_ref):
    low = field[:, :RIM]
    high = field[:, field.shape[1] - RIM :]
    first_ref[...] = jnp.where(even, high, low).astype(BF16)
    second_ref[...] = jnp.where(even, low, high).astype(BF16)


def setup_kernel(
    parts, brow, bcol, panel_dev, slot_rows, rank_ref, map_ref, field_ref, potential_ref, points_ref,
    nodes_ref, load_nodes_ref, chunk_ref, rim_first_ref, rim_second_ref,
):
    rank = rank_ref[0]
    tables = functools.partial(node_tables, map_ref, rank, brow, bcol, panel_dev, slot_rows)
    nodes = tables(slot_rows)
    nodes_ref[...] = jnp.broadcast_to(nodes, nodes_ref.shape)
    load_nodes_ref[...] = jnp.broadcast_to(tables(LOAD_ROWS), load_nodes_ref.shape)
    field = field_ref[...]
    write_rims(field, low_part(rank, 2) == 0, rim_first_ref, rim_second_ref)
    loads = load_rows(
        potential_ref[...], own_panels(map_ref, rank, panel_dev), brow * bcol, slot_rows
    )
    pieces = trace_rows(field, nodes, parts, brow, bcol * slot_rows)
    write_chunks(chunk_ref, pieces, loads, bcol, point_rows(points_ref[...].astype(F32)))


def hot_kernel(keys_ref, hot_ref, built_ref, sems):
    groups, width, _ = built_ref.shape
    copies = []
    for group in range(groups):
        for e in range(GROUP):
            key = keys_ref[group * GROUP + e : group * GROUP + e + 1, :]
            built_ref[group, :, e * LANES : (e + 1) * LANES] = one_hot_rows(low_part(key, width), width)
        copies.append(pltpu.make_async_copy(built_ref.at[group], hot_ref.at[group], sems.at[group]))
        copies[-1].start()
    for copy in copies:
        copy.wait()


def rim_correction(value, even, first_ref, second_ref, mass, weight):
    step = weight * penalty
    first, second = first_ref[...].astype(F32), second_ref[...].astype(F32)
    left, right = jnp.where(even, second, first), jnp.where(even, first, second)
    last = value.shape[1] - RIM
    low = value[:, :RIM] + step * left / mass[:, :RIM]
    high = value[:, last:] + step * right / mass[:, last:]
    return jnp.concatenate([low, value[:, RIM:last], high], axis=1)


def received_loads(chunk_ref, used, brow, columns):
    received = chunk_ref[...].astype(F32)[:, used : used + LOAD_ROWS]
    received = received.reshape(received.shape[0] * LOAD_ROWS, LANES)
    span = received.shape[0] // brow
    rows = []
    for r in range(brow):
        piece = received[r * span : (r + 1) * span]
        rows += [piece[:, :columns], piece[:, columns : HALVES * columns]]
    return jnp.transpose(jnp.concatenate(rows, axis=0))


def sweep_kernel(
    parts, weight, weight_before, rank_ref, coef_ref, field_ref, rhs_ref, mass_ref, keys_ref,
    matrix_ref, hot_ref, *more_refs,
):
    if weight_before is not None:
        first_ref, second_ref, out_ref, field_scr, *scratch = more_refs
    else:
        out_ref, *scratch = more_refs
    held_ref, sems, high_ref, low_ref, found_ref, local_ref, product_ref, yhigh_ref, ylow_ref, sum_ref = scratch
    groups = held_ref.shape[0]
    copies = [
        pltpu.make_async_copy(hot_ref.at[group], held_ref.at[group], sems.at[group])
        for group in range(groups)
    ]
    for copy in copies:
        copy.start()
    columns, count = field_ref.shape
    width = count // parts
    mass = mass_ref[...]
    if weight_before is None:
        field = field_ref[...]
        field_now = field_ref
    else:
        even = low_part(rank_ref[0], 2) == 0
        field = rim_correction(field_ref[...], even, first_ref, second_ref, mass, weight_before)
        field_scr[...] = field
        field_now = field_scr
    high, low = split_two(field)
    for h in range(parts):
        high_ref[h * columns : (h + 1) * columns] = high[:, h * width : (h + 1) * width]
        low_ref[h * columns : (h + 1) * columns] = low[:, h * width : (h + 1) * width]
    mat_high, mat_low = split_two(matrix_ref[...])
    matrix = jnp.concatenate(
        [
            jnp.concatenate([mat_high, mat_low], axis=1),
            jnp.concatenate([mat_high, jnp.zeros_like(mat_low)], axis=1),
        ],
        axis=0,
    )

    def gather(group):
        copies[group].wait()
        hot = held_ref[group]
        found_ref[group % 2] = dot(high_ref[...], hot) + dot(low_ref[...], hot)

    def pick(group):
        slot = group % 2
        for e in range(GROUP):
            element = group * GROUP + e
            key = keys_ref[element : element + 1, :]
            got = pick_part(found_ref[slot, :, e * LANES : (e + 1) * LANES], high_part(key, width), parts)
            got_high, got_low = split_two(got)
            local_ref[slot, e * columns : (e + 1) * columns, :LANES] = got_high
            local_ref[slot, e * columns : (e + 1) * columns, LANES:] = got_low

    def multiply(group):
        product_ref[group % 2] = dot(local_ref[group % 2], matrix)

    def scale(group):
        slot = group % 2
        for e in range(GROUP):
            element = group * GROUP + e
            part = high_part(keys_ref[element : element + 1, :], width)
            rows = product_ref[slot, e * columns : (e + 1) * columns]
            value = (rows[:, :LANES] + rows[:, LANES:]) * coef_ref[element]
            value_high, value_low = split_two(value)
            span = slice(e * LANES, (e + 1) * LANES)
            for h in range(parts):
                mask = jnp.where(part == h, 1.0, 0.0).astype(BF16)
                yhigh_ref[slot, h * columns : (h + 1) * columns, span] = value_high * mask
                ylow_ref[slot, h * columns : (h + 1) * columns, span] = value_low * mask

    def scatter(group):
        hot = held_ref[group]
        added = dot_nt(yhigh_ref[group % 2], hot) + dot_nt(ylow_ref[group % 2], hot)
        sum_ref[...] = added if group == 0 else sum_ref[...] + added

    gather(0)
    for group in range(groups):
        pick(group)
        if group + 1 < groups:
            gather(group + 1)
        multiply(group)
        if group:
            scatter(group - 1)
        scale(group)
    scatter(groups - 1)
    for h in range(parts):
        span = slice(h * width, (h + 1) * width)
        stiff = sum_ref[h * columns : (h + 1) * columns]
        out_ref[:, span] = (1.0 - weight) * field_now[:, span] + weight * (
            rhs_ref[:, span] - stiff
        ) / mass[:, span]


def loads_kernel(
    parts, brow, weight, used, rank_ref, nodes_ref, chunk_ref, forcing_ref, field_ref, first_ref,
    second_ref, mass_ref, rhs_ref, out_ref, rim_first_ref, rim_second_ref,
):
    columns, count = field_ref.shape
    loads = received_loads(chunk_ref, used, brow, columns)
    added = scatter_nodes(loads, nodes_ref[0:1, :], parts, count)
    rhs_ref[...] = forcing_ref[...] + added
    mass = mass_ref[...]
    even = low_part(rank_ref[0], 2) == 0
    field = field_ref[...] + weight * added / mass
    field = rim_correction(field, even, first_ref, second_ref, mass, weight)
    out_ref[...] = field
    write_rims(field, even, rim_first_ref, rim_second_ref)


def finish_kernel(
    parts, brow, bcol, panel_dev, slot_rows, weight, rank_ref, map_ref, nodes_ref, field_ref,
    first_ref, second_ref, mass_ref, potential_ref, out_ref, chunk_ref, rim_first_ref, rim_second_ref,
):
    rank = rank_ref[0]
    even = low_part(rank, 2) == 0
    field = rim_correction(field_ref[...], even, first_ref, second_ref, mass_ref[...], weight)
    out_ref[...] = field
    write_rims(field, even, rim_first_ref, rim_second_ref)
    loads = load_rows(
        potential_ref[...], own_panels(map_ref, rank, panel_dev), brow * bcol, slot_rows
    )
    pieces = trace_rows(field, nodes_ref[0:1, :], parts, brow, bcol * slot_rows)
    write_chunks(chunk_ref, pieces, loads, bcol)


def last_kernel(weight, rank_ref, field_ref, first_ref, second_ref, mass_ref, out_ref):
    even = low_part(rank_ref[0], 2) == 0
    out_ref[...] = rim_correction(field_ref[...], even, first_ref, second_ref, mass_ref[...], weight)


def density_groups(place_ref, map_ref, chunk_ref, brow, bcol, panel_dev, slot_rows):
    base = pl.multiple_of(place_ref[0] * (bcol * panel_dev), LANES)
    devices = brow * bcol
    columns = LANES // HALVES
    rows = BLOCKS * slot_rows
    panels = BLOCKS * panel_dev
    lane = lax.broadcasted_iota(jnp.int32, (1, panels), 1).astype(F32)
    block = jnp.floor((lane + 0.5) * (1.0 / panel_dev)).astype(jnp.int32)
    traces = chunk_ref[...].astype(F32)
    for group in range(bcol // BLOCKS):
        span = pl.ds(base + group * panels, panels)
        owner, slot = map_ref[0:1, span], map_ref[1:2, span]
        half, low = halves_of(slot, slot_rows)
        key = owner * rows + block * slot_rows + low
        near = traces[:, group * rows : (group + 1) * rows].reshape(devices * rows, LANES)
        found = dot(jnp.transpose(near).astype(BF16), one_hot_rows(key, devices * rows))
        density = jnp.where(half == 0, found[:columns], found[columns:])
        turned = jnp.concatenate([-density[columns // 2 :], density[: columns // 2]], axis=0)
        yield density.astype(BF16), turned.astype(BF16)


def write_parts(out_ref, total, panel_dev):
    for r in range(out_ref.shape[0]):
        out_ref[r] = total[:, r * panel_dev : (r + 1) * panel_dev]


def tile_kernel(
    brow, bcol, panel_dev, slot_rows, place_ref, map_ref, chunk_ref, out_ref, real_ref, imag_ref,
    target_ref, density_ref, turned_ref, built_real_ref, built_imag_ref, sum_ref, sems,
):
    count_all = brow * bcol * panel_dev
    soften = 0.5 * float(count_all) ** (-1.0 / 3.0)
    each = POINT_ROWS // 3
    row_index, col_index = place_ref[0], place_ref[1]
    start = bcol * slot_rows + LOAD_ROWS
    block = pl.program_id(0)

    def points_of(device):
        return chunk_ref[device].astype(F32)[start : start + POINT_ROWS]

    def copies(index):
        return (
            pltpu.make_async_copy(built_real_ref.at[index], real_ref.at[index], sems.at[0, index]),
            pltpu.make_async_copy(built_imag_ref.at[index], imag_ref.at[index], sems.at[1, index]),
        )

    @pl.when(block == 0)
    def prepare():
        near = [points_of(r * bcol + col_index) for r in range(brow)]
        for axis in range(3):
            rows = []
            for piece in near:
                for part in range(each):
                    wide = min(LANES, panel_dev - part * LANES)
                    rows.append(piece[axis * each + part : axis * each + part + 1, :wide])
            target_ref[axis : axis + 1, :] = jnp.concatenate(rows, axis=1)
        sum_ref[...] = jnp.zeros_like(sum_ref)
        groups = density_groups(place_ref, map_ref, chunk_ref, brow, bcol, panel_dev, slot_rows)
        for group, (density, turned) in enumerate(groups):
            for k in range(BLOCKS):
                span = slice(k * panel_dev, (k + 1) * panel_dev)
                density_ref[group * BLOCKS + k] = density[:, span]
                turned_ref[group * BLOCKS + k] = turned[:, span]

    source = jnp.transpose(points_of(row_index * bcol + block))
    step = 16
    for top in range(0, panel_dev, step):
        part, first = top // LANES, top % LANES
        squared = soften * soften
        for axis in range(3):
            column = source[first : first + step, axis * each + part : axis * each + part + 1]
            delta = column - target_ref[axis : axis + 1, :]
            squared = squared + delta * delta
        inverse = lax.rsqrt(squared)
        turns = (squared * inverse) * (wave_number / (2.0 * math.pi))
        turns = turns - jnp.floor(turns + 0.5)
        z = turns * turns
        sine = jnp.full_like(z, SIN_POLY[-1])
        for factor in SIN_POLY[-2::-1]:
            sine = sine * z + factor
        sine = sine * turns
        cosine = jnp.full_like(z, COS_POLY[-1])
        for factor in COS_POLY[-2::-1]:
            cosine = cosine * z + factor
        double = sine * (inverse * (2.0 / math.sqrt(float(count_all))))
        built_real_ref[block, top : top + step] = (
            inverse * (1.0 / math.sqrt(float(count_all))) - sine * double
        ).astype(BF16)
        built_imag_ref[block, top : top + step] = (cosine * double).astype(BF16)
    for copy in copies(block):
        copy.start()
    sum_ref[...] += dot(density_ref[block], built_real_ref[block]) + dot(
        turned_ref[block], built_imag_ref[block]
    )

    @pl.when(block == bcol - 1)
    def end():
        write_parts(out_ref, sum_ref[...], panel_dev)
        for index in range(bcol):
            for copy in copies(index):
                copy.wait()


def potential_kernel(
    brow, bcol, panel_dev, slot_rows, place_ref, map_ref, chunk_ref, real_ref, imag_ref, out_ref,
    held_real_ref, held_imag_ref, sems,
):
    copies = (
        pltpu.make_async_copy(real_ref, held_real_ref, sems.at[0]),
        pltpu.make_async_copy(imag_ref, held_imag_ref, sems.at[1]),
    )
    for copy in copies:
        copy.start()
    groups = list(density_groups(place_ref, map_ref, chunk_ref, brow, bcol, panel_dev, slot_rows))
    for copy in copies:
        copy.wait()
    total = None
    for group, (density, turned) in enumerate(groups):
        here = slice(group * BLOCKS, (group + 1) * BLOCKS)
        shape = (BLOCKS * panel_dev, brow * panel_dev)
        part = dot(density, held_real_ref[here].reshape(shape)) + dot(
            turned, held_imag_ref[here].reshape(shape)
        )
        total = part if total is None else total + part
    write_parts(out_ref, total, panel_dev)


def per_device(
    panel_points,
    panel_map,
    element_nodes,
    element_coef,
    element_matrix,
    node_mass,
    forcing,
    field_start,
    potential_start,
):
    columns, panel_dev = potential_start.shape
    count = field_start.shape[1]
    brow, bcol = lax.axis_size("brow"), lax.axis_size("bcol")
    devices = brow * bcol
    capacity = max(2, 2 * panel_dev // devices)
    slot_rows = -(-capacity // HALVES)
    used = bcol * slot_rows
    assert slot_rows <= LOAD_ROWS and columns * HALVES == LANES and bcol % BLOCKS == 0
    parts = 256 // columns
    width = count // parts
    row_panels = bcol * panel_dev
    row_index, col_index = lax.axis_index("brow"), lax.axis_index("bcol")
    rank = (row_index * bcol + col_index).reshape(1)
    place = jnp.stack([row_index, col_index])
    mass = node_mass.reshape(1, count)
    nodes_each, elements = element_nodes.shape
    assert elements % GROUP == 0
    keys = jnp.pad(element_nodes.T, ((0, 0), (0, LANES - nodes_each)))
    matrix = jnp.pad(element_matrix, ((0, LANES - nodes_each), (0, LANES - nodes_each)))
    smem = pl.BlockSpec(memory_space=pltpu.SMEM)
    vmem = pl.BlockSpec(memory_space=pltpu.VMEM)
    rim_shape = shape_of((columns, RIM), BF16)
    field_shape = shape_of((columns, count), F32)
    weights = [weight_of(sweep_index) for sweep_index in range(SWEEPS)]
    even_pairs = [(i, i ^ 1) for i in range(devices)]
    odd_pairs = [pair for i in range(1, devices - 1, 2) for pair in ((i, i + 1), (i + 1, i))]
    even = (rank[0] & 1) == 0

    def chunk_shape(rows, unit):
        return shape_of((devices, -(-rows // unit) * unit, LANES), BF16)

    def table_shape(stride):
        return shape_of((8, brow * (-(-HALVES * bcol * stride // LANES) * LANES)), jnp.int32)

    def exchange(first, second):
        return lax.ppermute(first, AXES, even_pairs), lax.ppermute(second, AXES, odd_pairs)

    def rims(field, halo, weight):
        first, second = (piece.astype(F32) for piece in halo)
        left, right = jnp.where(even, second, first), jnp.where(even, first, second)
        last = count - RIM
        low = field[:, :RIM] + (weight * penalty) * left / mass[:, :RIM]
        high = field[:, last:] + (weight * penalty) * right / mass[:, last:]
        return jnp.where(even, high, low).astype(BF16), jnp.where(even, low, high).astype(BF16)

    def swap_all(chunks):
        return lax.all_to_all(chunks, AXES, split_axis=0, concat_axis=0, tiled=True)

    hbm = pl.BlockSpec(memory_space=pltpu.HBM)
    hot_shape = (elements // GROUP, width, GROUP * LANES)
    hot_blocks = max(hot_shape[0], -(-48 * MIB // (2 * width * GROUP * LANES)))

    def sweep(field, rhs, weight, halo=(), weight_before=None):
        rows = parts * columns
        lanes = GROUP * LANES
        first = weight_before is None
        return call(
            functools.partial(sweep_kernel, parts, weight, weight_before),
            field_shape,
            5_000_000_000,
            limit=24,
            in_specs=[smem, smem] + [vmem] * 5 + [hbm] + [vmem] * len(halo),
            out_specs=vmem,
            scratch_shapes=([] if first else [pltpu.VMEM((columns, count), F32)])
            + [
                pltpu.VMEM(hot_shape, BF16),
                pltpu.SemaphoreType.DMA((elements // GROUP,)),
                pltpu.VMEM((rows, width), BF16),
                pltpu.VMEM((rows, width), BF16),
                pltpu.VMEM((2, rows, lanes), F32),
                pltpu.VMEM((2, GROUP * columns, 2 * LANES), BF16),
                pltpu.VMEM((2, GROUP * columns, 2 * LANES), F32),
                pltpu.VMEM((2, rows, lanes), BF16),
                pltpu.VMEM((2, rows, lanes), BF16),
                pltpu.VMEM((rows, width), F32),
            ],
        )(rank, element_coef, field, rhs, mass, keys, matrix, hot, *halo)

    def add_loads(chunks, field, halo, weight):
        return call(
            functools.partial(loads_kernel, parts, brow, weight, used),
            (field_shape, field_shape, rim_shape, rim_shape),
            500_000_000,
            in_specs=[smem] + [vmem] * 7,
            out_specs=(vmem,) * 4,
        )(rank, load_nodes, chunks, forcing, field, *halo, mass)

    tile_shape = (bcol, panel_dev, brow * panel_dev)
    parts_shape = shape_of((brow, columns, panel_dev), F32)
    sizes = (brow, bcol, panel_dev, slot_rows)

    def sum_parts(parts_out):
        return lax.psum_scatter(parts_out, "brow", scatter_dimension=0, tiled=False)

    nodes, load_nodes, chunks, *rim = call(
        functools.partial(setup_kernel, parts, brow, bcol, panel_dev, slot_rows),
        (
            table_shape(slot_rows),
            table_shape(LOAD_ROWS),
            chunk_shape(used + LOAD_ROWS + POINT_ROWS, 16),
            rim_shape,
            rim_shape,
        ),
        2_000_000_000,
        limit=56,
        in_specs=[smem] + [vmem] * 4,
        out_specs=(vmem,) * 5,
    )(rank, panel_map, field_start, potential_start, panel_points)
    hot = call(
        hot_kernel,
        shape_of((hot_blocks,) + hot_shape[1:], BF16),
        1_000_000_000,
        in_specs=[vmem],
        out_specs=hbm,
        scratch_shapes=[pltpu.VMEM(hot_shape, BF16), pltpu.SemaphoreType.DMA((hot_shape[0],))],
    )(keys)
    halo = exchange(*rim)
    chunks = swap_all(chunks)
    field = sweep(field_start, forcing, weights[0])
    parts_out, real_tile, imag_tile = call(
        functools.partial(tile_kernel, *sizes),
        (parts_shape, shape_of(tile_shape, BF16), shape_of(tile_shape, BF16)),
        8_000_000_000,
        limit=58,
        grid=(bcol,),
        in_specs=[smem, vmem, vmem],
        out_specs=(vmem, hbm, hbm),
        scratch_shapes=[
            pltpu.VMEM((8, brow * panel_dev), F32),
            pltpu.VMEM((bcol, columns, panel_dev), BF16),
            pltpu.VMEM((bcol, columns, panel_dev), BF16),
            pltpu.VMEM(tile_shape, BF16),
            pltpu.VMEM(tile_shape, BF16),
            pltpu.VMEM((columns, brow * panel_dev), F32),
            pltpu.SemaphoreType.DMA((2, bcol)),
        ],
    )(place, panel_map, chunks)
    potential = sum_parts(parts_out)
    rhs, field, *rim = add_loads(chunks, field, halo, weights[0])
    halo = exchange(*rim)
    field = sweep(field, rhs, weights[1])
    halo_next = exchange(*rims(field, halo, weights[1]))
    field = sweep(field, rhs, weights[2], halo, weights[1])
    field, chunks, *rim = call(
        functools.partial(finish_kernel, parts, brow, bcol, panel_dev, slot_rows, weights[2]),
        (field_shape, chunk_shape(used + LOAD_ROWS, 8), rim_shape, rim_shape),
        1_000_000_000,
        in_specs=[smem] + [vmem] * 7,
        out_specs=(vmem,) * 4,
    )(rank, panel_map, nodes, field, *halo_next, mass, potential)

    halo = exchange(*rim)
    chunks = swap_all(chunks)
    field = sweep(field, forcing, weights[0])
    parts_out = call(
        functools.partial(potential_kernel, *sizes),
        parts_shape,
        2_000_000_000,
        limit=58,
        in_specs=[smem, vmem, vmem, hbm, hbm],
        out_specs=vmem,
        scratch_shapes=[
            pltpu.VMEM(tile_shape, BF16),
            pltpu.VMEM(tile_shape, BF16),
            pltpu.SemaphoreType.DMA((2,)),
        ],
    )(place, panel_map, chunks, real_tile, imag_tile)
    parts_out, field = lax.optimization_barrier((parts_out, field))
    potential = sum_parts(parts_out)
    rhs, field, *rim = add_loads(chunks, field, halo, weights[0])
    halo = exchange(*rim)
    field = sweep(field, rhs, weights[1])
    halo_next = exchange(*rims(field, halo, weights[1]))
    field = sweep(field, rhs, weights[2], halo, weights[1])
    field = call(
        functools.partial(last_kernel, weights[2]),
        field_shape,
        100_000_000,
        in_specs=[smem] + [vmem] * 4,
        out_specs=vmem,
    )(rank, field, *halo_next, mass)
    return (field, potential)


def solution(mesh):
    placed = (
        P(None, AXES),
        P(),
        P(None, AXES),
        P(AXES),
        P(),
        P(AXES),
        P(None, AXES),
        P(None, AXES),
        P(None, AXES),
    )
    return jax.shard_map(
        per_device,
        mesh=mesh,
        in_specs=placed,
        out_specs=(P(None, AXES), P(None, AXES)),
        check_vma=False,
    )
```

profile of v0, /device:TPU:4, one launch (start us, length us, event | category | flops | bytes accessed | tf_op | source)
XLA Modules:
  0.0 137.7 jit_solution(10406224833681435637)
XLA Ops:
  7.2 0.0 copy-start.12
  7.2 0.0 copy-start.11
  7.2 3.3 %shard_map.104 = (s32[8,512]{1,0:T(8,128)}, s32[8,512]{1,0:T(8,128)}, bf16[32,64,128]{2,1,0:T(8,128)(2,1)}, bf16[64,128]{1,0:T(8,128)(2,1)}, bf16[64,128]{1,0:T(8,128)(2,1)}) custom-call(s32[1]{0:T(128)} %bitcast.rank_ref, s32[3,6144]{1,0:T(4,128)} %map_ref.7, f32[64,2048]{1,0:T(8,128)} %field_ref.3, f32[64,192]{1,0:T(8,128)} %potential_ref.1, ...), custom_call_target="tpu_custom_call" | custom-call | flops 2000000000 | bytes 1048576 | tf_op jit(solution)/shard_map/pallas_call | solution.py:612
  10.5 6.1 %all-to-all-start = ((bf16[32,64,128]{2,1,0:T(8,128)(2,1)}), bf16[32,64,128]{2,1,0:T(8,128)(2,1)S(1)}, u32[]{:S(2)}, u32[]{:S(2)}) async-start(bf16[32,64,128]{2,1,0:T(8,128)(2,1)} %get-tuple-element.26), calls=%async_computation | async-start | bytes 1048576 | tf_op jit(solution)/shard_map/all_to_all | solution.py:564
  16.6 0.0 reduce-scatter.7.cloned.1.call-start
  16.6 0.2 collective-permute-start
  16.8 6.1 %collective-permute-start.1 = (bf16[64,128]{1,0:T(8,128)(2,1)}, bf16[64,128]{1,0:T(8,128)(2,1)S(1)}, u32[]{:S(2)}, u32[]{:S(2)}) collective-permute-start(bf16[64,128]{1,0:T(8,128)(2,1)} %get-tuple-element.28), channel_id=1, source_target_pairs={{1,2},{2,1},{3,4},{4,3},{5,6},{6,5},{7,8},{8,7},{9,10},{10,9},{11,... | collective-permute-start | bytes 49160 | tf_op jit(solution)/shard_map/ppermute | solution.py:553
  23.0 0.0 copy-start.5
  23.0 0.0 copy-start
  23.0 0.0 copy-start.1
  23.0 0.0 copy-start.6
  23.0 2.2 %shard_map.105.hot_ref = bf16[96,512,512]{2,1,0:T(8,128)(2,1)} custom-call(s32[32,128]{1,0:T(8,128)S(1)} %pad.8.keys_ref), custom_call_target="tpu_custom_call" | custom-call | flops 1000000000 | bytes 1048576 | tf_op jit(solution)/shard_map/pallas_call | solution.py:626
  25.3 7.5 %shard_map.106.field_ref = f32[64,2048]{1,0:T(8,128)S(1)} custom-call(s32[1]{0:T(128)} %bitcast.rank_ref, f32[32]{0:T(128)S(1)} %copy-done.6, f32[64,2048]{1,0:T(8,128)S(1)} %copy-done.1, f32[64,2048]{1,0:T(8,128)S(1)} %copy-done, f32[1,2048]{1,0:T(1,128)S(1)} %bitcast.13, s32[32,128]{1,0:T(8,128)S(1)} %pad.8.keys_ref, f32[128,128]{1,0:T(8,128)S(1)} %pad.9.matrix_ref, ...), custom_call_target="tpu_custom_call" | custom-call | flops 5000000000 | bytes 1048576 | tf_op jit(solution)/shard_map/pallas_call | solution.py:574
  32.7 0.7 pad_add_fusion.place_ref
  33.4 0.0 collective-permute-done.first_ref
  33.4 0.0 collective-permute-done.1.second_ref
  33.4 0.0 all-to-all-done.chunk_ref
  33.4 0.0 copy-start.2
  33.4 0.4 shard_map.107
  33.9 0.1 collective-permute-start.2
  33.9 3.2 %collective-permute-start.3 = (bf16[64,128]{1,0:T(8,128)(2,1)S(1)}, bf16[64,128]{1,0:T(8,128)(2,1)S(1)}, u32[]{:S(2)}, u32[]{:S(2)}) collective-permute-start(bf16[64,128]{1,0:T(8,128)(2,1)S(1)} %get-tuple-element.32), channel_id=1, source_target_pairs={{1,2},{2,1},{3,4},{4,3},{5,6},{6,5},{7,8},{8,7},{9,10},{10,9},{11,... | collective-permute-start | bytes 49160 | tf_op jit(solution)/shard_map/ppermute | solution.py:553
  37.2 13.1 %shard_map.110 = (f32[4,64,192]{2,1,0:T(8,128)}, bf16[8,192,768]{2,1,0:T(8,128)(2,1)}, bf16[8,192,768]{2,1,0:T(8,128)(2,1)}) custom-call(s32[2]{0:T(128)} %pad_add_fusion.place_ref, s32[3,6144]{1,0:T(4,128)} %map_ref.7, bf16[32,64,128]{2,1,0:T(8,128)(2,1)} %copy-done.2), custom_call_target="tpu_custom_call" | custom-call | flops 8000000000 | bytes 1048576 | tf_op jit(solution)/shard_map/pallas_call | solution.py:637
  50.3 0.0 reduce-scatter.7.cloned.1.call-update
  50.3 7.5 %shard_map.108.field_ref = f32[64,2048]{1,0:T(8,128)S(1)} custom-call(s32[1]{0:T(128)} %bitcast.rank_ref, f32[32]{0:T(128)S(1)} %copy-done.6, f32[64,2048]{1,0:T(8,128)S(1)} %get-tuple-element.29.field_ref, f32[64,2048]{1,0:T(8,128)S(1)} %get-tuple-element.30.rhs_ref, f32[1,2048]{1,0:T(1,128)S(1)} %bitcast.15, s32[32,128]{1,0:T(8,128)S(1)} %pad.8.keys_ref, ...), custom_call_target="tpu_custom_call" | custom-call | flops 5000000000 | bytes 1048576 | tf_op jit(solution)/shard_map/pallas_call | solution.py:574
  57.8 0.0 collective-permute-done.2.more_refs_0_
  57.8 0.0 collective-permute-done.3.more_refs_1_
  57.9 0.1 collective-permute-start.4
  57.9 0.0 copy-start.7
  57.9 0.0 copy-start.10
  58.0 6.2 %collective-permute-start.5 = (bf16[64,128]{1,0:T(8,128)(2,1)S(1)}, bf16[64,128]{1,0:T(8,128)(2,1)S(1)}, u32[]{:S(2)}, u32[]{:S(2)}) collective-permute-start(bf16[64,128]{1,0:T(8,128)(2,1)S(1)} %get-tuple-element.48), channel_id=1, source_target_pairs={{1,2},{2,1},{3,4},{4,3},{5,6},{6,5},{7,8},{8,7},{9,10},{10,9},{11,... | collective-permute-start | bytes 49160 | tf_op jit(solution)/shard_map/ppermute | solution.py:553
  64.2 7.4 %shard_map.109.field_ref = f32[64,2048]{1,0:T(8,128)S(1)} custom-call(s32[1]{0:T(128)} %bitcast.rank_ref, f32[32]{0:T(128)S(1)} %copy-done.6, f32[64,2048]{1,0:T(8,128)S(1)} %shard_map.108.field_ref, f32[64,2048]{1,0:T(8,128)S(1)} %get-tuple-element.30.rhs_ref, f32[1,2048]{1,0:T(1,128)S(1)} %bitcast.16, s32[32,128]{1,0:T(8,128)S(1)} %pad.8.keys_ref, ...), custom_call_target="tpu_custom_call" | custom-call | flops 5000000000 | bytes 1048576 | tf_op jit(solution)/shard_map/pallas_call | solution.py:574
  71.7 0.0 collective-permute-done.4.first_ref
  71.7 0.0 collective-permute-done.5.second_ref
  71.7 2.9 %reduce-scatter.7.cloned.1.call-done = f32[1,64,192]{2,1,0:T(8,128)} async-done(((f32[4,64,192]{2,1,0:T(8,128)}), f32[1,64,192]{2,1,0:T(8,128)}) %reduce-scatter.7.cloned.1.call-update) | async-done | bytes 49168
  74.6 0.0 copy-done.10
  74.6 0.8 copy-done.8
  75.4 1.5 %shard_map.111 = (f32[64,2048]{1,0:T(8,128)S(1)}, bf16[32,56,128]{2,1,0:T(8,128)(2,1)}, bf16[64,128]{1,0:T(8,128)(2,1)S(1)}, bf16[64,128]{1,0:T(8,128)(2,1)S(1)}) custom-call(s32[1]{0:T(128)} %bitcast.rank_ref, s32[3,6144]{1,0:T(4,128)S(1)} %copy-done.7, s32[8,512]{1,0:T(8,128)S(1)} %copy-done.10, f32[64,2048]{1,0:T(8,128)S(1)} %shard_map.109.field_ref, ...), custom_call_target="tpu_custom_call" | custom-call | flops 1000000000 | bytes 1048576 | tf_op jit(solution)/shard_map/pallas_call | solution.py:661
  76.9 4.9 %all-to-all-start.1 = ((bf16[32,56,128]{2,1,0:T(8,128)(2,1)}), bf16[32,56,128]{2,1,0:T(8,128)(2,1)S(1)}, u32[]{:S(2)}, u32[]{:S(2)}) async-start(bf16[32,56,128]{2,1,0:T(8,128)(2,1)} %get-tuple-element.34), calls=%async_computation.1 | async-start | bytes 917504 | tf_op jit(solution)/shard_map/all_to_all | solution.py:564
  81.8 0.0 reduce-scatter.9.cloned.1.call-start
  81.9 0.2 collective-permute-start.6
  82.1 6.3 %collective-permute-start.7 = (bf16[64,128]{1,0:T(8,128)(2,1)S(1)}, bf16[64,128]{1,0:T(8,128)(2,1)S(1)}, u32[]{:S(2)}, u32[]{:S(2)}) collective-permute-start(bf16[64,128]{1,0:T(8,128)(2,1)S(1)} %get-tuple-element.40), channel_id=1, source_target_pairs={{1,2},{2,1},{3,4},{4,3},{5,6},{6,5},{7,8},{8,7},{9,10},{10,9},{11,... | collective-permute-start | bytes 49160 | tf_op jit(solution)/shard_map/ppermute | solution.py:553
  88.4 7.4 %shard_map.113.field_ref = f32[64,2048]{1,0:T(8,128)S(1)} custom-call(s32[1]{0:T(128)} %bitcast.rank_ref, f32[32]{0:T(128)S(1)} %copy-done.6, f32[64,2048]{1,0:T(8,128)S(1)} %get-tuple-element.37.field_ref, f32[64,2048]{1,0:T(8,128)S(1)} %copy-done, f32[1,2048]{1,0:T(1,128)S(1)} %bitcast.18, s32[32,128]{1,0:T(8,128)S(1)} %pad.8.keys_ref, ...), custom_call_target="tpu_custom_call" | custom-call | flops 5000000000 | bytes 1048576 | tf_op jit(solution)/shard_map/pallas_call | solution.py:574
  95.8 0.0 all-to-all-done.1.chunk_ref
  95.9 0.0 copy-start.3
  95.9 0.8 copy-done.3
  96.6 5.4 %shard_map.112 = f32[4,64,192]{2,1,0:T(8,128)} custom-call(s32[2]{0:T(128)} %pad_add_fusion.place_ref, s32[3,6144]{1,0:T(4,128)} %map_ref.7, bf16[32,56,128]{2,1,0:T(8,128)(2,1)} %copy-done.3, bf16[8,192,768]{2,1,0:T(8,128)(2,1)} %get-tuple-element.35.real_ref, bf16[8,192,768]{2,1,0:T(8,128)(2,1)} %get-tuple-element.36.imag_ref), custom_call_target="tpu_custom_call" | custom-call | flops 2000000000 | bytes 1048576 | tf_op jit(solution)/shard_map/pallas_call | solution.py:672
  102.0 0.0 collective-permute-done.6.first_ref
  102.0 0.0 collective-permute-done.7.second_ref
  102.0 0.0 copy-start.4
  102.0 1.0 copy-done.4
  103.0 0.4 shard_map.114
  103.5 0.1 collective-permute-start.8
  103.5 3.7 %collective-permute-start.9 = (bf16[64,128]{1,0:T(8,128)(2,1)S(1)}, bf16[64,128]{1,0:T(8,128)(2,1)S(1)}, u32[]{:S(2)}, u32[]{:S(2)}) collective-permute-start(bf16[64,128]{1,0:T(8,128)(2,1)S(1)} %get-tuple-element.44), channel_id=1, source_target_pairs={{1,2},{2,1},{3,4},{4,3},{5,6},{6,5},{7,8},{8,7},{9,10},{10,9},{11,... | collective-permute-start | bytes 49160 | tf_op jit(solution)/shard_map/ppermute | solution.py:553
  107.3 0.0 reduce-scatter.9.cloned.1.call-update
  107.3 7.4 %shard_map.115.field_ref = f32[64,2048]{1,0:T(8,128)S(1)} custom-call(s32[1]{0:T(128)} %bitcast.rank_ref, f32[32]{0:T(128)S(1)} %copy-done.6, f32[64,2048]{1,0:T(8,128)S(1)} %get-tuple-element.41.field_ref, f32[64,2048]{1,0:T(8,128)S(1)} %get-tuple-element.42.rhs_ref, f32[1,2048]{1,0:T(1,128)S(1)} %bitcast.20, s32[32,128]{1,0:T(8,128)S(1)} %pad.8.keys_ref, ...), custom_call_target="tpu_custom_call" | custom-call | flops 5000000000 | bytes 1048576 | tf_op jit(solution)/shard_map/pallas_call | solution.py:574
  114.8 0.0 collective-permute-done.8.more_refs_0_
  114.8 0.0 collective-permute-done.9.more_refs_1_
  114.8 0.1 collective-permute-start.10
  114.9 5.7 %collective-permute-start.11 = (bf16[64,128]{1,0:T(8,128)(2,1)S(1)}, bf16[64,128]{1,0:T(8,128)(2,1)S(1)}, u32[]{:S(2)}, u32[]{:S(2)}) collective-permute-start(bf16[64,128]{1,0:T(8,128)(2,1)S(1)} %get-tuple-element.46), channel_id=1, source_target_pairs={{1,2},{2,1},{3,4},{4,3},{5,6},{6,5},{7,8},{8,7},{9,10},{10,9},{11,... | collective-permute-start | bytes 49160 | tf_op jit(solution)/shard_map/ppermute | solution.py:553
  120.6 7.4 %shard_map.116.field_ref = f32[64,2048]{1,0:T(8,128)S(1)} custom-call(s32[1]{0:T(128)} %bitcast.rank_ref, f32[32]{0:T(128)S(1)} %copy-done.6, f32[64,2048]{1,0:T(8,128)S(1)} %shard_map.115.field_ref, f32[64,2048]{1,0:T(8,128)S(1)} %get-tuple-element.42.rhs_ref, f32[1,2048]{1,0:T(1,128)S(1)} %bitcast.21, s32[32,128]{1,0:T(8,128)S(1)} %pad.8.keys_ref, ...), custom_call_target="tpu_custom_call" | custom-call | flops 5000000000 | bytes 1048576 | tf_op jit(solution)/shard_map/pallas_call | solution.py:574
  128.0 0.0 collective-permute-done.10.first_ref
  128.0 0.0 collective-permute-done.11.second_ref
  128.0 0.8 shard_map.117
  128.9 2.0 %reduce-scatter.9.cloned.1.call-done = f32[1,64,192]{2,1,0:T(8,128)} async-done(((f32[4,64,192]{2,1,0:T(8,128)}), f32[1,64,192]{2,1,0:T(8,128)}) %reduce-scatter.9.cloned.1.call-update) | async-done | bytes 49168
  (16 shorter events, 0.1 us)
Async XLA Ops:
  7.2 15.8 %copy-start.12 = (s32[125,32]{0,1:T(8,128)S(1)}, s32[125,32]{0,1:T(8,128)}, u32[]{:S(2)}) copy-start(s32[125,32]{0,1:T(8,128)} %param.11) | copy-start | bytes 48004
  7.2 15.8 %copy-start.11 = (f32[125,125]{1,0:T(8,128)S(1)}, f32[125,125]{1,0:T(8,128)}, u32[]{:S(2)}) copy-start(f32[125,125]{1,0:T(8,128)} %param.13) | copy-start | bytes 187504
  10.5 22.9 %all-to-all-start = ((bf16[32,64,128]{2,1,0:T(8,128)(2,1)}), bf16[32,64,128]{2,1,0:T(8,128)(2,1)S(1)}, u32[]{:S(2)}, u32[]{:S(2)}) async-start(bf16[32,64,128]{2,1,0:T(8,128)(2,1)} %get-tuple-element.26), calls=%async_computation | async-start | bytes 1048576 | tf_op jit(solution)/shard_map/all_to_all | solution.py:564
  16.6 58.0 %reduce-scatter.7.cloned.1.call-start = ((), (), s32[]{:S(2)}) async-start(), calls=%async_computation.4 | async-start | bytes 327680
  16.6 16.8 %collective-permute-start = (bf16[64,128]{1,0:T(8,128)(2,1)}, bf16[64,128]{1,0:T(8,128)(2,1)S(1)}, u32[]{:S(2)}, u32[]{:S(2)}) collective-permute-start(bf16[64,128]{1,0:T(8,128)(2,1)} %get-tuple-element.27), channel_id=1, source_target_pairs={{0,1},{1,0},{2,3},{3,2},{4,5},{5,4},{6,7},{7,6},{8,9},{9,8},{10,11... | collective-permute-start | bytes 49160 | tf_op jit(solution)/shard_map/ppermute | solution.py:553
  16.8 16.6 %collective-permute-start.1 = (bf16[64,128]{1,0:T(8,128)(2,1)}, bf16[64,128]{1,0:T(8,128)(2,1)S(1)}, u32[]{:S(2)}, u32[]{:S(2)}) collective-permute-start(bf16[64,128]{1,0:T(8,128)(2,1)} %get-tuple-element.28), channel_id=1, source_target_pairs={{1,2},{2,1},{3,4},{4,3},{5,6},{6,5},{7,8},{8,7},{9,10},{10,9},{11,... | collective-permute-start | bytes 49160 | tf_op jit(solution)/shard_map/ppermute | solution.py:553
  23.0 2.2 %copy-start.5 = (f32[2048]{0:T(1024)S(1)}, f32[2048]{0:T(1024)}, u32[]{:S(2)}) copy-start(f32[2048]{0:T(1024)} %param.14) | copy-start | bytes 24580
  23.0 2.2 %copy-start = (f32[64,2048]{1,0:T(8,128)S(1)}, f32[64,2048]{1,0:T(8,128)}, u32[]{:S(2)}) copy-start(f32[64,2048]{1,0:T(8,128)} %forcing_ref.3) | copy-start | bytes 1572868
  23.0 2.2 %copy-start.1 = (f32[64,2048]{1,0:T(8,128)S(1)}, f32[64,2048]{1,0:T(8,128)}, u32[]{:S(2)}) copy-start(f32[64,2048]{1,0:T(8,128)} %field_ref.3) | copy-start | bytes 1572868
  23.0 2.2 %copy-start.6 = (f32[32]{0:T(128)S(1)}, f32[32]{0:T(128)}, u32[]{:S(2)}) copy-start(f32[32]{0:T(128)} %coef_ref.11) | copy-start | bytes 388
  25.3 8.2 %copy-start.9 = (s32[8,512]{1,0:T(8,128)S(1)}, s32[8,512]{1,0:T(8,128)}, u32[]{:S(2)}) copy-start(s32[8,512]{1,0:T(8,128)} %get-tuple-element.24.nodes_ref) | copy-start | bytes 49156
  33.4 3.8 %copy-start.2 = (bf16[32,64,128]{2,1,0:T(8,128)(2,1)}, bf16[32,64,128]{2,1,0:T(8,128)(2,1)S(1)}, u32[]{:S(2)}) copy-start(bf16[32,64,128]{2,1,0:T(8,128)(2,1)S(1)} %all-to-all-done.chunk_ref) | copy-start | bytes 1572868
  33.9 24.0 %collective-permute-start.2 = (bf16[64,128]{1,0:T(8,128)(2,1)S(1)}, bf16[64,128]{1,0:T(8,128)(2,1)S(1)}, u32[]{:S(2)}, u32[]{:S(2)}) collective-permute-start(bf16[64,128]{1,0:T(8,128)(2,1)S(1)} %get-tuple-element.31), channel_id=1, source_target_pairs={{0,1},{1,0},{2,3},{3,2},{4,5},{5,4},{6,7},{7,6},{8,9},{9,8},{10,11... | collective-permute-start | bytes 49160 | tf_op jit(solution)/shard_map/ppermute | solution.py:553
  33.9 23.9 %collective-permute-start.3 = (bf16[64,128]{1,0:T(8,128)(2,1)S(1)}, bf16[64,128]{1,0:T(8,128)(2,1)S(1)}, u32[]{:S(2)}, u32[]{:S(2)}) collective-permute-start(bf16[64,128]{1,0:T(8,128)(2,1)S(1)} %get-tuple-element.32), channel_id=1, source_target_pairs={{1,2},{2,1},{3,4},{4,3},{5,6},{6,5},{7,8},{8,7},{9,10},{10,9},{11,... | collective-permute-start | bytes 49160 | tf_op jit(solution)/shard_map/ppermute | solution.py:553
  57.9 13.8 %collective-permute-start.4 = (bf16[64,128]{1,0:T(8,128)(2,1)S(1)}, bf16[64,128]{1,0:T(8,128)(2,1)S(1)}, u32[]{:S(2)}, u32[]{:S(2)}) collective-permute-start(bf16[64,128]{1,0:T(8,128)(2,1)S(1)} %get-tuple-element.49), channel_id=1, source_target_pairs={{0,1},{1,0},{2,3},{3,2},{4,5},{5,4},{6,7},{7,6},{8,9},{9,8},{10,11... | collective-permute-start | bytes 49160 | tf_op jit(solution)/shard_map/ppermute | solution.py:553
  57.9 16.6 %copy-start.7 = (s32[3,6144]{1,0:T(4,128)S(1)}, s32[3,6144]{1,0:T(4,128)}, u32[]{:S(2)}) copy-start(s32[3,6144]{1,0:T(4,128)} %map_ref.7) | copy-start | bytes 221188
  57.9 16.6 %copy-start.10 = (s32[8,512]{1,0:T(8,128)S(1)}, s32[8,512]{1,0:T(8,128)}, u32[]{:S(2)}) copy-start(s32[8,512]{1,0:T(8,128)} %get-tuple-element.25.nodes_ref) | copy-start | bytes 49156
  58.0 13.7 %collective-permute-start.5 = (bf16[64,128]{1,0:T(8,128)(2,1)S(1)}, bf16[64,128]{1,0:T(8,128)(2,1)S(1)}, u32[]{:S(2)}, u32[]{:S(2)}) collective-permute-start(bf16[64,128]{1,0:T(8,128)(2,1)S(1)} %get-tuple-element.48), channel_id=1, source_target_pairs={{1,2},{2,1},{3,4},{4,3},{5,6},{6,5},{7,8},{8,7},{9,10},{10,9},{11,... | collective-permute-start | bytes 49160 | tf_op jit(solution)/shard_map/ppermute | solution.py:553
  74.6 0.8 copy-start.8
  76.9 19.0 %all-to-all-start.1 = ((bf16[32,56,128]{2,1,0:T(8,128)(2,1)}), bf16[32,56,128]{2,1,0:T(8,128)(2,1)S(1)}, u32[]{:S(2)}, u32[]{:S(2)}) async-start(bf16[32,56,128]{2,1,0:T(8,128)(2,1)} %get-tuple-element.34), calls=%async_computation.1 | async-start | bytes 917504 | tf_op jit(solution)/shard_map/all_to_all | solution.py:564
  81.8 49.1 %reduce-scatter.9.cloned.1.call-start = ((), (), s32[]{:S(2)}) async-start(), calls=%async_computation.5 | async-start | bytes 327680
  81.9 20.1 %collective-permute-start.6 = (bf16[64,128]{1,0:T(8,128)(2,1)S(1)}, bf16[64,128]{1,0:T(8,128)(2,1)S(1)}, u32[]{:S(2)}, u32[]{:S(2)}) collective-permute-start(bf16[64,128]{1,0:T(8,128)(2,1)S(1)} %get-tuple-element.39), channel_id=1, source_target_pairs={{0,1},{1,0},{2,3},{3,2},{4,5},{5,4},{6,7},{7,6},{8,9},{9,8},{10,11... | collective-permute-start | bytes 49160 | tf_op jit(solution)/shard_map/ppermute | solution.py:553
  82.1 19.9 %collective-permute-start.7 = (bf16[64,128]{1,0:T(8,128)(2,1)S(1)}, bf16[64,128]{1,0:T(8,128)(2,1)S(1)}, u32[]{:S(2)}, u32[]{:S(2)}) collective-permute-start(bf16[64,128]{1,0:T(8,128)(2,1)S(1)} %get-tuple-element.40), channel_id=1, source_target_pairs={{1,2},{2,1},{3,4},{4,3},{5,6},{6,5},{7,8},{8,7},{9,10},{10,9},{11,... | collective-permute-start | bytes 49160 | tf_op jit(solution)/shard_map/ppermute | solution.py:553
  95.9 0.8 copy-start.3
  102.0 1.0 copy-start.4
  103.5 11.3 %collective-permute-start.8 = (bf16[64,128]{1,0:T(8,128)(2,1)S(1)}, bf16[64,128]{1,0:T(8,128)(2,1)S(1)}, u32[]{:S(2)}, u32[]{:S(2)}) collective-permute-start(bf16[64,128]{1,0:T(8,128)(2,1)S(1)} %get-tuple-element.43), channel_id=1, source_target_pairs={{0,1},{1,0},{2,3},{3,2},{4,5},{5,4},{6,7},{7,6},{8,9},{9,8},{10,11... | collective-permute-start | bytes 49160 | tf_op jit(solution)/shard_map/ppermute | solution.py:553
  103.5 11.2 %collective-permute-start.9 = (bf16[64,128]{1,0:T(8,128)(2,1)S(1)}, bf16[64,128]{1,0:T(8,128)(2,1)S(1)}, u32[]{:S(2)}, u32[]{:S(2)}) collective-permute-start(bf16[64,128]{1,0:T(8,128)(2,1)S(1)} %get-tuple-element.44), channel_id=1, source_target_pairs={{1,2},{2,1},{3,4},{4,3},{5,6},{6,5},{7,8},{8,7},{9,10},{10,9},{11,... | collective-permute-start | bytes 49160 | tf_op jit(solution)/shard_map/ppermute | solution.py:553
  114.8 13.2 %collective-permute-start.10 = (bf16[64,128]{1,0:T(8,128)(2,1)S(1)}, bf16[64,128]{1,0:T(8,128)(2,1)S(1)}, u32[]{:S(2)}, u32[]{:S(2)}) collective-permute-start(bf16[64,128]{1,0:T(8,128)(2,1)S(1)} %get-tuple-element.47), channel_id=1, source_target_pairs={{0,1},{1,0},{2,3},{3,2},{4,5},{5,4},{6,7},{7,6},{8,9},{9,8},{10,11... | collective-permute-start | bytes 49160 | tf_op jit(solution)/shard_map/ppermute | solution.py:553
  114.9 13.1 %collective-permute-start.11 = (bf16[64,128]{1,0:T(8,128)(2,1)S(1)}, bf16[64,128]{1,0:T(8,128)(2,1)S(1)}, u32[]{:S(2)}, u32[]{:S(2)}) collective-permute-start(bf16[64,128]{1,0:T(8,128)(2,1)S(1)} %get-tuple-element.46), channel_id=1, source_target_pairs={{1,2},{2,1},{3,4},{4,3},{5,6},{6,5},{7,8},{8,7},{9,10},{10,9},{11,... | collective-permute-start | bytes 49160 | tf_op jit(solution)/shard_map/ppermute | solution.py:553
Sparse Core Ops, SparseCore 0:
  50.5 24.0 reduce-scatter.6
  107.4 23.3 reduce-scatter.8
where the time goes:
time: 140 us; the launch traced here: 138 us
  Pallas kernels  71.7 us (51%)
  starting transfers between devices  43.1 us (31%)
  between operations  14.5 us (10%)
  waiting for transfers between devices  4.94 us (4%)
  local copies, waits for them, and re-layouts  2.69 us (2%)
    pallas_call x6, Pallas kernels, sweep(): call(functools.partial(sweep_kernel, parts, weight, weight_before), field...  44.7 us
    ppermute x6, starting transfers between devices, exchange(): lax.ppermute(second, AXES, odd_pairs)  31.3 us
    pallas_call x1, Pallas kernels, per_device(): call(functools.partial(tile_kernel, *sizes), (parts_shape, shape_of(tile_...  13.1 us
    all_to_all x2, starting transfers between devices, swap_all(): return lax.all_to_all(chunks, AXES, split_axis=0, concat_axis=0, tiled=True)  11 us
    pallas_call x1, Pallas kernels, per_device(): call(functools.partial(potential_kernel, *sizes), parts_shape, 2000000000...  5.36 us
    unnamed x4, waiting for transfers between devices  4.9 us
    pallas_call x1, Pallas kernels, per_device(): call(functools.partial(setup_kernel, parts, brow, bcol, panel_dev, slot_r...  3.27 us
  transfers between devices with their start and end apart: 16, of which 2 were waited for; matrix products, arithmetic and copies ran while one was open for 1% of the time, Pallas kernels for 48%

commit v1 on v0

--- a/solution.py
+++ b/solution.py
@@ -14,7 +14,7 @@
 LOAD_ROWS = 8
 POINT_ROWS = 8
 HALVES = 2
-GROUP = 4
+GROUP = 8
 BLOCKS = 4
 
 wave_number = 20.0
@@ -211,19 +211,6 @@
     write_chunks(chunk_ref, pieces, loads, bcol, point_rows(points_ref[...].astype(F32)))
 
 
-def hot_kernel(keys_ref, hot_ref, built_ref, sems):
-    groups, width, _ = built_ref.shape
-    copies = []
-    for group in range(groups):
-        for e in range(GROUP):
-            key = keys_ref[group * GROUP + e : group * GROUP + e + 1, :]
-            built_ref[group, :, e * LANES : (e + 1) * LANES] = one_hot_rows(low_part(key, width), width)
-        copies.append(pltpu.make_async_copy(built_ref.at[group], hot_ref.at[group], sems.at[group]))
-        copies[-1].start()
-    for copy in copies:
-        copy.wait()
-
-
 def rim_correction(value, even, first_ref, second_ref, mass, weight):
     step = weight * penalty
     first, second = first_ref[...].astype(F32), second_ref[...].astype(F32)
@@ -246,21 +233,23 @@
 
 
 def sweep_kernel(
-    parts, weight, weight_before, rank_ref, coef_ref, field_ref, rhs_ref, mass_ref, keys_ref,
-    matrix_ref, hot_ref, *more_refs,
+    parts, weight, weight_before, build, rank_ref, coef_ref, field_ref, rhs_ref, mass_ref, keys_ref,
+    matrix_ref, *more_refs,
 ):
-    if weight_before is not None:
-        first_ref, second_ref, out_ref, field_scr, *scratch = more_refs
+    if build:
+        out_ref, hot_ref, *scratch = more_refs
+    elif weight_before is None:
+        hot_ref, out_ref, *scratch = more_refs
     else:
-        out_ref, *scratch = more_refs
-    held_ref, sems, high_ref, low_ref, found_ref, local_ref, product_ref, yhigh_ref, ylow_ref, sum_ref = scratch
+        hot_ref, first_ref, second_ref, out_ref, field_scr, *scratch = more_refs
+    held_ref, sems, high_ref, low_ref, found_ref, local_ref, yhigh_ref, ylow_ref, sum_ref = scratch
     groups = held_ref.shape[0]
-    copies = [
-        pltpu.make_async_copy(hot_ref.at[group], held_ref.at[group], sems.at[group])
-        for group in range(groups)
-    ]
-    for copy in copies:
-        copy.start()
+    copies = []
+    for group in range(groups):
+        ends = (held_ref.at[group], hot_ref.at[group])
+        copies.append(pltpu.make_async_copy(*(ends if build else ends[::-1]), sems.at[group]))
+        if not build:
+            copies[-1].start()
     columns, count = field_ref.shape
     width = count // parts
     mass = mass_ref[...]
@@ -286,11 +275,17 @@
     )
 
     def gather(group):
-        copies[group].wait()
+        if build:
+            for e in range(GROUP):
+                key = keys_ref[group * GROUP + e : group * GROUP + e + 1, :]
+                held_ref[group, :, e * LANES : (e + 1) * LANES] = one_hot_rows(low_part(key, width), width)
+            copies[group].start()
+        else:
+            copies[group].wait()
         hot = held_ref[group]
         found_ref[group % 2] = dot(high_ref[...], hot) + dot(low_ref[...], hot)
 
-    def pick(group):
+    def multiply(group):
         slot = group % 2
         for e in range(GROUP):
             element = group * GROUP + e
@@ -300,15 +295,11 @@
             local_ref[slot, e * columns : (e + 1) * columns, :LANES] = got_high
             local_ref[slot, e * columns : (e + 1) * columns, LANES:] = got_low
 
-    def multiply(group):
-        product_ref[group % 2] = dot(local_ref[group % 2], matrix)
-
-    def scale(group):
-        slot = group % 2
+        product = dot(local_ref[slot], matrix)
         for e in range(GROUP):
             element = group * GROUP + e
             part = high_part(keys_ref[element : element + 1, :], width)
-            rows = product_ref[slot, e * columns : (e + 1) * columns]
+            rows = product[e * columns : (e + 1) * columns]
             value = (rows[:, :LANES] + rows[:, LANES:]) * coef_ref[element]
             value_high, value_low = split_two(value)
             span = slice(e * LANES, (e + 1) * LANES)
@@ -324,14 +315,13 @@
 
     gather(0)
     for group in range(groups):
-        pick(group)
         if group + 1 < groups:
             gather(group + 1)
         multiply(group)
-        if group:
-            scatter(group - 1)
-        scale(group)
-    scatter(groups - 1)
+        scatter(group)
+    if build:
+        for copy in copies:
+            copy.wait()
     for h in range(parts):
         span = slice(h * width, (h + 1) * width)
         stiff = sum_ref[h * columns : (h + 1) * columns]
@@ -356,9 +346,16 @@
     write_rims(field, even, rim_first_ref, rim_second_ref)
 
 
+def total(parts_ref):
+    value = parts_ref[0]
+    for r in range(1, parts_ref.shape[0]):
+        value = value + parts_ref[r]
+    return value
+
+
 def finish_kernel(
     parts, brow, bcol, panel_dev, slot_rows, weight, rank_ref, map_ref, nodes_ref, field_ref,
-    first_ref, second_ref, mass_ref, potential_ref, out_ref, chunk_ref, rim_first_ref, rim_second_ref,
+    first_ref, second_ref, mass_ref, parts_ref, out_ref, chunk_ref, rim_first_ref, rim_second_ref,
 ):
     rank = rank_ref[0]
     even = low_part(rank, 2) == 0
@@ -366,19 +363,22 @@
     out_ref[...] = field
     write_rims(field, even, rim_first_ref, rim_second_ref)
     loads = load_rows(
-        potential_ref[...], own_panels(map_ref, rank, panel_dev), brow * bcol, slot_rows
+        total(parts_ref), own_panels(map_ref, rank, panel_dev), brow * bcol, slot_rows
     )
     pieces = trace_rows(field, nodes_ref[0:1, :], parts, brow, bcol * slot_rows)
     write_chunks(chunk_ref, pieces, loads, bcol)
 
 
-def last_kernel(weight, rank_ref, field_ref, first_ref, second_ref, mass_ref, out_ref):
+def last_kernel(
+    weight, rank_ref, field_ref, first_ref, second_ref, mass_ref, parts_ref, out_ref, potential_ref
+):
     even = low_part(rank_ref[0], 2) == 0
     out_ref[...] = rim_correction(field_ref[...], even, first_ref, second_ref, mass_ref[...], weight)
-
-
-def density_groups(place_ref, map_ref, chunk_ref, brow, bcol, panel_dev, slot_rows):
-    base = pl.multiple_of(place_ref[0] * (bcol * panel_dev), LANES)
+    potential_ref[...] = total(parts_ref)
+
+
+def density_groups(rank_ref, map_ref, chunk_ref, brow, bcol, panel_dev, slot_rows):
+    base = pl.multiple_of(high_part(rank_ref[0], bcol) * (bcol * panel_dev), LANES)
     devices = brow * bcol
     columns = LANES // HALVES
     rows = BLOCKS * slot_rows
@@ -403,53 +403,73 @@
         out_ref[r] = total[:, r * panel_dev : (r + 1) * panel_dev]
 
 
+def split_three(value):
+    high = value.astype(BF16).astype(F32)
+    middle = (value - high).astype(BF16).astype(F32)
+    return [high, middle, value - high - middle]
+
+
+def squares(axes):
+    return sum(row * row for row in axes[1:]) + axes[0] * axes[0]
+
+
+def rows_of(rows, dtype=BF16):
+    row_id = lax.broadcasted_iota(jnp.int32, (16, rows[0].shape[1]), 0)
+    value = jnp.zeros(row_id.shape, F32)
+    for index, row in enumerate(rows):
+        value = jnp.where(row_id == index, row, value)
+    return value.astype(dtype)
+
+
 def tile_kernel(
-    brow, bcol, panel_dev, slot_rows, place_ref, map_ref, chunk_ref, out_ref, real_ref, imag_ref,
-    target_ref, density_ref, turned_ref, built_real_ref, built_imag_ref, sum_ref, sems,
+    brow, bcol, panel_dev, slot_rows, rank_ref, map_ref, chunk_ref, out_ref, tile_ref,
+    target_ref, density_ref, turned_ref, distance_ref, built_ref, sum_ref, sems,
 ):
     count_all = brow * bcol * panel_dev
     soften = 0.5 * float(count_all) ** (-1.0 / 3.0)
     each = POINT_ROWS // 3
-    row_index, col_index = place_ref[0], place_ref[1]
+    row_index, col_index = high_part(rank_ref[0], bcol), low_part(rank_ref[0], bcol)
     start = bcol * slot_rows + LOAD_ROWS
     block = pl.program_id(0)
 
     def points_of(device):
         return chunk_ref[device].astype(F32)[start : start + POINT_ROWS]
 
-    def copies(index):
-        return (
-            pltpu.make_async_copy(built_real_ref.at[index], real_ref.at[index], sems.at[0, index]),
-            pltpu.make_async_copy(built_imag_ref.at[index], imag_ref.at[index], sems.at[1, index]),
-        )
+    def copy_of(index):
+        return pltpu.make_async_copy(built_ref.at[index], tile_ref.at[index], sems.at[index])
 
     @pl.when(block == 0)
     def prepare():
         near = [points_of(r * bcol + col_index) for r in range(brow)]
+        axes = []
         for axis in range(3):
             rows = []
             for piece in near:
                 for part in range(each):
                     wide = min(LANES, panel_dev - part * LANES)
                     rows.append(piece[axis * each + part : axis * each + part + 1, :wide])
-            target_ref[axis : axis + 1, :] = jnp.concatenate(rows, axis=1)
+            axes.append(jnp.concatenate(rows, axis=1))
+        norms = split_three(squares(axes) + soften * soften)
+        target_ref[...] = rows_of([-2.0 * row for row in axes] + [jnp.ones_like(axes[0])] * 3 + norms)
         sum_ref[...] = jnp.zeros_like(sum_ref)
-        groups = density_groups(place_ref, map_ref, chunk_ref, brow, bcol, panel_dev, slot_rows)
+        groups = density_groups(rank_ref, map_ref, chunk_ref, brow, bcol, panel_dev, slot_rows)
         for group, (density, turned) in enumerate(groups):
             for k in range(BLOCKS):
                 span = slice(k * panel_dev, (k + 1) * panel_dev)
                 density_ref[group * BLOCKS + k] = density[:, span]
                 turned_ref[group * BLOCKS + k] = turned[:, span]
 
-    source = jnp.transpose(points_of(row_index * bcol + block))
+    piece = points_of(row_index * bcol + block)
+    axes = [
+        jnp.concatenate([piece[axis * each + part : axis * each + part + 1] for part in range(each)], axis=1)
+        for axis in range(3)
+    ]
+    norms = split_three(squares(axes))
+    source = jnp.transpose(rows_of(axes + norms + [jnp.ones_like(axes[0])] * 3, F32)).astype(BF16)
+    distance_ref[...] = dot(source[:panel_dev], target_ref[...])
     step = 16
     for top in range(0, panel_dev, step):
-        part, first = top // LANES, top % LANES
-        squared = soften * soften
-        for axis in range(3):
-            column = source[first : first + step, axis * each + part : axis * each + part + 1]
-            delta = column - target_ref[axis : axis + 1, :]
-            squared = squared + delta * delta
+        squared = distance_ref[top : top + step]
         inverse = lax.rsqrt(squared)
         turns = (squared * inverse) * (wave_number / (2.0 * math.pi))
         turns = turns - jnp.floor(turns + 0.5)
@@ -462,46 +482,41 @@
         for factor in COS_POLY[-2::-1]:
             cosine = cosine * z + factor
         double = sine * (inverse * (2.0 / math.sqrt(float(count_all))))
-        built_real_ref[block, top : top + step] = (
+        built_ref[block, 0, top : top + step] = (
             inverse * (1.0 / math.sqrt(float(count_all))) - sine * double
         ).astype(BF16)
-        built_imag_ref[block, top : top + step] = (cosine * double).astype(BF16)
-    for copy in copies(block):
-        copy.start()
-    sum_ref[...] += dot(density_ref[block], built_real_ref[block]) + dot(
-        turned_ref[block], built_imag_ref[block]
+        built_ref[block, 1, top : top + step] = (cosine * double).astype(BF16)
+    copy_of(block).start()
+    sum_ref[...] += dot(density_ref[block], built_ref[block, 0]) + dot(
+        turned_ref[block], built_ref[block, 1]
     )
 
     @pl.when(block == bcol - 1)
     def end():
         write_parts(out_ref, sum_ref[...], panel_dev)
         for index in range(bcol):
-            for copy in copies(index):
-                copy.wait()
+            copy_of(index).wait()
 
 
 def potential_kernel(
-    brow, bcol, panel_dev, slot_rows, place_ref, map_ref, chunk_ref, real_ref, imag_ref, out_ref,
-    held_real_ref, held_imag_ref, sems,
+    brow, bcol, panel_dev, slot_rows, rank_ref, map_ref, chunk_ref, tile_ref, out_ref, held_ref, sems,
 ):
-    copies = (
-        pltpu.make_async_copy(real_ref, held_real_ref, sems.at[0]),
-        pltpu.make_async_copy(imag_ref, held_imag_ref, sems.at[1]),
-    )
+    copies = [
+        pltpu.make_async_copy(tile_ref.at[block], held_ref.at[block], sems.at[block])
+        for block in range(bcol)
+    ]
     for copy in copies:
         copy.start()
-    groups = list(density_groups(place_ref, map_ref, chunk_ref, brow, bcol, panel_dev, slot_rows))
-    for copy in copies:
-        copy.wait()
-    total = None
+    whole = None
+    groups = density_groups(rank_ref, map_ref, chunk_ref, brow, bcol, panel_dev, slot_rows)
     for group, (density, turned) in enumerate(groups):
-        here = slice(group * BLOCKS, (group + 1) * BLOCKS)
-        shape = (BLOCKS * panel_dev, brow * panel_dev)
-        part = dot(density, held_real_ref[here].reshape(shape)) + dot(
-            turned, held_imag_ref[here].reshape(shape)
-        )
-        total = part if total is None else total + part
-    write_parts(out_ref, total, panel_dev)
+        for k in range(BLOCKS):
+            block = group * BLOCKS + k
+            copies[block].wait()
+            span = slice(k * panel_dev, (k + 1) * panel_dev)
+            part = dot(density[:, span], held_ref[block, 0]) + dot(turned[:, span], held_ref[block, 1])
+            whole = part if whole is None else whole + part
+    write_parts(out_ref, whole, panel_dev)
 
 
 def per_device(
@@ -528,7 +543,6 @@
     row_panels = bcol * panel_dev
     row_index, col_index = lax.axis_index("brow"), lax.axis_index("bcol")
     rank = (row_index * bcol + col_index).reshape(1)
-    place = jnp.stack([row_index, col_index])
     mass = node_mass.reshape(1, count)
     nodes_each, elements = element_nodes.shape
     assert elements % GROUP == 0
@@ -565,33 +579,37 @@
 
     hbm = pl.BlockSpec(memory_space=pltpu.HBM)
     hot_shape = (elements // GROUP, width, GROUP * LANES)
-    hot_blocks = max(hot_shape[0], -(-48 * MIB // (2 * width * GROUP * LANES)))
-
-    def sweep(field, rhs, weight, halo=(), weight_before=None):
+    tile_shape = (bcol, HALVES, panel_dev, brow * panel_dev)
+
+    def padded_shape(shape):
+        blocks = max(shape[0], -(-48 * MIB // (2 * math.prod(shape[1:]))))
+        return shape_of((blocks,) + shape[1:], BF16)
+
+    def sweep(field, rhs, weight, halo=(), weight_before=None, hot=None):
         rows = parts * columns
         lanes = GROUP * LANES
-        first = weight_before is None
+        build = hot is None
+        more = () if build else (hot, *halo)
         return call(
-            functools.partial(sweep_kernel, parts, weight, weight_before),
-            field_shape,
+            functools.partial(sweep_kernel, parts, weight, weight_before, build),
+            (field_shape, padded_shape(hot_shape)) if build else field_shape,
             5_000_000_000,
             limit=24,
-            in_specs=[smem, smem] + [vmem] * 5 + [hbm] + [vmem] * len(halo),
-            out_specs=vmem,
-            scratch_shapes=([] if first else [pltpu.VMEM((columns, count), F32)])
+            in_specs=[smem, smem] + [vmem] * 5 + [hbm] * (not build) + [vmem] * len(halo),
+            out_specs=(vmem, hbm) if build else vmem,
+            scratch_shapes=[pltpu.VMEM((columns, count), F32)] * bool(halo)
             + [
                 pltpu.VMEM(hot_shape, BF16),
-                pltpu.SemaphoreType.DMA((elements // GROUP,)),
+                pltpu.SemaphoreType.DMA((hot_shape[0],)),
                 pltpu.VMEM((rows, width), BF16),
                 pltpu.VMEM((rows, width), BF16),
                 pltpu.VMEM((2, rows, lanes), F32),
                 pltpu.VMEM((2, GROUP * columns, 2 * LANES), BF16),
-                pltpu.VMEM((2, GROUP * columns, 2 * LANES), F32),
                 pltpu.VMEM((2, rows, lanes), BF16),
                 pltpu.VMEM((2, rows, lanes), BF16),
                 pltpu.VMEM((rows, width), F32),
             ],
-        )(rank, element_coef, field, rhs, mass, keys, matrix, hot, *halo)
+        )(rank, element_coef, field, rhs, mass, keys, matrix, *more)
 
     def add_loads(chunks, field, halo, weight):
         return call(
@@ -602,12 +620,12 @@
             out_specs=(vmem,) * 4,
         )(rank, load_nodes, chunks, forcing, field, *halo, mass)
 
-    tile_shape = (bcol, panel_dev, brow * panel_dev)
     parts_shape = shape_of((brow, columns, panel_dev), F32)
     sizes = (brow, bcol, panel_dev, slot_rows)
-
-    def sum_parts(parts_out):
-        return lax.psum_scatter(parts_out, "brow", scatter_dimension=0, tiled=False)
+    tile_mib = -(-(2 * math.prod(tile_shape)) // MIB)
+
+    def swap_parts(parts_out):
+        return lax.all_to_all(parts_out, "brow", split_axis=0, concat_axis=0, tiled=True)
 
     nodes, load_nodes, chunks, *rim = call(
         functools.partial(setup_kernel, parts, brow, bcol, panel_dev, slot_rows),
@@ -623,80 +641,66 @@
         in_specs=[smem] + [vmem] * 4,
         out_specs=(vmem,) * 5,
     )(rank, panel_map, field_start, potential_start, panel_points)
-    hot = call(
-        hot_kernel,
-        shape_of((hot_blocks,) + hot_shape[1:], BF16),
-        1_000_000_000,
-        in_specs=[vmem],
-        out_specs=hbm,
-        scratch_shapes=[pltpu.VMEM(hot_shape, BF16), pltpu.SemaphoreType.DMA((hot_shape[0],))],
-    )(keys)
     halo = exchange(*rim)
     chunks = swap_all(chunks)
-    field = sweep(field_start, forcing, weights[0])
-    parts_out, real_tile, imag_tile = call(
+    field, hot = sweep(field_start, forcing, weights[0])
+    parts_out, tiles = call(
         functools.partial(tile_kernel, *sizes),
-        (parts_shape, shape_of(tile_shape, BF16), shape_of(tile_shape, BF16)),
+        (parts_shape, padded_shape(tile_shape)),
         8_000_000_000,
-        limit=58,
+        limit=16 + tile_mib,
         grid=(bcol,),
         in_specs=[smem, vmem, vmem],
-        out_specs=(vmem, hbm, hbm),
+        out_specs=(vmem, hbm),
         scratch_shapes=[
-            pltpu.VMEM((8, brow * panel_dev), F32),
+            pltpu.VMEM((16, brow * panel_dev), BF16),
             pltpu.VMEM((bcol, columns, panel_dev), BF16),
             pltpu.VMEM((bcol, columns, panel_dev), BF16),
-            pltpu.VMEM(tile_shape, BF16),
+            pltpu.VMEM((panel_dev, brow * panel_dev), F32),
             pltpu.VMEM(tile_shape, BF16),
             pltpu.VMEM((columns, brow * panel_dev), F32),
-            pltpu.SemaphoreType.DMA((2, bcol)),
+            pltpu.SemaphoreType.DMA((bcol,)),
         ],
-    )(place, panel_map, chunks)
-    potential = sum_parts(parts_out)
+    )(rank, panel_map, chunks)
+    parts_in = swap_parts(parts_out)
     rhs, field, *rim = add_loads(chunks, field, halo, weights[0])
     halo = exchange(*rim)
-    field = sweep(field, rhs, weights[1])
+    field = sweep(field, rhs, weights[1], hot=hot)
     halo_next = exchange(*rims(field, halo, weights[1]))
-    field = sweep(field, rhs, weights[2], halo, weights[1])
+    field = sweep(field, rhs, weights[2], halo, weights[1], hot)
     field, chunks, *rim = call(
         functools.partial(finish_kernel, parts, brow, bcol, panel_dev, slot_rows, weights[2]),
         (field_shape, chunk_shape(used + LOAD_ROWS, 8), rim_shape, rim_shape),
         1_000_000_000,
         in_specs=[smem] + [vmem] * 7,
         out_specs=(vmem,) * 4,
-    )(rank, panel_map, nodes, field, *halo_next, mass, potential)
+    )(rank, panel_map, nodes, field, *halo_next, mass, parts_in)
 
     halo = exchange(*rim)
     chunks = swap_all(chunks)
-    field = sweep(field, forcing, weights[0])
+    field = sweep(field, forcing, weights[0], hot=hot)
     parts_out = call(
         functools.partial(potential_kernel, *sizes),
         parts_shape,
         2_000_000_000,
-        limit=58,
-        in_specs=[smem, vmem, vmem, hbm, hbm],
+        limit=16 + tile_mib,
+        in_specs=[smem, vmem, vmem, hbm],
         out_specs=vmem,
-        scratch_shapes=[
-            pltpu.VMEM(tile_shape, BF16),
-            pltpu.VMEM(tile_shape, BF16),
-            pltpu.SemaphoreType.DMA((2,)),
-        ],
-    )(place, panel_map, chunks, real_tile, imag_tile)
-    parts_out, field = lax.optimization_barrier((parts_out, field))
-    potential = sum_parts(parts_out)
+        scratch_shapes=[pltpu.VMEM(tile_shape, BF16), pltpu.SemaphoreType.DMA((bcol,))],
+    )(rank, panel_map, chunks, tiles)
+    parts_in = swap_parts(parts_out)
     rhs, field, *rim = add_loads(chunks, field, halo, weights[0])
     halo = exchange(*rim)
-    field = sweep(field, rhs, weights[1])
+    field = sweep(field, rhs, weights[1], hot=hot)
     halo_next = exchange(*rims(field, halo, weights[1]))
-    field = sweep(field, rhs, weights[2], halo, weights[1])
-    field = call(
+    field = sweep(field, rhs, weights[2], halo, weights[1], hot)
+    return call(
         functools.partial(last_kernel, weights[2]),
-        field_shape,
+        (field_shape, shape_of((columns, panel_dev), F32)),
         100_000_000,
-        in_specs=[smem] + [vmem] * 4,
-        out_specs=vmem,
-    )(rank, field, *halo_next, mass)
-    return (field, potential)
+        in_specs=[smem] + [vmem] * 5,
+        out_specs=(vmem, vmem),
+    )(rank, field, *halo_next, mass, parts_in)
 
 
 def solution(mesh):

time: 140 us -> 127 us (0.907)
  between operations: 14.5 us -> 1.08 us
  local copies, waits for them, and re-layouts: 2.69 us -> 8.38 us
  waiting for transfers between devices: 4.94 us -> 0.04 us
  starting transfers between devices: 43.1 us -> 47.6 us
  Pallas kernels: 71.7 us -> 67.9 us
    all_to_all x0 -> x2, starting transfers between devices: none -> 7.59 us  [swap_parts(): lax.all_to_all(parts_out, 'brow', split_axis=0, concat_axis=0, tiled=True)]
    unnamed x4 -> x0, waiting for transfers between devices: 4.9 us -> none
    unnamed x26 -> x28, local copies, waits for them, and re-layouts: 2.67 us -> 6.8 us
    all_to_all x2, starting transfers between devices: 11 us -> 8.44 us  [swap_all(): return lax.all_to_all(chunks, AXES, split_axis=0, concat_axis=0, tiled=True)]
    pallas_call x9 -> x8, Pallas kernels: 60.8 us -> 58.3 us  [the longest x6 47.3 us: sweep(): call(functools.partial(sweep_kernel, parts, weight, weight_before, build)...]
  transfers between devices with their start and end apart: 16 -> 16, of which waited for: 2 -> 0; matrix products, arithmetic and copies ran while one was open for 1% -> 1% of each run, Pallas kernels for 48% -> 50%
where the time goes in v1:
time: 127 us; the launch traced here: 125 us
  Pallas kernels  67.9 us (53%)
  starting transfers between devices  47.6 us (37%)
  local copies, waits for them, and re-layouts  8.38 us (7%)
    pallas_call x6, Pallas kernels, sweep(): call(functools.partial(sweep_kernel, parts, weight, weight_before, build)...  47.3 us
    ppermute x6, starting transfers between devices, exchange(): lax.ppermute(second, AXES, odd_pairs)  30.5 us
    pallas_call x1, Pallas kernels, per_device(): call(functools.partial(tile_kernel, *sizes), (parts_shape, padded_shape(t...  10.2 us
    all_to_all x2, starting transfers between devices, swap_all(): return lax.all_to_all(chunks, AXES, split_axis=0, concat_axis=0, tiled=True)  8.44 us
    all_to_all x2, starting transfers between devices, swap_parts(): lax.all_to_all(parts_out, 'brow', split_axis=0, concat_axis=0, tiled=True)  7.59 us
    unnamed x28, local copies, waits for them, and re-layouts  6.8 us
    pallas_call x1, Pallas kernels, per_device(): call(functools.partial(potential_kernel, *sizes), parts_shape, 2000000000...  4 us
    pallas_call x1, Pallas kernels, per_device(): call(functools.partial(setup_kernel, parts, brow, bcol, panel_dev, slot_r...  3.24 us
  transfers between devices with their start and end apart: 16, of which 0 were waited for; matrix products, arithmetic and copies ran while one was open for 1% of the time, Pallas kernels for 50%

profile of v1, /device:TPU:4, one launch (start us, length us, event | category | flops | bytes accessed | tf_op | source)
XLA Modules:
  0.0 125.0 jit_solution(15852606625701250232)
XLA Ops:
  0.6 0.0 copy-start.9
  0.6 0.0 copy-start.5
  0.7 3.2 %shard_map.104 = (s32[8,512]{1,0:T(8,128)}, s32[8,512]{1,0:T(8,128)}, bf16[32,64,128]{2,1,0:T(8,128)(2,1)}, bf16[64,128]{1,0:T(8,128)(2,1)}, bf16[64,128]{1,0:T(8,128)(2,1)}) custom-call(s32[1]{0:T(128)} %bitcast.rank_ref, s32[3,6144]{1,0:T(4,128)} %map_ref.7, f32[64,2048]{1,0:T(8,128)} %field_ref.3, f32[64,192]{1,0:T(8,128)} %potential_ref.1, ...), custom_call_target="tpu_custom_call" | custom-call | flops 2000000000 | bytes 1048576 | tf_op jit(solution)/shard_map/pallas_call | solution.py:630
  3.9 6.1 %all-to-all-start = ((bf16[32,64,128]{2,1,0:T(8,128)(2,1)}), bf16[32,64,128]{2,1,0:T(8,128)(2,1)S(1)}, u32[]{:S(2)}, u32[]{:S(2)}) async-start(bf16[32,64,128]{2,1,0:T(8,128)(2,1)} %get-tuple-element.25), calls=%async_computation | async-start | bytes 1048576 | tf_op jit(solution)/shard_map/all_to_all | solution.py:578
  10.0 0.2 collective-permute-start
  10.2 6.1 %collective-permute-start.1 = (bf16[64,128]{1,0:T(8,128)(2,1)}, bf16[64,128]{1,0:T(8,128)(2,1)S(1)}, u32[]{:S(2)}, u32[]{:S(2)}) collective-permute-start(bf16[64,128]{1,0:T(8,128)(2,1)} %get-tuple-element.28), channel_id=1, source_target_pairs={{1,2},{2,1},{3,4},{4,3},{5,6},{6,5},{7,8},{8,7},{9,10},{10,9},{11,... | collective-permute-start | bytes 49160 | tf_op jit(solution)/shard_map/ppermute | solution.py:567
  16.3 0.7 pad.8.keys_ref
  17.0 0.8 pad.9.matrix_ref
  17.9 1.0 copy-done
  18.9 0.7 copy-done.3
  19.6 0.7 copy-done.8
  20.3 1.0 copy-done.10
  21.3 7.2 %shard_map.105 = (f32[64,2048]{1,0:T(8,128)S(1)}, bf16[48,512,1024]{2,1,0:T(8,128)(2,1)}) custom-call(s32[1]{0:T(128)} %bitcast.rank_ref, f32[32]{0:T(128)S(1)} %copy-done.8, f32[64,2048]{1,0:T(8,128)S(1)} %copy-done.10, f32[64,2048]{1,0:T(8,128)S(1)} %copy-done, f32[1,2048]{1,0:T(1,128)S(1)} %bitcast.7, s32[32,128]{1,0:T(8,128)S(1)} %pad.8.keys_ref, ...), custom_call_target="tpu_custom_call" | custom-call | flops 5000000000 | bytes 1048576 | tf_op jit(solution)/shard_map/pallas_call | solution.py:593
  28.6 0.0 collective-permute-done.first_ref
  28.6 0.0 collective-permute-done.1.second_ref
  28.6 0.0 all-to-all-done.chunk_ref
  28.6 0.0 copy-start.1
  28.6 1.0 copy-done.1
  29.6 0.7 copy-done.4
  30.3 0.7 copy-done.11
  31.1 0.4 shard_map.106
  31.5 0.1 collective-permute-start.2
  31.6 3.1 %collective-permute-start.3 = (bf16[64,128]{1,0:T(8,128)(2,1)S(1)}, bf16[64,128]{1,0:T(8,128)(2,1)S(1)}, u32[]{:S(2)}, u32[]{:S(2)}) collective-permute-start(bf16[64,128]{1,0:T(8,128)(2,1)S(1)} %get-tuple-element.33), channel_id=1, source_target_pairs={{1,2},{2,1},{3,4},{4,3},{5,6},{6,5},{7,8},{8,7},{9,10},{10,9},{11,... | collective-permute-start | bytes 49160 | tf_op jit(solution)/shard_map/ppermute | solution.py:567
  34.6 0.0 copy-start.6
  34.6 0.9 copy-done.6
  35.5 10.2 %shard_map.109 = (f32[4,64,192]{2,1,0:T(8,128)}, bf16[86,2,192,768]{3,2,1,0:T(8,128)(2,1)}) custom-call(s32[1]{0:T(128)} %bitcast.rank_ref, s32[3,6144]{1,0:T(4,128)S(1)} %copy-done.6, bf16[32,64,128]{2,1,0:T(8,128)(2,1)S(1)} %all-to-all-done.chunk_ref), custom_call_target="tpu_custom_call" | custom-call | flops 8000000000 | bytes 1048576 | tf_op jit(solution)/shard_map/pallas_call | solution.py:647
  45.7 3.6 %all-to-all-start.1 = ((f32[4,64,192]{2,1,0:T(8,128)}), f32[4,64,192]{2,1,0:T(8,128)S(1)}, u32[]{:S(2)}, u32[]{:S(2)}) async-start(f32[4,64,192]{2,1,0:T(8,128)} %get-tuple-element.34), calls=%async_computation.1 | async-start | bytes 524288 | tf_op jit(solution)/shard_map/all_to_all | solution.py:628
  49.3 0.0 copy-start.7
  49.3 0.0 copy-start.13
  49.4 0.0 copy-start.2
  49.4 8.0 %shard_map.107.field_ref = f32[64,2048]{1,0:T(8,128)S(1)} custom-call(s32[1]{0:T(128)} %bitcast.rank_ref, f32[32]{0:T(128)S(1)} %copy-done.9, f32[64,2048]{1,0:T(8,128)S(1)} %get-tuple-element.29.field_ref, f32[64,2048]{1,0:T(8,128)S(1)} %get-tuple-element.30.rhs_ref, f32[1,2048]{1,0:T(1,128)S(1)} %bitcast.10, s32[32,128]{1,0:T(8,128)S(1)} %pad.8.keys_ref, ...), custom_call_target="tpu_custom_call" | custom-call | flops 5000000000 | bytes 1048576 | tf_op jit(solution)/shard_map/pallas_call | solution.py:593
  57.4 0.0 collective-permute-done.2.more_refs_1_
  57.4 0.0 collective-permute-done.3.more_refs_2_
  57.4 6.1 %collective-permute-start.5 = (bf16[64,128]{1,0:T(8,128)(2,1)S(1)}, bf16[64,128]{1,0:T(8,128)(2,1)S(1)}, u32[]{:S(2)}, u32[]{:S(2)}) collective-permute-start(bf16[64,128]{1,0:T(8,128)(2,1)S(1)} %get-tuple-element.46), channel_id=1, source_target_pairs={{1,2},{2,1},{3,4},{4,3},{5,6},{6,5},{7,8},{8,7},{9,10},{10,9},{11,... | collective-permute-start | bytes 49160 | tf_op jit(solution)/shard_map/ppermute | solution.py:567
  63.6 0.1 collective-permute-start.4
  63.6 8.0 %shard_map.108.field_ref = f32[64,2048]{1,0:T(8,128)S(1)} custom-call(s32[1]{0:T(128)} %bitcast.rank_ref, f32[32]{0:T(128)S(1)} %copy-done.9, f32[64,2048]{1,0:T(8,128)S(1)} %shard_map.107.field_ref, f32[64,2048]{1,0:T(8,128)S(1)} %get-tuple-element.30.rhs_ref, f32[1,2048]{1,0:T(1,128)S(1)} %bitcast.11, s32[32,128]{1,0:T(8,128)S(1)} %pad.8.keys_ref, ...), custom_call_target="tpu_custom_call" | custom-call | flops 5000000000 | bytes 1048576 | tf_op jit(solution)/shard_map/pallas_call | solution.py:593
  71.7 0.0 collective-permute-done.5.second_ref
  71.7 0.0 collective-permute-done.4.first_ref
  71.7 0.0 all-to-all-done.1.parts_ref
  71.7 0.0 copy-done.7
  71.7 0.0 copy-done.13
  71.7 1.5 %shard_map.110 = (f32[64,2048]{1,0:T(8,128)S(1)}, bf16[32,56,128]{2,1,0:T(8,128)(2,1)}, bf16[64,128]{1,0:T(8,128)(2,1)S(1)}, bf16[64,128]{1,0:T(8,128)(2,1)S(1)}) custom-call(s32[1]{0:T(128)} %bitcast.rank_ref, s32[3,6144]{1,0:T(4,128)S(1)} %copy-done.7, s32[8,512]{1,0:T(8,128)S(1)} %copy-done.13, f32[64,2048]{1,0:T(8,128)S(1)} %shard_map.108.field_ref, ...), custom_call_target="tpu_custom_call" | custom-call | flops 1000000000 | bytes 1048576 | tf_op jit(solution)/shard_map/pallas_call | solution.py:671
  73.2 2.3 %all-to-all-start.2 = ((bf16[32,56,128]{2,1,0:T(8,128)(2,1)}), bf16[32,56,128]{2,1,0:T(8,128)(2,1)S(1)}, u32[]{:S(2)}, u32[]{:S(2)}) async-start(bf16[32,56,128]{2,1,0:T(8,128)(2,1)} %get-tuple-element.35), calls=%async_computation.2 | async-start | bytes 917504 | tf_op jit(solution)/shard_map/all_to_all | solution.py:578
  75.5 0.6 collective-permute-start.6
  76.1 5.9 %collective-permute-start.7 = (bf16[64,128]{1,0:T(8,128)(2,1)S(1)}, bf16[64,128]{1,0:T(8,128)(2,1)S(1)}, u32[]{:S(2)}, u32[]{:S(2)}) collective-permute-start(bf16[64,128]{1,0:T(8,128)(2,1)S(1)} %get-tuple-element.38), channel_id=1, source_target_pairs={{1,2},{2,1},{3,4},{4,3},{5,6},{6,5},{7,8},{8,7},{9,10},{10,9},{11,... | collective-permute-start | bytes 49160 | tf_op jit(solution)/shard_map/ppermute | solution.py:567
  82.0 8.0 %shard_map.111.field_ref = f32[64,2048]{1,0:T(8,128)S(1)} custom-call(s32[1]{0:T(128)} %bitcast.rank_ref, f32[32]{0:T(128)S(1)} %copy-done.9, f32[64,2048]{1,0:T(8,128)S(1)} %get-tuple-element.36.field_ref, f32[64,2048]{1,0:T(8,128)S(1)} %copy-done.2, f32[1,2048]{1,0:T(1,128)S(1)} %bitcast.13, s32[32,128]{1,0:T(8,128)S(1)} %pad.8.keys_ref, ...), custom_call_target="tpu_custom_call" | custom-call | flops 5000000000 | bytes 1048576 | tf_op jit(solution)/shard_map/pallas_call | solution.py:593
  90.0 0.0 all-to-all-done.2.chunk_ref
  90.0 4.0 %shard_map.115 = f32[4,64,192]{2,1,0:T(8,128)} custom-call(s32[1]{0:T(128)} %bitcast.rank_ref, s32[3,6144]{1,0:T(4,128)S(1)} %copy-done.7, bf16[32,56,128]{2,1,0:T(8,128)(2,1)S(1)} %all-to-all-done.2.chunk_ref, bf16[86,2,192,768]{3,2,1,0:T(8,128)(2,1)} %get-tuple-element.43.tile_ref), custom_call_target="tpu_custom_call" | custom-call | flops 2000000000 | bytes 1048576 | tf_op jit(solution)/shard_map/pallas_call | solution.py:682
  94.0 4.0 %all-to-all-start.3 = ((f32[4,64,192]{2,1,0:T(8,128)}), f32[4,64,192]{2,1,0:T(8,128)S(1)}, u32[]{:S(2)}, u32[]{:S(2)}) async-start(f32[4,64,192]{2,1,0:T(8,128)} %shard_map.115), calls=%async_computation.3 | async-start | bytes 524288 | tf_op jit(solution)/shard_map/all_to_all | solution.py:628
  98.0 0.0 collective-permute-done.6.first_ref
  98.0 0.0 collective-permute-done.7.second_ref
  98.0 0.4 shard_map.112
  98.5 0.1 collective-permute-start.8
  98.5 3.4 %collective-permute-start.9 = (bf16[64,128]{1,0:T(8,128)(2,1)S(1)}, bf16[64,128]{1,0:T(8,128)(2,1)S(1)}, u32[]{:S(2)}, u32[]{:S(2)}) collective-permute-start(bf16[64,128]{1,0:T(8,128)(2,1)S(1)} %get-tuple-element.42), channel_id=1, source_target_pairs={{1,2},{2,1},{3,4},{4,3},{5,6},{6,5},{7,8},{8,7},{9,10},{10,9},{11,... | collective-permute-start | bytes 49160 | tf_op jit(solution)/shard_map/ppermute | solution.py:567
  101.9 8.0 %shard_map.113.field_ref = f32[64,2048]{1,0:T(8,128)S(1)} custom-call(s32[1]{0:T(128)} %bitcast.rank_ref, f32[32]{0:T(128)S(1)} %copy-done.9, f32[64,2048]{1,0:T(8,128)S(1)} %get-tuple-element.39.field_ref, f32[64,2048]{1,0:T(8,128)S(1)} %get-tuple-element.40.rhs_ref, f32[1,2048]{1,0:T(1,128)S(1)} %bitcast.15, s32[32,128]{1,0:T(8,128)S(1)} %pad.8.keys_ref, ...), custom_call_target="tpu_custom_call" | custom-call | flops 5000000000 | bytes 1048576 | tf_op jit(solution)/shard_map/pallas_call | solution.py:593
  109.9 0.0 collective-permute-done.8.more_refs_1_
  110.0 0.0 collective-permute-done.9.more_refs_2_
  110.0 6.0 %collective-permute-start.11 = (bf16[64,128]{1,0:T(8,128)(2,1)S(1)}, bf16[64,128]{1,0:T(8,128)(2,1)S(1)}, u32[]{:S(2)}, u32[]{:S(2)}) collective-permute-start(bf16[64,128]{1,0:T(8,128)(2,1)S(1)} %get-tuple-element.44), channel_id=1, source_target_pairs={{1,2},{2,1},{3,4},{4,3},{5,6},{6,5},{7,8},{8,7},{9,10},{10,9},{11,... | collective-permute-start | bytes 49160 | tf_op jit(solution)/shard_map/ppermute | solution.py:567
  116.0 0.1 collective-permute-start.10
  116.1 8.0 %shard_map.114.field_ref = f32[64,2048]{1,0:T(8,128)S(1)} custom-call(s32[1]{0:T(128)} %bitcast.rank_ref, f32[32]{0:T(128)S(1)} %copy-done.9, f32[64,2048]{1,0:T(8,128)S(1)} %shard_map.113.field_ref, f32[64,2048]{1,0:T(8,128)S(1)} %get-tuple-element.40.rhs_ref, f32[1,2048]{1,0:T(1,128)S(1)} %bitcast.16, s32[32,128]{1,0:T(8,128)S(1)} %pad.8.keys_ref, ...), custom_call_target="tpu_custom_call" | custom-call | flops 5000000000 | bytes 1048576 | tf_op jit(solution)/shard_map/pallas_call | solution.py:593
  124.2 0.0 collective-permute-done.11.second_ref
  124.2 0.0 collective-permute-done.10.first_ref
  124.2 0.0 all-to-all-done.3.parts_ref
  124.2 0.9 shard_map.116
  (14 shorter events, 0.1 us)
Async XLA Ops:
  0.6 48.7 %copy-start.9 = (f32[32]{0:T(128)S(1)}, f32[32]{0:T(128)}, u32[]{:S(2)}) copy-start(f32[32]{0:T(128)} %coef_ref.11) | copy-start | bytes 388
  0.6 48.7 %copy-start.5 = (f32[2048]{0:T(1024)S(1)}, f32[2048]{0:T(1024)}, u32[]{:S(2)}) copy-start(f32[2048]{0:T(1024)} %param.14) | copy-start | bytes 24580
  3.9 24.7 %all-to-all-start = ((bf16[32,64,128]{2,1,0:T(8,128)(2,1)}), bf16[32,64,128]{2,1,0:T(8,128)(2,1)S(1)}, u32[]{:S(2)}, u32[]{:S(2)}) async-start(bf16[32,64,128]{2,1,0:T(8,128)(2,1)} %get-tuple-element.25), calls=%async_computation | async-start | bytes 1048576 | tf_op jit(solution)/shard_map/all_to_all | solution.py:578
  10.0 18.6 %collective-permute-start = (bf16[64,128]{1,0:T(8,128)(2,1)}, bf16[64,128]{1,0:T(8,128)(2,1)S(1)}, u32[]{:S(2)}, u32[]{:S(2)}) collective-permute-start(bf16[64,128]{1,0:T(8,128)(2,1)} %get-tuple-element.27), channel_id=1, source_target_pairs={{0,1},{1,0},{2,3},{3,2},{4,5},{5,4},{6,7},{7,6},{8,9},{9,8},{10,11... | collective-permute-start | bytes 49160 | tf_op jit(solution)/shard_map/ppermute | solution.py:567
  10.2 18.4 %collective-permute-start.1 = (bf16[64,128]{1,0:T(8,128)(2,1)}, bf16[64,128]{1,0:T(8,128)(2,1)S(1)}, u32[]{:S(2)}, u32[]{:S(2)}) collective-permute-start(bf16[64,128]{1,0:T(8,128)(2,1)} %get-tuple-element.28), channel_id=1, source_target_pairs={{1,2},{2,1},{3,4},{4,3},{5,6},{6,5},{7,8},{8,7},{9,10},{10,9},{11,... | collective-permute-start | bytes 49160 | tf_op jit(solution)/shard_map/ppermute | solution.py:567
  17.9 1.0 copy-start
  18.9 0.7 copy-start.3
  19.6 0.7 copy-start.8
  20.3 1.0 copy-start.10
  28.6 1.0 copy-start.1
  29.6 0.7 copy-start.4
  30.3 0.7 copy-start.11
  31.5 25.9 %collective-permute-start.2 = (bf16[64,128]{1,0:T(8,128)(2,1)S(1)}, bf16[64,128]{1,0:T(8,128)(2,1)S(1)}, u32[]{:S(2)}, u32[]{:S(2)}) collective-permute-start(bf16[64,128]{1,0:T(8,128)(2,1)S(1)} %get-tuple-element.32), channel_id=1, source_target_pairs={{0,1},{1,0},{2,3},{3,2},{4,5},{5,4},{6,7},{7,6},{8,9},{9,8},{10,11... | collective-permute-start | bytes 49160 | tf_op jit(solution)/shard_map/ppermute | solution.py:567
  31.6 25.8 %collective-permute-start.3 = (bf16[64,128]{1,0:T(8,128)(2,1)S(1)}, bf16[64,128]{1,0:T(8,128)(2,1)S(1)}, u32[]{:S(2)}, u32[]{:S(2)}) collective-permute-start(bf16[64,128]{1,0:T(8,128)(2,1)S(1)} %get-tuple-element.33), channel_id=1, source_target_pairs={{1,2},{2,1},{3,4},{4,3},{5,6},{6,5},{7,8},{8,7},{9,10},{10,9},{11,... | collective-permute-start | bytes 49160 | tf_op jit(solution)/shard_map/ppermute | solution.py:567
  34.6 0.9 copy-start.6
  45.7 26.0 %all-to-all-start.1 = ((f32[4,64,192]{2,1,0:T(8,128)}), f32[4,64,192]{2,1,0:T(8,128)S(1)}, u32[]{:S(2)}, u32[]{:S(2)}) async-start(f32[4,64,192]{2,1,0:T(8,128)} %get-tuple-element.34), calls=%async_computation.1 | async-start | bytes 524288 | tf_op jit(solution)/shard_map/all_to_all | solution.py:628
  49.3 22.4 %copy-start.7 = (s32[3,6144]{1,0:T(4,128)S(1)}, s32[3,6144]{1,0:T(4,128)}, u32[]{:S(2)}) copy-start(s32[3,6144]{1,0:T(4,128)} %map_ref.7) | copy-start | bytes 221188
  49.3 22.4 %copy-start.13 = (s32[8,512]{1,0:T(8,128)S(1)}, s32[8,512]{1,0:T(8,128)}, u32[]{:S(2)}) copy-start(s32[8,512]{1,0:T(8,128)} %get-tuple-element.24.nodes_ref) | copy-start | bytes 49156
  49.4 32.6 %copy-start.2 = (f32[64,2048]{1,0:T(8,128)S(1)}, f32[64,2048]{1,0:T(8,128)}, u32[]{:S(2)}) copy-start(f32[64,2048]{1,0:T(8,128)} %forcing_ref.3) | copy-start | bytes 1572868
  57.4 14.2 %collective-permute-start.5 = (bf16[64,128]{1,0:T(8,128)(2,1)S(1)}, bf16[64,128]{1,0:T(8,128)(2,1)S(1)}, u32[]{:S(2)}, u32[]{:S(2)}) collective-permute-start(bf16[64,128]{1,0:T(8,128)(2,1)S(1)} %get-tuple-element.46), channel_id=1, source_target_pairs={{1,2},{2,1},{3,4},{4,3},{5,6},{6,5},{7,8},{8,7},{9,10},{10,9},{11,... | collective-permute-start | bytes 49160 | tf_op jit(solution)/shard_map/ppermute | solution.py:567
  63.6 8.1 %collective-permute-start.4 = (bf16[64,128]{1,0:T(8,128)(2,1)S(1)}, bf16[64,128]{1,0:T(8,128)(2,1)S(1)}, u32[]{:S(2)}, u32[]{:S(2)}) collective-permute-start(bf16[64,128]{1,0:T(8,128)(2,1)S(1)} %get-tuple-element.47), channel_id=1, source_target_pairs={{0,1},{1,0},{2,3},{3,2},{4,5},{5,4},{6,7},{7,6},{8,9},{9,8},{10,11... | collective-permute-start | bytes 49160 | tf_op jit(solution)/shard_map/ppermute | solution.py:567
  73.2 16.8 %all-to-all-start.2 = ((bf16[32,56,128]{2,1,0:T(8,128)(2,1)}), bf16[32,56,128]{2,1,0:T(8,128)(2,1)S(1)}, u32[]{:S(2)}, u32[]{:S(2)}) async-start(bf16[32,56,128]{2,1,0:T(8,128)(2,1)} %get-tuple-element.35), calls=%async_computation.2 | async-start | bytes 917504 | tf_op jit(solution)/shard_map/all_to_all | solution.py:578
  75.5 22.5 %collective-permute-start.6 = (bf16[64,128]{1,0:T(8,128)(2,1)S(1)}, bf16[64,128]{1,0:T(8,128)(2,1)S(1)}, u32[]{:S(2)}, u32[]{:S(2)}) collective-permute-start(bf16[64,128]{1,0:T(8,128)(2,1)S(1)} %get-tuple-element.37), channel_id=1, source_target_pairs={{0,1},{1,0},{2,3},{3,2},{4,5},{5,4},{6,7},{7,6},{8,9},{9,8},{10,11... | collective-permute-start | bytes 49160 | tf_op jit(solution)/shard_map/ppermute | solution.py:567
  76.1 21.9 %collective-permute-start.7 = (bf16[64,128]{1,0:T(8,128)(2,1)S(1)}, bf16[64,128]{1,0:T(8,128)(2,1)S(1)}, u32[]{:S(2)}, u32[]{:S(2)}) collective-permute-start(bf16[64,128]{1,0:T(8,128)(2,1)S(1)} %get-tuple-element.38), channel_id=1, source_target_pairs={{1,2},{2,1},{3,4},{4,3},{5,6},{6,5},{7,8},{8,7},{9,10},{10,9},{11,... | collective-permute-start | bytes 49160 | tf_op jit(solution)/shard_map/ppermute | solution.py:567
  82.0 16.1 %copy-start.12 = (s32[8,512]{1,0:T(8,128)S(1)}, s32[8,512]{1,0:T(8,128)}, u32[]{:S(2)}) copy-start(s32[8,512]{1,0:T(8,128)} %get-tuple-element.23.nodes_ref) | copy-start | bytes 49156
  94.0 30.2 %all-to-all-start.3 = ((f32[4,64,192]{2,1,0:T(8,128)}), f32[4,64,192]{2,1,0:T(8,128)S(1)}, u32[]{:S(2)}, u32[]{:S(2)}) async-start(f32[4,64,192]{2,1,0:T(8,128)} %shard_map.115), calls=%async_computation.3 | async-start | bytes 524288 | tf_op jit(solution)/shard_map/all_to_all | solution.py:628
  98.5 11.5 %collective-permute-start.8 = (bf16[64,128]{1,0:T(8,128)(2,1)S(1)}, bf16[64,128]{1,0:T(8,128)(2,1)S(1)}, u32[]{:S(2)}, u32[]{:S(2)}) collective-permute-start(bf16[64,128]{1,0:T(8,128)(2,1)S(1)} %get-tuple-element.41), channel_id=1, source_target_pairs={{0,1},{1,0},{2,3},{3,2},{4,5},{5,4},{6,7},{7,6},{8,9},{9,8},{10,11... | collective-permute-start | bytes 49160 | tf_op jit(solution)/shard_map/ppermute | solution.py:567
  98.5 11.4 %collective-permute-start.9 = (bf16[64,128]{1,0:T(8,128)(2,1)S(1)}, bf16[64,128]{1,0:T(8,128)(2,1)S(1)}, u32[]{:S(2)}, u32[]{:S(2)}) collective-permute-start(bf16[64,128]{1,0:T(8,128)(2,1)S(1)} %get-tuple-element.42), channel_id=1, source_target_pairs={{1,2},{2,1},{3,4},{4,3},{5,6},{6,5},{7,8},{8,7},{9,10},{10,9},{11,... | collective-permute-start | bytes 49160 | tf_op jit(solution)/shard_map/ppermute | solution.py:567
  110.0 14.2 %collective-permute-start.11 = (bf16[64,128]{1,0:T(8,128)(2,1)S(1)}, bf16[64,128]{1,0:T(8,128)(2,1)S(1)}, u32[]{:S(2)}, u32[]{:S(2)}) collective-permute-start(bf16[64,128]{1,0:T(8,128)(2,1)S(1)} %get-tuple-element.44), channel_id=1, source_target_pairs={{1,2},{2,1},{3,4},{4,3},{5,6},{6,5},{7,8},{8,7},{9,10},{10,9},{11,... | collective-permute-start | bytes 49160 | tf_op jit(solution)/shard_map/ppermute | solution.py:567
  116.0 8.1 %collective-permute-start.10 = (bf16[64,128]{1,0:T(8,128)(2,1)S(1)}, bf16[64,128]{1,0:T(8,128)(2,1)S(1)}, u32[]{:S(2)}, u32[]{:S(2)}) collective-permute-start(bf16[64,128]{1,0:T(8,128)(2,1)S(1)} %get-tuple-element.45), channel_id=1, source_target_pairs={{0,1},{1,0},{2,3},{3,2},{4,5},{5,4},{6,7},{7,6},{8,9},{9,8},{10,11... | collective-permute-start | bytes 49160 | tf_op jit(solution)/shard_map/ppermute | solution.py:567

commit v2 on v1

--- a/solution.py
+++ b/solution.py
@@ -34,7 +34,7 @@
     return 1.0 / (1.25 + 0.75 * math.cos(math.pi * (2 * sweep + 1) / (2.0 * SWEEPS)))
 
 
-def call(kernel, out_shape, cost, limit=16, **more):
+def call(kernel, out_shape, cost, limit=28, **more):
     return pl.pallas_call(
         kernel,
         out_shape=out_shape,
@@ -48,6 +48,18 @@
     return jax.ShapeDtypeStruct(shape, dtype)
 
 
+def kept(shape, dtype):
+    return pltpu.VMEM(shape, dtype)
+
+
+def in_hbm(*arrays):
+    return tuple(pltpu.with_memory_space_constraint(array, pltpu.HBM) for array in arrays)
+
+
+def in_vmem(*arrays):
+    return tuple(pltpu.with_memory_space_constraint(array, pltpu.VMEM) for array in arrays)
+
+
 def dot(a, b):
     return jnp.dot(a, b, preferred_element_type=F32)
 
@@ -75,8 +87,8 @@
 
 
 def one_hot_rows(key, rows):
-    seen = lax.broadcasted_iota(jnp.int32, (rows, key.shape[1]), 0)
-    return jnp.where(seen == key, 1.0, 0.0).astype(BF16)
+    seen = lax.broadcasted_iota(jnp.int16, (rows, key.shape[1]), 0)
+    return jnp.where(seen == key.astype(jnp.int16), BF16(1), BF16(0))
 
 
 def pick_part(stacked, part, parts):
@@ -195,18 +207,28 @@
 
 def setup_kernel(
     parts, brow, bcol, panel_dev, slot_rows, rank_ref, map_ref, field_ref, potential_ref, points_ref,
-    nodes_ref, load_nodes_ref, chunk_ref, rim_first_ref, rim_second_ref,
+    element_nodes_ref, element_matrix_ref, node_mass_ref,
+    nodes_ref, load_nodes_ref, row_map_ref, own_map_ref, keys_ref, matrix_ref, mass_ref,
+    chunk_ref, rim_first_ref, rim_second_ref,
 ):
     rank = rank_ref[0]
+    row_panels = bcol * panel_dev
+    base = pl.multiple_of(high_part(rank, bcol) * row_panels, LANES)
+    row_map_ref[...] = map_ref[:, pl.ds(base, row_panels)]
+    own_map = own_panels(map_ref, rank, panel_dev)
+    own_map_ref[...] = own_map
+    keys_ref[...] = jnp.zeros_like(keys_ref)
+    keys_ref[:, : element_nodes_ref.shape[1]] = element_nodes_ref[...]
+    matrix_ref[...] = jnp.zeros_like(matrix_ref)
+    matrix_ref[: element_matrix_ref.shape[0], : element_matrix_ref.shape[1]] = element_matrix_ref[...]
+    mass_ref[...] = node_mass_ref[...]
     tables = functools.partial(node_tables, map_ref, rank, brow, bcol, panel_dev, slot_rows)
     nodes = tables(slot_rows)
     nodes_ref[...] = jnp.broadcast_to(nodes, nodes_ref.shape)
     load_nodes_ref[...] = jnp.broadcast_to(tables(LOAD_ROWS), load_nodes_ref.shape)
     field = field_ref[...]
     write_rims(field, low_part(rank, 2) == 0, rim_first_ref, rim_second_ref)
-    loads = load_rows(
-        potential_ref[...], own_panels(map_ref, rank, panel_dev), brow * bcol, slot_rows
-    )
+    loads = load_rows(potential_ref[...], own_map, brow * bcol, slot_rows)
     pieces = trace_rows(field, nodes, parts, brow, bcol * slot_rows)
     write_chunks(chunk_ref, pieces, loads, bcol, point_rows(points_ref[...].astype(F32)))
 
@@ -237,19 +259,16 @@
     matrix_ref, *more_refs,
 ):
     if build:
-        out_ref, hot_ref, *scratch = more_refs
+        out_ref, hot_ref, total_ref, sem, *scratch = more_refs
+        copy = pltpu.make_async_copy(rhs_ref, total_ref, sem)
+        copy.start()
+        rhs_ref = total_ref
     elif weight_before is None:
         hot_ref, out_ref, *scratch = more_refs
     else:
         hot_ref, first_ref, second_ref, out_ref, field_scr, *scratch = more_refs
-    held_ref, sems, high_ref, low_ref, found_ref, local_ref, yhigh_ref, ylow_ref, sum_ref = scratch
-    groups = held_ref.shape[0]
-    copies = []
-    for group in range(groups):
-        ends = (held_ref.at[group], hot_ref.at[group])
-        copies.append(pltpu.make_async_copy(*(ends if build else ends[::-1]), sems.at[group]))
-        if not build:
-            copies[-1].start()
+    high_ref, low_ref, found_ref, local_ref, yhigh_ref, ylow_ref, sum_ref = scratch
+    groups = hot_ref.shape[0]
     columns, count = field_ref.shape
     width = count // parts
     mass = mass_ref[...]
@@ -278,11 +297,8 @@
         if build:
             for e in range(GROUP):
                 key = keys_ref[group * GROUP + e : group * GROUP + e + 1, :]
-                held_ref[group, :, e * LANES : (e + 1) * LANES] = one_hot_rows(low_part(key, width), width)
-            copies[group].start()
-        else:
-            copies[group].wait()
-        hot = held_ref[group]
+                hot_ref[group, :, e * LANES : (e + 1) * LANES] = one_hot_rows(low_part(key, width), width)
+        hot = hot_ref[group]
         found_ref[group % 2] = dot(high_ref[...], hot) + dot(low_ref[...], hot)
 
     def multiply(group):
@@ -309,7 +325,7 @@
                 ylow_ref[slot, h * columns : (h + 1) * columns, span] = value_low * mask
 
     def scatter(group):
-        hot = held_ref[group]
+        hot = hot_ref[group]
         added = dot_nt(yhigh_ref[group % 2], hot) + dot_nt(ylow_ref[group % 2], hot)
         sum_ref[...] = added if group == 0 else sum_ref[...] + added
 
@@ -320,8 +336,7 @@
         multiply(group)
         scatter(group)
     if build:
-        for copy in copies:
-            copy.wait()
+        copy.wait()
     for h in range(parts):
         span = slice(h * width, (h + 1) * width)
         stiff = sum_ref[h * columns : (h + 1) * columns]
@@ -354,7 +369,7 @@
 
 
 def finish_kernel(
-    parts, brow, bcol, panel_dev, slot_rows, weight, rank_ref, map_ref, nodes_ref, field_ref,
+    parts, brow, bcol, panel_dev, slot_rows, weight, rank_ref, own_map_ref, nodes_ref, field_ref,
     first_ref, second_ref, mass_ref, parts_ref, out_ref, chunk_ref, rim_first_ref, rim_second_ref,
 ):
     rank = rank_ref[0]
@@ -362,9 +377,7 @@
     field = rim_correction(field_ref[...], even, first_ref, second_ref, mass_ref[...], weight)
     out_ref[...] = field
     write_rims(field, even, rim_first_ref, rim_second_ref)
-    loads = load_rows(
-        total(parts_ref), own_panels(map_ref, rank, panel_dev), brow * bcol, slot_rows
-    )
+    loads = load_rows(total(parts_ref), own_map_ref[...], brow * bcol, slot_rows)
     pieces = trace_rows(field, nodes_ref[0:1, :], parts, brow, bcol * slot_rows)
     write_chunks(chunk_ref, pieces, loads, bcol)
 
@@ -377,8 +390,7 @@
     potential_ref[...] = total(parts_ref)
 
 
-def density_groups(rank_ref, map_ref, chunk_ref, brow, bcol, panel_dev, slot_rows):
-    base = pl.multiple_of(high_part(rank_ref[0], bcol) * (bcol * panel_dev), LANES)
+def density_groups(map_ref, chunk_ref, brow, bcol, panel_dev, slot_rows):
     devices = brow * bcol
     columns = LANES // HALVES
     rows = BLOCKS * slot_rows
@@ -387,7 +399,7 @@
     block = jnp.floor((lane + 0.5) * (1.0 / panel_dev)).astype(jnp.int32)
     traces = chunk_ref[...].astype(F32)
     for group in range(bcol // BLOCKS):
-        span = pl.ds(base + group * panels, panels)
+        span = slice(group * panels, (group + 1) * panels)
         owner, slot = map_ref[0:1, span], map_ref[1:2, span]
         half, low = halves_of(slot, slot_rows)
         key = owner * rows + block * slot_rows + low
@@ -423,7 +435,7 @@
 
 def tile_kernel(
     brow, bcol, panel_dev, slot_rows, rank_ref, map_ref, chunk_ref, out_ref, tile_ref,
-    target_ref, density_ref, turned_ref, distance_ref, built_ref, sum_ref, sems,
+    target_ref, density_ref, turned_ref, distance_ref, sum_ref,
 ):
     count_all = brow * bcol * panel_dev
     soften = 0.5 * float(count_all) ** (-1.0 / 3.0)
@@ -434,9 +446,6 @@
 
     def points_of(device):
         return chunk_ref[device].astype(F32)[start : start + POINT_ROWS]
-
-    def copy_of(index):
-        return pltpu.make_async_copy(built_ref.at[index], tile_ref.at[index], sems.at[index])
 
     @pl.when(block == 0)
     def prepare():
@@ -452,7 +461,7 @@
         norms = split_three(squares(axes) + soften * soften)
         target_ref[...] = rows_of([-2.0 * row for row in axes] + [jnp.ones_like(axes[0])] * 3 + norms)
         sum_ref[...] = jnp.zeros_like(sum_ref)
-        groups = density_groups(rank_ref, map_ref, chunk_ref, brow, bcol, panel_dev, slot_rows)
+        groups = density_groups(map_ref, chunk_ref, brow, bcol, panel_dev, slot_rows)
         for group, (density, turned) in enumerate(groups):
             for k in range(BLOCKS):
                 span = slice(k * panel_dev, (k + 1) * panel_dev)
@@ -482,39 +491,29 @@
         for factor in COS_POLY[-2::-1]:
             cosine = cosine * z + factor
         double = sine * (inverse * (2.0 / math.sqrt(float(count_all))))
-        built_ref[block, 0, top : top + step] = (
+        tile_ref[block, 0, top : top + step] = (
             inverse * (1.0 / math.sqrt(float(count_all))) - sine * double
         ).astype(BF16)
-        built_ref[block, 1, top : top + step] = (cosine * double).astype(BF16)
-    copy_of(block).start()
-    sum_ref[...] += dot(density_ref[block], built_ref[block, 0]) + dot(
-        turned_ref[block], built_ref[block, 1]
+        tile_ref[block, 1, top : top + step] = (cosine * double).astype(BF16)
+    sum_ref[...] += dot(density_ref[block], tile_ref[block, 0]) + dot(
+        turned_ref[block], tile_ref[block, 1]
     )
 
     @pl.when(block == bcol - 1)
     def end():
         write_parts(out_ref, sum_ref[...], panel_dev)
-        for index in range(bcol):
-            copy_of(index).wait()
 
 
 def potential_kernel(
-    brow, bcol, panel_dev, slot_rows, rank_ref, map_ref, chunk_ref, tile_ref, out_ref, held_ref, sems,
+    brow, bcol, panel_dev, slot_rows, map_ref, chunk_ref, tile_ref, out_ref,
 ):
-    copies = [
-        pltpu.make_async_copy(tile_ref.at[block], held_ref.at[block], sems.at[block])
-        for block in range(bcol)
-    ]
-    for copy in copies:
-        copy.start()
     whole = None
-    groups = density_groups(rank_ref, map_ref, chunk_ref, brow, bcol, panel_dev, slot_rows)
+    groups = density_groups(map_ref, chunk_ref, brow, bcol, panel_dev, slot_rows)
     for group, (density, turned) in enumerate(groups):
         for k in range(BLOCKS):
             block = group * BLOCKS + k
-            copies[block].wait()
             span = slice(k * panel_dev, (k + 1) * panel_dev)
-            part = dot(density[:, span], held_ref[block, 0]) + dot(turned[:, span], held_ref[block, 1])
+            part = dot(density[:, span], tile_ref[block, 0]) + dot(turned[:, span], tile_ref[block, 1])
             whole = part if whole is None else whole + part
     write_parts(out_ref, whole, panel_dev)
 
@@ -543,11 +542,8 @@
     row_panels = bcol * panel_dev
     row_index, col_index = lax.axis_index("brow"), lax.axis_index("bcol")
     rank = (row_index * bcol + col_index).reshape(1)
-    mass = node_mass.reshape(1, count)
     nodes_each, elements = element_nodes.shape
     assert elements % GROUP == 0
-    keys = jnp.pad(element_nodes.T, ((0, 0), (0, LANES - nodes_each)))
-    matrix = jnp.pad(element_matrix, ((0, LANES - nodes_each), (0, LANES - nodes_each)))
     smem = pl.BlockSpec(memory_space=pltpu.SMEM)
     vmem = pl.BlockSpec(memory_space=pltpu.VMEM)
     rim_shape = shape_of((columns, RIM), BF16)
@@ -561,7 +557,7 @@
         return shape_of((devices, -(-rows // unit) * unit, LANES), BF16)
 
     def table_shape(stride):
-        return shape_of((8, brow * (-(-HALVES * bcol * stride // LANES) * LANES)), jnp.int32)
+        return 8, brow * (-(-HALVES * bcol * stride // LANES) * LANES)
 
     def exchange(first, second):
         return lax.ppermute(first, AXES, even_pairs), lax.ppermute(second, AXES, odd_pairs)
@@ -570,8 +566,8 @@
         first, second = (piece.astype(F32) for piece in halo)
         left, right = jnp.where(even, second, first), jnp.where(even, first, second)
         last = count - RIM
-        low = field[:, :RIM] + (weight * penalty) * left / mass[:, :RIM]
-        high = field[:, last:] + (weight * penalty) * right / mass[:, last:]
+        low = field[:, :RIM] + (weight * penalty) * left / node_mass[:RIM]
+        high = field[:, last:] + (weight * penalty) * right / node_mass[last:]
         return jnp.where(even, high, low).astype(BF16), jnp.where(even, low, high).astype(BF16)
 
     def swap_all(chunks):
@@ -580,27 +576,24 @@
     hbm = pl.BlockSpec(memory_space=pltpu.HBM)
     hot_shape = (elements // GROUP, width, GROUP * LANES)
     tile_shape = (bcol, HALVES, panel_dev, brow * panel_dev)
-
-    def padded_shape(shape):
-        blocks = max(shape[0], -(-48 * MIB // (2 * math.prod(shape[1:]))))
-        return shape_of((blocks,) + shape[1:], BF16)
 
     def sweep(field, rhs, weight, halo=(), weight_before=None, hot=None):
         rows = parts * columns
         lanes = GROUP * LANES
         build = hot is None
-        more = () if build else (hot, *halo)
+        if build:
+            given = (rank, *in_hbm(element_coef, field, rhs), *in_vmem(mass, keys, matrix))
+        else:
+            given = (rank, *in_hbm(element_coef), field, rhs, *in_vmem(mass, keys, matrix, hot), *halo)
         return call(
             functools.partial(sweep_kernel, parts, weight, weight_before, build),
-            (field_shape, padded_shape(hot_shape)) if build else field_shape,
+            (field_shape, kept(hot_shape, BF16), kept((columns, count), F32)) if build else field_shape,
             5_000_000_000,
-            limit=24,
-            in_specs=[smem, smem] + [vmem] * 5 + [hbm] * (not build) + [vmem] * len(halo),
-            out_specs=(vmem, hbm) if build else vmem,
-            scratch_shapes=[pltpu.VMEM((columns, count), F32)] * bool(halo)
+            in_specs=[smem, smem, vmem, hbm if build else vmem] + [vmem] * (len(given) - 4),
+            out_specs=(vmem,) * 3 if build else vmem,
+            scratch_shapes=[pltpu.SemaphoreType.DMA] * build
+            + [pltpu.VMEM((columns, count), F32)] * bool(halo)
             + [
-                pltpu.VMEM(hot_shape, BF16),
-                pltpu.SemaphoreType.DMA((hot_shape[0],)),
                 pltpu.VMEM((rows, width), BF16),
                 pltpu.VMEM((rows, width), BF16),
                 pltpu.VMEM((2, rows, lanes), F32),
@@ -609,7 +602,7 @@
                 pltpu.VMEM((2, rows, lanes), BF16),
                 pltpu.VMEM((rows, width), F32),
             ],
-        )(rank, element_coef, field, rhs, mass, keys, matrix, *more)
+        )(*given)
 
     def add_loads(chunks, field, halo, weight):
         return call(
@@ -618,50 +611,56 @@
             500_000_000,
             in_specs=[smem] + [vmem] * 7,
             out_specs=(vmem,) * 4,
-        )(rank, load_nodes, chunks, forcing, field, *halo, mass)
+        )(rank, *in_vmem(load_nodes), chunks, *in_vmem(forcing_kept), field, *halo, *in_vmem(mass))
 
     parts_shape = shape_of((brow, columns, panel_dev), F32)
     sizes = (brow, bcol, panel_dev, slot_rows)
-    tile_mib = -(-(2 * math.prod(tile_shape)) // MIB)
 
     def swap_parts(parts_out):
         return lax.all_to_all(parts_out, "brow", split_axis=0, concat_axis=0, tiled=True)
 
-    nodes, load_nodes, chunks, *rim = call(
+    (nodes, load_nodes, row_map, own_map, keys, matrix, mass, chunks, *rim) = call(
         functools.partial(setup_kernel, parts, brow, bcol, panel_dev, slot_rows),
         (
-            table_shape(slot_rows),
-            table_shape(LOAD_ROWS),
+            kept(table_shape(slot_rows), jnp.int32),
+            kept(table_shape(LOAD_ROWS), jnp.int32),
+            kept((3, row_panels), jnp.int32),
+            kept((3, panel_dev), jnp.int32),
+            kept((elements, LANES), jnp.int32),
+            kept((LANES, LANES), F32),
+            kept((1, count), F32),
             chunk_shape(used + LOAD_ROWS + POINT_ROWS, 16),
-            rim_shape,
-            rim_shape,
+            kept(rim_shape.shape, BF16),
+            kept(rim_shape.shape, BF16),
         ),
         2_000_000_000,
-        limit=56,
-        in_specs=[smem] + [vmem] * 4,
-        out_specs=(vmem,) * 5,
-    )(rank, panel_map, field_start, potential_start, panel_points)
+        in_specs=[smem] + [vmem] * 7,
+        out_specs=(vmem,) * 10,
+    )(
+        rank,
+        *in_hbm(
+            panel_map, field_start, potential_start, panel_points, element_nodes.T, element_matrix,
+            node_mass.reshape(1, count),
+        ),
+    )
     halo = exchange(*rim)
     chunks = swap_all(chunks)
-    field, hot = sweep(field_start, forcing, weights[0])
+    field, hot, forcing_kept = sweep(field_start, forcing, weights[0])
     parts_out, tiles = call(
         functools.partial(tile_kernel, *sizes),
-        (parts_shape, padded_shape(tile_shape)),
+        (parts_shape, kept(tile_shape, BF16)),
         8_000_000_000,
-        limit=16 + tile_mib,
         grid=(bcol,),
         in_specs=[smem, vmem, vmem],
-        out_specs=(vmem, hbm),
+        out_specs=(vmem, vmem),
         scratch_shapes=[
             pltpu.VMEM((16, brow * panel_dev), BF16),
             pltpu.VMEM((bcol, columns, panel_dev), BF16),
             pltpu.VMEM((bcol, columns, panel_dev), BF16),
             pltpu.VMEM((panel_dev, brow * panel_dev), F32),
-            pltpu.VMEM(tile_shape, BF16),
             pltpu.VMEM((columns, brow * panel_dev), F32),
-            pltpu.SemaphoreType.DMA((bcol,)),
         ],
-    )(rank, panel_map, chunks)
+    )(rank, *in_vmem(row_map), chunks)
     parts_in = swap_parts(parts_out)
     rhs, field, *rim = add_loads(chunks, field, halo, weights[0])
     halo = exchange(*rim)
@@ -674,20 +673,18 @@
         1_000_000_000,
         in_specs=[smem] + [vmem] * 7,
         out_specs=(vmem,) * 4,
-    )(rank, panel_map, nodes, field, *halo_next, mass, parts_in)
+    )(rank, *in_vmem(own_map, nodes), field, *halo_next, *in_vmem(mass), parts_in)
 
     halo = exchange(*rim)
     chunks = swap_all(chunks)
-    field = sweep(field, forcing, weights[0], hot=hot)
+    field = sweep(field, *in_vmem(forcing_kept), weights[0], hot=hot)
     parts_out = call(
         functools.partial(potential_kernel, *sizes),
         parts_shape,
         2_000_000_000,
-        limit=16 + tile_mib,
-        in_specs=[smem, vmem, vmem, hbm],
+        in_specs=[vmem] * 3,
         out_specs=vmem,
-        scratch_shapes=[pltpu.VMEM(tile_shape, BF16), pltpu.SemaphoreType.DMA((bcol,))],
-    )(rank, panel_map, chunks, tiles)
+    )(*in_vmem(row_map), chunks, *in_vmem(tiles))
     parts_in = swap_parts(parts_out)
     rhs, field, *rim = add_loads(chunks, field, halo, weights[0])
     halo = exchange(*rim)
@@ -700,7 +697,7 @@
         100_000_000,
         in_specs=[smem] + [vmem] * 5,
         out_specs=(vmem, vmem),
-    )(rank, field, *halo_next, mass, parts_in)
+    )(rank, field, *halo_next, *in_vmem(mass), parts_in)
 
 
 def solution(mesh):

time: 127 us -> 121 us (0.953); the launches traced: 125 us -> 120 us
  Pallas kernels: 67.9 us -> 58.7 us
  local copies, waits for them, and re-layouts: 8.38 us -> 13.7 us
    pallas_call x6, Pallas kernels: 47.3 us -> 40.7 us  [sweep(): call(functools.partial(sweep_kernel, parts, weight, weight_before, build)...]
    unnamed x28 -> x12, local copies, waits for them, and re-layouts: 6.8 us -> 13 us
    pad x2 -> x0, local copies, waits for them, and re-layouts: 1.57 us -> none  [the longest x1 0.85 us: per_device(): jnp.pad(element_matrix, ((0, LANES - nodes_each), (0, LANES - nodes_each)))]
    pallas_call x1, Pallas kernels: 4 us -> 2.49 us  [per_device(): call(functools.partial(potential_kernel, *sizes), parts_shape, 2000000000...]
  transfers between devices with their start and end apart: 16 -> 16, of which waited for: 0 -> 0; matrix products, arithmetic and copies ran while one was open for 1% -> 1% of each run, Pallas kernels for 50% -> 44%
where the time goes in v2:
time: 121 us; the launch traced here: 120 us
  Pallas kernels  58.7 us (49%)
  starting transfers between devices  46.9 us (39%)
  local copies, waits for them, and re-layouts  13.7 us (11%)
    pallas_call x6, Pallas kernels, sweep(): call(functools.partial(sweep_kernel, parts, weight, weight_before, build)...  40.7 us
    ppermute x6, starting transfers between devices, exchange(): lax.ppermute(second, AXES, odd_pairs)  30.9 us
    unnamed x12, local copies, waits for them, and re-layouts  13 us
    pallas_call x1, Pallas kernels, per_device(): call(functools.partial(tile_kernel, *sizes), (parts_shape, kept(tile_shap...  9.29 us
    all_to_all x2, starting transfers between devices, swap_all(): return lax.all_to_all(chunks, AXES, split_axis=0, concat_axis=0, tiled=True)  8.44 us
    all_to_all x2, starting transfers between devices, swap_parts(): lax.all_to_all(parts_out, 'brow', split_axis=0, concat_axis=0, tiled=True)  6.97 us
    pallas_call x1, Pallas kernels, per_device(): call(functools.partial(setup_kernel, parts, brow, bcol, panel_dev, slot_r...  3.29 us
    pallas_call x1, Pallas kernels, per_device(): call(functools.partial(potential_kernel, *sizes), parts_shape, 2000000000...  2.49 us
  transfers between devices with their start and end apart: 16, of which 0 were waited for; matrix products, arithmetic and copies ran while one was open for 1% of the time, Pallas kernels for 44%

profile of v2, /device:TPU:4, one launch (start us, length us, event | category | flops | bytes accessed | tf_op | source)
XLA Modules:
  0.0 120.4 jit_solution(9897884535989210538)
XLA Ops:
  0.6 3.3 %shard_map.104 = (s32[8,512]{1,0:T(8,128)S(1)}, s32[8,512]{1,0:T(8,128)S(1)}, s32[3,1536]{1,0:T(4,128)S(1)}, s32[3,192]{1,0:T(4,128)S(1)}, s32[32,128]{1,0:T(8,1...) custom-call(s32[1]{0:T(128)} %bitcast.rank_ref, ...), custom_call_target="tpu_custom_call" | custom-call | flops 2000000000 | bytes 1048576 | tf_op jit(solution)/shard_map/pallas_call | solution.py:622
  3.9 6.1 %all-to-all-start = ((bf16[32,64,128]{2,1,0:T(8,128)(2,1)}), bf16[32,64,128]{2,1,0:T(8,128)(2,1)S(1)}, u32[]{:S(2)}, u32[]{:S(2)}) async-start(bf16[32,64,128]{2,1,0:T(8,128)(2,1)} %get-tuple-element.32), calls=%async_computation | async-start | bytes 1048576 | tf_op jit(solution)/shard_map/all_to_all | solution.py:574
  10.0 0.2 collective-permute-start
  10.2 6.1 %collective-permute-start.1 = (bf16[64,128]{1,0:T(8,128)(2,1)S(1)}, bf16[64,128]{1,0:T(8,128)(2,1)S(1)}, u32[]{:S(2)}, u32[]{:S(2)}) collective-permute-start(bf16[64,128]{1,0:T(8,128)(2,1)S(1)} %get-tuple-element.39), channel_id=1, source_target_pairs={{1,2},{2,1},{3,4},{4,3},{5,6},{6,5},{7,8},{8,7},{9,10},{10,9},{11,... | collective-permute-start | bytes 49160 | tf_op jit(solution)/shard_map/ppermute | solution.py:563
  16.3 7.7 %shard_map.105 = (f32[64,2048]{1,0:T(8,128)S(1)}, bf16[4,512,1024]{2,1,0:T(8,128)(2,1)S(1)}, f32[64,2048]{1,0:T(8,128)S(1)}) custom-call(s32[1]{0:T(128)} %bitcast.rank_ref, f32[32]{0:T(128)} %coef_ref.11, f32[64,2048]{1,0:T(8,128)} %field_ref.3, f32[64,2048]{1,0:T(8,128)} %rhs_ref.1, f32[1,2048]{1,0:T(1,128)S(1)} %get-tuple-element.33.mass_ref, ...), custom_call_target="tpu_custom_call" | custom-call | flops 5000000000 | bytes 1048576 | tf_op jit(solution)/shard_map/pallas_call | solution.py:588
  24.0 0.0 copy-start.2
  24.0 2.0 %copy-done.2 = bf16[4,512,1024]{2,1,0:T(8,128)(2,1)} copy-done((bf16[4,512,1024]{2,1,0:T(8,128)(2,1)}, bf16[4,512,1024]{2,1,0:T(8,128)(2,1)S(1)}, u32[]{:S(2)}) %copy-start.2) | copy-done | bytes 4194328
  26.0 0.7 fusion.12
  26.8 0.0 collective-permute-done.first_ref
  26.8 0.0 collective-permute-done.1.second_ref
  26.8 0.0 all-to-all-done.chunk_ref
  26.8 0.4 shard_map.106
  27.2 0.1 collective-permute-start.2
  27.3 3.1 %collective-permute-start.3 = (bf16[64,128]{1,0:T(8,128)(2,1)S(1)}, bf16[64,128]{1,0:T(8,128)(2,1)S(1)}, u32[]{:S(2)}, u32[]{:S(2)}) collective-permute-start(bf16[64,128]{1,0:T(8,128)(2,1)S(1)} %get-tuple-element.44), channel_id=1, source_target_pairs={{1,2},{2,1},{3,4},{4,3},{5,6},{6,5},{7,8},{8,7},{9,10},{10,9},{11,... | collective-permute-start | bytes 49160 | tf_op jit(solution)/shard_map/ppermute | solution.py:563
  30.3 9.3 %shard_map.109 = (f32[4,64,192]{2,1,0:T(8,128)}, bf16[8,2,192,768]{3,2,1,0:T(8,128)(2,1)S(1)}) custom-call(s32[1]{0:T(128)} %bitcast.rank_ref, s32[3,1536]{1,0:T(4,128)S(1)} %get-tuple-element.45.map_ref, bf16[32,64,128]{2,1,0:T(8,128)(2,1)S(1)} %all-to-all-done.chunk_ref), custom_call_target="tpu_custom_call" | custom-call | flops 8000000000 | bytes 1048576 | tf_op jit(solution)/shard_map/pallas_call | solution.py:649
  39.6 0.0 copy-start
  39.6 2.1 %copy-done = bf16[8,2,192,768]{3,2,1,0:T(8,128)(2,1)} copy-done((bf16[8,2,192,768]{3,2,1,0:T(8,128)(2,1)}, bf16[8,2,192,768]{3,2,1,0:T(8,128)(2,1)S(1)}, u32[]{:S(2)}) %copy-start) | copy-done | bytes 4718616
  41.8 3.6 %all-to-all-start.1 = ((f32[4,64,192]{2,1,0:T(8,128)}), f32[4,64,192]{2,1,0:T(8,128)S(1)}, u32[]{:S(2)}, u32[]{:S(2)}) async-start(f32[4,64,192]{2,1,0:T(8,128)} %get-tuple-element.46), calls=%async_computation.1 | async-start | bytes 524288 | tf_op jit(solution)/shard_map/all_to_all | solution.py:620
  45.4 0.0 copy-start.3
  45.4 2.2 %copy-done.3 = bf16[4,512,1024]{2,1,0:T(8,128)(2,1)S(1)} copy-done((bf16[4,512,1024]{2,1,0:T(8,128)(2,1)S(1)}, bf16[4,512,1024]{2,1,0:T(8,128)(2,1)}, u32[]{:S(2)}) %copy-start.3) | copy-done | bytes 4194328
  47.5 6.6 %shard_map.107.field_ref = f32[64,2048]{1,0:T(8,128)S(1)} custom-call(s32[1]{0:T(128)} %bitcast.rank_ref, f32[32]{0:T(128)} %coef_ref.11, f32[64,2048]{1,0:T(8,128)S(1)} %get-tuple-element.40.field_ref, f32[64,2048]{1,0:T(8,128)S(1)} %get-tuple-element.41.rhs_ref, f32[1,2048]{1,0:T(1,128)S(1)} %get-tuple-element.33.mass_ref, ...), custom_call_target="tpu_custom_call" | custom-call | flops 5000000000 | bytes 1048576 | tf_op jit(solution)/shard_map/pallas_call | solution.py:588
  54.1 0.0 collective-permute-done.2.more_refs_1_
  54.2 0.0 collective-permute-done.3.more_refs_2_
  54.2 0.1 collective-permute-start.4
  54.3 6.1 %collective-permute-start.5 = (bf16[64,128]{1,0:T(8,128)(2,1)S(1)}, bf16[64,128]{1,0:T(8,128)(2,1)S(1)}, u32[]{:S(2)}, u32[]{:S(2)}) collective-permute-start(bf16[64,128]{1,0:T(8,128)(2,1)S(1)} %get-tuple-element.58), channel_id=1, source_target_pairs={{1,2},{2,1},{3,4},{4,3},{5,6},{6,5},{7,8},{8,7},{9,10},{10,9},{11,... | collective-permute-start | bytes 49160 | tf_op jit(solution)/shard_map/ppermute | solution.py:563
  60.4 6.6 %shard_map.108.field_ref = f32[64,2048]{1,0:T(8,128)S(1)} custom-call(s32[1]{0:T(128)} %bitcast.rank_ref, f32[32]{0:T(128)} %coef_ref.11, f32[64,2048]{1,0:T(8,128)S(1)} %shard_map.107.field_ref, f32[64,2048]{1,0:T(8,128)S(1)} %get-tuple-element.41.rhs_ref, f32[1,2048]{1,0:T(1,128)S(1)} %get-tuple-element.33.mass_ref, ...), custom_call_target="tpu_custom_call" | custom-call | flops 5000000000 | bytes 1048576 | tf_op jit(solution)/shard_map/pallas_call | solution.py:588
  67.0 0.0 collective-permute-done.4.first_ref
  67.0 0.0 collective-permute-done.5.second_ref
  67.0 0.0 all-to-all-done.1.parts_ref
  67.0 1.3 %shard_map.110 = (f32[64,2048]{1,0:T(8,128)S(1)}, bf16[32,56,128]{2,1,0:T(8,128)(2,1)}, bf16[64,128]{1,0:T(8,128)(2,1)S(1)}, bf16[64,128]{1,0:T(8,128)(2,1)S(1)}) custom-call(s32[1]{0:T(128)} %bitcast.rank_ref, s32[3,192]{1,0:T(4,128)S(1)} %get-tuple-element.30.own_map_ref, s32[8,512]{1,0:T(8,128)S(1)} %get-tuple-element.31.nodes_ref, ...), custom_call_target="tpu_custom_call" | custom-call | flops 1000000000 | bytes 1048576 | tf_op jit(solution)/shard_map/pallas_call | solution.py:670
  68.3 2.3 %all-to-all-start.2 = ((bf16[32,56,128]{2,1,0:T(8,128)(2,1)}), bf16[32,56,128]{2,1,0:T(8,128)(2,1)S(1)}, u32[]{:S(2)}, u32[]{:S(2)}) async-start(bf16[32,56,128]{2,1,0:T(8,128)(2,1)} %get-tuple-element.47), calls=%async_computation.2 | async-start | bytes 917504 | tf_op jit(solution)/shard_map/all_to_all | solution.py:574
  70.7 0.1 collective-permute-start.6
  70.8 6.2 %collective-permute-start.7 = (bf16[64,128]{1,0:T(8,128)(2,1)S(1)}, bf16[64,128]{1,0:T(8,128)(2,1)S(1)}, u32[]{:S(2)}, u32[]{:S(2)}) collective-permute-start(bf16[64,128]{1,0:T(8,128)(2,1)S(1)} %get-tuple-element.50), channel_id=1, source_target_pairs={{1,2},{2,1},{3,4},{4,3},{5,6},{6,5},{7,8},{8,7},{9,10},{10,9},{11,... | collective-permute-start | bytes 49160 | tf_op jit(solution)/shard_map/ppermute | solution.py:563
  77.0 0.0 copy-start.4
  77.0 2.2 %copy-done.4 = bf16[4,512,1024]{2,1,0:T(8,128)(2,1)S(1)} copy-done((bf16[4,512,1024]{2,1,0:T(8,128)(2,1)S(1)}, bf16[4,512,1024]{2,1,0:T(8,128)(2,1)}, u32[]{:S(2)}) %copy-start.4) | copy-done | bytes 4194328
  79.2 6.6 %shard_map.111.field_ref = f32[64,2048]{1,0:T(8,128)S(1)} custom-call(s32[1]{0:T(128)} %bitcast.rank_ref, f32[32]{0:T(128)} %coef_ref.11, f32[64,2048]{1,0:T(8,128)S(1)} %get-tuple-element.48.field_ref, f32[64,2048]{1,0:T(8,128)S(1)} %get-tuple-element.36.forcing_ref.rhs_ref, f32[1,2048]{1,0:T(1,128)S(1)} %get-tuple-element.33.mass_ref, ...), custom_call_target="tpu_custom_call" | custom-call | flops 5000000000 | bytes 1048576 | tf_op jit(solution)/shard_map/pallas_call | solution.py:588
  85.8 0.0 all-to-all-done.2.chunk_ref
  85.8 0.0 copy-start.1
  85.8 2.3 %copy-done.1 = bf16[8,2,192,768]{3,2,1,0:T(8,128)(2,1)S(1)} copy-done((bf16[8,2,192,768]{3,2,1,0:T(8,128)(2,1)S(1)}, bf16[8,2,192,768]{3,2,1,0:T(8,128)(2,1)}, u32[]{:S(2)}) %copy-start.1) | copy-done | bytes 4718616
  88.1 2.5 %shard_map.115 = f32[4,64,192]{2,1,0:T(8,128)} custom-call(s32[3,1536]{1,0:T(4,128)S(1)} %get-tuple-element.45.map_ref, bf16[32,56,128]{2,1,0:T(8,128)(2,1)S(1)} %all-to-all-done.2.chunk_ref, bf16[8,2,192,768]{3,2,1,0:T(8,128)(2,1)S(1)} %copy-done.1), custom_call_target="tpu_custom_call" | custom-call | flops 2000000000 | bytes 1048576 | tf_op jit(solution)/shard_map/pallas_call | solution.py:681
  90.6 3.4 %all-to-all-start.3 = ((f32[4,64,192]{2,1,0:T(8,128)}), f32[4,64,192]{2,1,0:T(8,128)S(1)}, u32[]{:S(2)}, u32[]{:S(2)}) async-start(f32[4,64,192]{2,1,0:T(8,128)} %shard_map.115), calls=%async_computation.3 | async-start | bytes 524288 | tf_op jit(solution)/shard_map/all_to_all | solution.py:620
  94.0 0.0 collective-permute-done.6.first_ref
  94.1 0.0 collective-permute-done.7.second_ref
  94.1 0.4 shard_map.112
  94.5 0.1 collective-permute-start.8
  94.6 3.3 %collective-permute-start.9 = (bf16[64,128]{1,0:T(8,128)(2,1)S(1)}, bf16[64,128]{1,0:T(8,128)(2,1)S(1)}, u32[]{:S(2)}, u32[]{:S(2)}) collective-permute-start(bf16[64,128]{1,0:T(8,128)(2,1)S(1)} %get-tuple-element.54), channel_id=1, source_target_pairs={{1,2},{2,1},{3,4},{4,3},{5,6},{6,5},{7,8},{8,7},{9,10},{10,9},{11,... | collective-permute-start | bytes 49160 | tf_op jit(solution)/shard_map/ppermute | solution.py:563
  97.9 0.0 copy-start.5
  97.9 2.2 %copy-done.5 = bf16[4,512,1024]{2,1,0:T(8,128)(2,1)S(1)} copy-done((bf16[4,512,1024]{2,1,0:T(8,128)(2,1)S(1)}, bf16[4,512,1024]{2,1,0:T(8,128)(2,1)}, u32[]{:S(2)}) %copy-start.5) | copy-done | bytes 4194328
  100.1 6.6 %shard_map.113.field_ref = f32[64,2048]{1,0:T(8,128)S(1)} custom-call(s32[1]{0:T(128)} %bitcast.rank_ref, f32[32]{0:T(128)} %coef_ref.11, f32[64,2048]{1,0:T(8,128)S(1)} %get-tuple-element.51.field_ref, f32[64,2048]{1,0:T(8,128)S(1)} %get-tuple-element.52.rhs_ref, f32[1,2048]{1,0:T(1,128)S(1)} %get-tuple-element.33.mass_ref, ...), custom_call_target="tpu_custom_call" | custom-call | flops 5000000000 | bytes 1048576 | tf_op jit(solution)/shard_map/pallas_call | solution.py:588
  106.7 0.0 collective-permute-done.8.more_refs_1_
  106.7 0.0 collective-permute-done.9.more_refs_2_
  106.7 0.1 collective-permute-start.10
  106.8 6.1 %collective-permute-start.11 = (bf16[64,128]{1,0:T(8,128)(2,1)S(1)}, bf16[64,128]{1,0:T(8,128)(2,1)S(1)}, u32[]{:S(2)}, u32[]{:S(2)}) collective-permute-start(bf16[64,128]{1,0:T(8,128)(2,1)S(1)} %get-tuple-element.56), channel_id=1, source_target_pairs={{1,2},{2,1},{3,4},{4,3},{5,6},{6,5},{7,8},{8,7},{9,10},{10,9},{11,... | collective-permute-start | bytes 49160 | tf_op jit(solution)/shard_map/ppermute | solution.py:563
  112.9 6.6 %shard_map.114.field_ref = f32[64,2048]{1,0:T(8,128)S(1)} custom-call(s32[1]{0:T(128)} %bitcast.rank_ref, f32[32]{0:T(128)} %coef_ref.11, f32[64,2048]{1,0:T(8,128)S(1)} %shard_map.113.field_ref, f32[64,2048]{1,0:T(8,128)S(1)} %get-tuple-element.52.rhs_ref, f32[1,2048]{1,0:T(1,128)S(1)} %get-tuple-element.33.mass_ref, ...), custom_call_target="tpu_custom_call" | custom-call | flops 5000000000 | bytes 1048576 | tf_op jit(solution)/shard_map/pallas_call | solution.py:588
  119.5 0.0 collective-permute-done.10.first_ref
  119.5 0.0 collective-permute-done.11.second_ref
  119.5 0.0 all-to-all-done.3.parts_ref
  119.6 0.9 shard_map.116
  (2 shorter events, 0.0 us)
Async XLA Ops:
  3.9 22.8 %all-to-all-start = ((bf16[32,64,128]{2,1,0:T(8,128)(2,1)}), bf16[32,64,128]{2,1,0:T(8,128)(2,1)S(1)}, u32[]{:S(2)}, u32[]{:S(2)}) async-start(bf16[32,64,128]{2,1,0:T(8,128)(2,1)} %get-tuple-element.32), calls=%async_computation | async-start | bytes 1048576 | tf_op jit(solution)/shard_map/all_to_all | solution.py:574
  10.0 16.7 %collective-permute-start = (bf16[64,128]{1,0:T(8,128)(2,1)S(1)}, bf16[64,128]{1,0:T(8,128)(2,1)S(1)}, u32[]{:S(2)}, u32[]{:S(2)}) collective-permute-start(bf16[64,128]{1,0:T(8,128)(2,1)S(1)} %get-tuple-element.38), channel_id=1, source_target_pairs={{0,1},{1,0},{2,3},{3,2},{4,5},{5,4},{6,7},{7,6},{8,9},{9,8},{10,11... | collective-permute-start | bytes 49160 | tf_op jit(solution)/shard_map/ppermute | solution.py:563
  10.2 16.5 %collective-permute-start.1 = (bf16[64,128]{1,0:T(8,128)(2,1)S(1)}, bf16[64,128]{1,0:T(8,128)(2,1)S(1)}, u32[]{:S(2)}, u32[]{:S(2)}) collective-permute-start(bf16[64,128]{1,0:T(8,128)(2,1)S(1)} %get-tuple-element.39), channel_id=1, source_target_pairs={{1,2},{2,1},{3,4},{4,3},{5,6},{6,5},{7,8},{8,7},{9,10},{10,9},{11,... | collective-permute-start | bytes 49160 | tf_op jit(solution)/shard_map/ppermute | solution.py:563
  24.0 2.0 %copy-start.2 = (bf16[4,512,1024]{2,1,0:T(8,128)(2,1)}, bf16[4,512,1024]{2,1,0:T(8,128)(2,1)S(1)}, u32[]{:S(2)}) copy-start(bf16[4,512,1024]{2,1,0:T(8,128)(2,1)S(1)} %get-tuple-element.42.more_refs_0_) | copy-start | bytes 12582916
  27.2 27.0 %collective-permute-start.2 = (bf16[64,128]{1,0:T(8,128)(2,1)S(1)}, bf16[64,128]{1,0:T(8,128)(2,1)S(1)}, u32[]{:S(2)}, u32[]{:S(2)}) collective-permute-start(bf16[64,128]{1,0:T(8,128)(2,1)S(1)} %get-tuple-element.43), channel_id=1, source_target_pairs={{0,1},{1,0},{2,3},{3,2},{4,5},{5,4},{6,7},{7,6},{8,9},{9,8},{10,11... | collective-permute-start | bytes 49160 | tf_op jit(solution)/shard_map/ppermute | solution.py:563
  27.3 26.9 %collective-permute-start.3 = (bf16[64,128]{1,0:T(8,128)(2,1)S(1)}, bf16[64,128]{1,0:T(8,128)(2,1)S(1)}, u32[]{:S(2)}, u32[]{:S(2)}) collective-permute-start(bf16[64,128]{1,0:T(8,128)(2,1)S(1)} %get-tuple-element.44), channel_id=1, source_target_pairs={{1,2},{2,1},{3,4},{4,3},{5,6},{6,5},{7,8},{8,7},{9,10},{10,9},{11,... | collective-permute-start | bytes 49160 | tf_op jit(solution)/shard_map/ppermute | solution.py:563
  39.6 2.1 %copy-start = (bf16[8,2,192,768]{3,2,1,0:T(8,128)(2,1)}, bf16[8,2,192,768]{3,2,1,0:T(8,128)(2,1)S(1)}, u32[]{:S(2)}) copy-start(bf16[8,2,192,768]{3,2,1,0:T(8,128)(2,1)S(1)} %get-tuple-element.55.tile_ref) | copy-start | bytes 14155780
  41.8 25.2 %all-to-all-start.1 = ((f32[4,64,192]{2,1,0:T(8,128)}), f32[4,64,192]{2,1,0:T(8,128)S(1)}, u32[]{:S(2)}, u32[]{:S(2)}) async-start(f32[4,64,192]{2,1,0:T(8,128)} %get-tuple-element.46), calls=%async_computation.1 | async-start | bytes 524288 | tf_op jit(solution)/shard_map/all_to_all | solution.py:620
  45.4 2.2 %copy-start.3 = (bf16[4,512,1024]{2,1,0:T(8,128)(2,1)S(1)}, bf16[4,512,1024]{2,1,0:T(8,128)(2,1)}, u32[]{:S(2)}) copy-start(bf16[4,512,1024]{2,1,0:T(8,128)(2,1)} %copy-done.2) | copy-start | bytes 12582916
  54.2 12.8 %collective-permute-start.4 = (bf16[64,128]{1,0:T(8,128)(2,1)S(1)}, bf16[64,128]{1,0:T(8,128)(2,1)S(1)}, u32[]{:S(2)}, u32[]{:S(2)}) collective-permute-start(bf16[64,128]{1,0:T(8,128)(2,1)S(1)} %get-tuple-element.59), channel_id=1, source_target_pairs={{0,1},{1,0},{2,3},{3,2},{4,5},{5,4},{6,7},{7,6},{8,9},{9,8},{10,11... | collective-permute-start | bytes 49160 | tf_op jit(solution)/shard_map/ppermute | solution.py:563
  54.3 12.7 %collective-permute-start.5 = (bf16[64,128]{1,0:T(8,128)(2,1)S(1)}, bf16[64,128]{1,0:T(8,128)(2,1)S(1)}, u32[]{:S(2)}, u32[]{:S(2)}) collective-permute-start(bf16[64,128]{1,0:T(8,128)(2,1)S(1)} %get-tuple-element.58), channel_id=1, source_target_pairs={{1,2},{2,1},{3,4},{4,3},{5,6},{6,5},{7,8},{8,7},{9,10},{10,9},{11,... | collective-permute-start | bytes 49160 | tf_op jit(solution)/shard_map/ppermute | solution.py:563
  68.3 17.5 %all-to-all-start.2 = ((bf16[32,56,128]{2,1,0:T(8,128)(2,1)}), bf16[32,56,128]{2,1,0:T(8,128)(2,1)S(1)}, u32[]{:S(2)}, u32[]{:S(2)}) async-start(bf16[32,56,128]{2,1,0:T(8,128)(2,1)} %get-tuple-element.47), calls=%async_computation.2 | async-start | bytes 917504 | tf_op jit(solution)/shard_map/all_to_all | solution.py:574
  70.7 23.4 %collective-permute-start.6 = (bf16[64,128]{1,0:T(8,128)(2,1)S(1)}, bf16[64,128]{1,0:T(8,128)(2,1)S(1)}, u32[]{:S(2)}, u32[]{:S(2)}) collective-permute-start(bf16[64,128]{1,0:T(8,128)(2,1)S(1)} %get-tuple-element.49), channel_id=1, source_target_pairs={{0,1},{1,0},{2,3},{3,2},{4,5},{5,4},{6,7},{7,6},{8,9},{9,8},{10,11... | collective-permute-start | bytes 49160 | tf_op jit(solution)/shard_map/ppermute | solution.py:563
  70.8 23.3 %collective-permute-start.7 = (bf16[64,128]{1,0:T(8,128)(2,1)S(1)}, bf16[64,128]{1,0:T(8,128)(2,1)S(1)}, u32[]{:S(2)}, u32[]{:S(2)}) collective-permute-start(bf16[64,128]{1,0:T(8,128)(2,1)S(1)} %get-tuple-element.50), channel_id=1, source_target_pairs={{1,2},{2,1},{3,4},{4,3},{5,6},{6,5},{7,8},{8,7},{9,10},{10,9},{11,... | collective-permute-start | bytes 49160 | tf_op jit(solution)/shard_map/ppermute | solution.py:563
  77.0 2.2 %copy-start.4 = (bf16[4,512,1024]{2,1,0:T(8,128)(2,1)S(1)}, bf16[4,512,1024]{2,1,0:T(8,128)(2,1)}, u32[]{:S(2)}) copy-start(bf16[4,512,1024]{2,1,0:T(8,128)(2,1)} %copy-done.2) | copy-start | bytes 12582916
  85.8 2.3 %copy-start.1 = (bf16[8,2,192,768]{3,2,1,0:T(8,128)(2,1)S(1)}, bf16[8,2,192,768]{3,2,1,0:T(8,128)(2,1)}, u32[]{:S(2)}) copy-start(bf16[8,2,192,768]{3,2,1,0:T(8,128)(2,1)} %copy-done) | copy-start | bytes 14155780
  90.6 28.9 %all-to-all-start.3 = ((f32[4,64,192]{2,1,0:T(8,128)}), f32[4,64,192]{2,1,0:T(8,128)S(1)}, u32[]{:S(2)}, u32[]{:S(2)}) async-start(f32[4,64,192]{2,1,0:T(8,128)} %shard_map.115), calls=%async_computation.3 | async-start | bytes 524288 | tf_op jit(solution)/shard_map/all_to_all | solution.py:620
  94.5 12.2 %collective-permute-start.8 = (bf16[64,128]{1,0:T(8,128)(2,1)S(1)}, bf16[64,128]{1,0:T(8,128)(2,1)S(1)}, u32[]{:S(2)}, u32[]{:S(2)}) collective-permute-start(bf16[64,128]{1,0:T(8,128)(2,1)S(1)} %get-tuple-element.53), channel_id=1, source_target_pairs={{0,1},{1,0},{2,3},{3,2},{4,5},{5,4},{6,7},{7,6},{8,9},{9,8},{10,11... | collective-permute-start | bytes 49160 | tf_op jit(solution)/shard_map/ppermute | solution.py:563
  94.6 12.1 %collective-permute-start.9 = (bf16[64,128]{1,0:T(8,128)(2,1)S(1)}, bf16[64,128]{1,0:T(8,128)(2,1)S(1)}, u32[]{:S(2)}, u32[]{:S(2)}) collective-permute-start(bf16[64,128]{1,0:T(8,128)(2,1)S(1)} %get-tuple-element.54), channel_id=1, source_target_pairs={{1,2},{2,1},{3,4},{4,3},{5,6},{6,5},{7,8},{8,7},{9,10},{10,9},{11,... | collective-permute-start | bytes 49160 | tf_op jit(solution)/shard_map/ppermute | solution.py:563
  97.9 2.2 %copy-start.5 = (bf16[4,512,1024]{2,1,0:T(8,128)(2,1)S(1)}, bf16[4,512,1024]{2,1,0:T(8,128)(2,1)}, u32[]{:S(2)}) copy-start(bf16[4,512,1024]{2,1,0:T(8,128)(2,1)} %copy-done.2) | copy-start | bytes 12582916
  106.7 12.8 %collective-permute-start.10 = (bf16[64,128]{1,0:T(8,128)(2,1)S(1)}, bf16[64,128]{1,0:T(8,128)(2,1)S(1)}, u32[]{:S(2)}, u32[]{:S(2)}) collective-permute-start(bf16[64,128]{1,0:T(8,128)(2,1)S(1)} %get-tuple-element.57), channel_id=1, source_target_pairs={{0,1},{1,0},{2,3},{3,2},{4,5},{5,4},{6,7},{7,6},{8,9},{9,8},{10,11... | collective-permute-start | bytes 49160 | tf_op jit(solution)/shard_map/ppermute | solution.py:563
  106.8 12.8 %collective-permute-start.11 = (bf16[64,128]{1,0:T(8,128)(2,1)S(1)}, bf16[64,128]{1,0:T(8,128)(2,1)S(1)}, u32[]{:S(2)}, u32[]{:S(2)}) collective-permute-start(bf16[64,128]{1,0:T(8,128)(2,1)S(1)} %get-tuple-element.56), channel_id=1, source_target_pairs={{1,2},{2,1},{3,4},{4,3},{5,6},{6,5},{7,8},{8,7},{9,10},{10,9},{11,... | collective-permute-start | bytes 49160 | tf_op jit(solution)/shard_map/ppermute | solution.py:563

commit v3 on v2

--- a/solution.py
+++ b/solution.py
@@ -14,7 +14,7 @@
 LOAD_ROWS = 8
 POINT_ROWS = 8
 HALVES = 2
-GROUP = 8
+GROUP = 4
 BLOCKS = 4
 
 wave_number = 20.0
@@ -27,6 +27,7 @@
 SIN_POLY = (3.14159264, -5.16771008, 2.55007752, -0.59829129, 0.07765766)
 COS_POLY = (0.99999995, -4.93479283, 4.05841135, -1.33187657, 0.21968961)
 
+ROUNDER = 1.5 * 2.0**23
 MIB = 1024 * 1024
 
 
@@ -255,19 +256,19 @@
 
 
 def sweep_kernel(
-    parts, weight, weight_before, build, rank_ref, coef_ref, field_ref, rhs_ref, mass_ref, keys_ref,
+    parts, weight, weight_before, keep, rank_ref, coef_ref, field_ref, rhs_ref, mass_ref, keys_ref,
     matrix_ref, *more_refs,
 ):
-    if build:
-        out_ref, hot_ref, total_ref, sem, *scratch = more_refs
-        copy = pltpu.make_async_copy(rhs_ref, total_ref, sem)
+    if keep:
+        out_ref, kept_ref, sem, *scratch = more_refs
+        copy = pltpu.make_async_copy(rhs_ref, kept_ref, sem)
         copy.start()
-        rhs_ref = total_ref
+        rhs_ref = kept_ref
     elif weight_before is None:
-        hot_ref, out_ref, *scratch = more_refs
+        out_ref, *scratch = more_refs
     else:
-        hot_ref, first_ref, second_ref, out_ref, field_scr, *scratch = more_refs
-    high_ref, low_ref, found_ref, local_ref, yhigh_ref, ylow_ref, sum_ref = scratch
+        first_ref, second_ref, out_ref, field_scr, *scratch = more_refs
+    hot_ref, high_ref, low_ref, found_ref, local_ref, product_ref, yhigh_ref, ylow_ref, sum_ref = scratch
     groups = hot_ref.shape[0]
     columns, count = field_ref.shape
     width = count // parts
@@ -293,15 +294,16 @@
         axis=0,
     )
 
+    def build(group):
+        for e in range(GROUP):
+            key = keys_ref[group * GROUP + e : group * GROUP + e + 1, :]
+            hot_ref[group, :, e * LANES : (e + 1) * LANES] = one_hot_rows(low_part(key, width), width)
+
     def gather(group):
-        if build:
-            for e in range(GROUP):
-                key = keys_ref[group * GROUP + e : group * GROUP + e + 1, :]
-                hot_ref[group, :, e * LANES : (e + 1) * LANES] = one_hot_rows(low_part(key, width), width)
         hot = hot_ref[group]
         found_ref[group % 2] = dot(high_ref[...], hot) + dot(low_ref[...], hot)
 
-    def multiply(group):
+    def pick(group):
         slot = group % 2
         for e in range(GROUP):
             element = group * GROUP + e
@@ -311,11 +313,16 @@
             local_ref[slot, e * columns : (e + 1) * columns, :LANES] = got_high
             local_ref[slot, e * columns : (e + 1) * columns, LANES:] = got_low
 
-        product = dot(local_ref[slot], matrix)
+
+    def multiply(group):
+        product_ref[group % 2] = dot(local_ref[group % 2], matrix)
+
+    def scale(group):
+        slot = group % 2
         for e in range(GROUP):
             element = group * GROUP + e
             part = high_part(keys_ref[element : element + 1, :], width)
-            rows = product[e * columns : (e + 1) * columns]
+            rows = product_ref[slot, e * columns : (e + 1) * columns]
             value = (rows[:, :LANES] + rows[:, LANES:]) * coef_ref[element]
             value_high, value_low = split_two(value)
             span = slice(e * LANES, (e + 1) * LANES)
@@ -329,13 +336,21 @@
         added = dot_nt(yhigh_ref[group % 2], hot) + dot_nt(ylow_ref[group % 2], hot)
         sum_ref[...] = added if group == 0 else sum_ref[...] + added
 
+    build(0)
     gather(0)
+    build(1)
     for group in range(groups):
+        pick(group)
         if group + 1 < groups:
             gather(group + 1)
+        if group + 2 < groups:
+            build(group + 2)
         multiply(group)
-        scatter(group)
-    if build:
+        if group:
+            scatter(group - 1)
+        scale(group)
+    scatter(groups - 1)
+    if keep:
         copy.wait()
     for h in range(parts):
         span = slice(h * width, (h + 1) * width)
@@ -435,7 +450,7 @@
 
 def tile_kernel(
     brow, bcol, panel_dev, slot_rows, rank_ref, map_ref, chunk_ref, out_ref, tile_ref,
-    target_ref, density_ref, turned_ref, distance_ref, sum_ref,
+    target_ref, density_ref, turned_ref, distance_ref, built_ref, sum_ref, sems,
 ):
     count_all = brow * bcol * panel_dev
     soften = 0.5 * float(count_all) ** (-1.0 / 3.0)
@@ -446,6 +461,9 @@
 
     def points_of(device):
         return chunk_ref[device].astype(F32)[start : start + POINT_ROWS]
+
+    def copy_of(index):
+        return pltpu.make_async_copy(built_ref.at[index], tile_ref.at[index], sems.at[index])
 
     @pl.when(block == 0)
     def prepare():
@@ -481,7 +499,7 @@
         squared = distance_ref[top : top + step]
         inverse = lax.rsqrt(squared)
         turns = (squared * inverse) * (wave_number / (2.0 * math.pi))
-        turns = turns - jnp.floor(turns + 0.5)
+        turns = turns - ((turns + ROUNDER) - ROUNDER)
         z = turns * turns
         sine = jnp.full_like(z, SIN_POLY[-1])
         for factor in SIN_POLY[-2::-1]:
@@ -491,29 +509,39 @@
         for factor in COS_POLY[-2::-1]:
             cosine = cosine * z + factor
         double = sine * (inverse * (2.0 / math.sqrt(float(count_all))))
-        tile_ref[block, 0, top : top + step] = (
+        built_ref[block, 0, top : top + step] = (
             inverse * (1.0 / math.sqrt(float(count_all))) - sine * double
         ).astype(BF16)
-        tile_ref[block, 1, top : top + step] = (cosine * double).astype(BF16)
-    sum_ref[...] += dot(density_ref[block], tile_ref[block, 0]) + dot(
-        turned_ref[block], tile_ref[block, 1]
+        built_ref[block, 1, top : top + step] = (cosine * double).astype(BF16)
+    copy_of(block).start()
+    sum_ref[...] += dot(density_ref[block], built_ref[block, 0]) + dot(
+        turned_ref[block], built_ref[block, 1]
     )
 
     @pl.when(block == bcol - 1)
     def end():
         write_parts(out_ref, sum_ref[...], panel_dev)
+        for index in range(bcol):
+            copy_of(index).wait()
 
 
 def potential_kernel(
-    brow, bcol, panel_dev, slot_rows, map_ref, chunk_ref, tile_ref, out_ref,
+    brow, bcol, panel_dev, slot_rows, map_ref, chunk_ref, tile_ref, out_ref, held_ref, sems,
 ):
+    copies = [
+        pltpu.make_async_copy(tile_ref.at[block], held_ref.at[block], sems.at[block])
+        for block in range(bcol)
+    ]
+    for copy in copies:
+        copy.start()
     whole = None
     groups = density_groups(map_ref, chunk_ref, brow, bcol, panel_dev, slot_rows)
     for group, (density, turned) in enumerate(groups):
         for k in range(BLOCKS):
             block = group * BLOCKS + k
+            copies[block].wait()
             span = slice(k * panel_dev, (k + 1) * panel_dev)
-            part = dot(density[:, span], tile_ref[block, 0]) + dot(turned[:, span], tile_ref[block, 1])
+            part = dot(density[:, span], held_ref[block, 0]) + dot(turned[:, span], held_ref[block, 1])
             whole = part if whole is None else whole + part
     write_parts(out_ref, whole, panel_dev)
 
@@ -566,8 +594,8 @@
         first, second = (piece.astype(F32) for piece in halo)
         left, right = jnp.where(even, second, first), jnp.where(even, first, second)
         last = count - RIM
-        low = field[:, :RIM] + (weight * penalty) * left / node_mass[:RIM]
-        high = field[:, last:] + (weight * penalty) * right / node_mass[last:]
+        low = field[:, :RIM] + (weight * penalty) * left / mass[:, :RIM]
+        high = field[:, last:] + (weight * penalty) * right / mass[:, last:]
         return jnp.where(even, high, low).astype(BF16), jnp.where(even, low, high).astype(BF16)
 
     def swap_all(chunks):
@@ -577,27 +605,26 @@
     hot_shape = (elements // GROUP, width, GROUP * LANES)
     tile_shape = (bcol, HALVES, panel_dev, brow * panel_dev)
 
-    def sweep(field, rhs, weight, halo=(), weight_before=None, hot=None):
+    def sweep(field, rhs, weight, halo=(), weight_before=None, keep=False):
         rows = parts * columns
         lanes = GROUP * LANES
-        build = hot is None
-        if build:
-            given = (rank, *in_hbm(element_coef, field, rhs), *in_vmem(mass, keys, matrix))
-        else:
-            given = (rank, *in_hbm(element_coef), field, rhs, *in_vmem(mass, keys, matrix, hot), *halo)
+        large = in_hbm(field, rhs) if keep else (field, rhs)
+        given = (rank, *in_hbm(element_coef), *large, *in_vmem(mass, keys, matrix), *halo)
         return call(
-            functools.partial(sweep_kernel, parts, weight, weight_before, build),
-            (field_shape, kept(hot_shape, BF16), kept((columns, count), F32)) if build else field_shape,
+            functools.partial(sweep_kernel, parts, weight, weight_before, keep),
+            (field_shape, kept((columns, count), F32)) if keep else field_shape,
             5_000_000_000,
-            in_specs=[smem, smem, vmem, hbm if build else vmem] + [vmem] * (len(given) - 4),
-            out_specs=(vmem,) * 3 if build else vmem,
-            scratch_shapes=[pltpu.SemaphoreType.DMA] * build
+            in_specs=[smem, smem, vmem, hbm if keep else vmem] + [vmem] * (len(given) - 4),
+            out_specs=(vmem, vmem) if keep else vmem,
+            scratch_shapes=[pltpu.SemaphoreType.DMA] * keep
             + [pltpu.VMEM((columns, count), F32)] * bool(halo)
             + [
+                pltpu.VMEM(hot_shape, BF16),
                 pltpu.VMEM((rows, width), BF16),
                 pltpu.VMEM((rows, width), BF16),
                 pltpu.VMEM((2, rows, lanes), F32),
                 pltpu.VMEM((2, GROUP * columns, 2 * LANES), BF16),
+                pltpu.VMEM((2, GROUP * columns, 2 * LANES), F32),
                 pltpu.VMEM((2, rows, lanes), BF16),
                 pltpu.VMEM((2, rows, lanes), BF16),
                 pltpu.VMEM((rows, width), F32),
@@ -615,6 +642,7 @@
 
     parts_shape = shape_of((brow, columns, panel_dev), F32)
     sizes = (brow, bcol, panel_dev, slot_rows)
+    tile_mib = -(-(2 * math.prod(tile_shape)) // MIB)
 
     def swap_parts(parts_out):
         return lax.all_to_all(parts_out, "brow", split_axis=0, concat_axis=0, tiled=True)
@@ -645,28 +673,31 @@
     )
     halo = exchange(*rim)
     chunks = swap_all(chunks)
-    field, hot, forcing_kept = sweep(field_start, forcing, weights[0])
+    field, forcing_kept = sweep(field_start, forcing, weights[0], keep=True)
     parts_out, tiles = call(
         functools.partial(tile_kernel, *sizes),
-        (parts_shape, kept(tile_shape, BF16)),
+        (parts_shape, pltpu.HBM(tile_shape, BF16)),
         8_000_000_000,
         grid=(bcol,),
+        limit=16 + tile_mib,
         in_specs=[smem, vmem, vmem],
-        out_specs=(vmem, vmem),
+        out_specs=(vmem, hbm),
         scratch_shapes=[
             pltpu.VMEM((16, brow * panel_dev), BF16),
             pltpu.VMEM((bcol, columns, panel_dev), BF16),
             pltpu.VMEM((bcol, columns, panel_dev), BF16),
             pltpu.VMEM((panel_dev, brow * panel_dev), F32),
+            pltpu.VMEM(tile_shape, BF16),
             pltpu.VMEM((columns, brow * panel_dev), F32),
+            pltpu.SemaphoreType.DMA((bcol,)),
         ],
     )(rank, *in_vmem(row_map), chunks)
     parts_in = swap_parts(parts_out)
     rhs, field, *rim = add_loads(chunks, field, halo, weights[0])
     halo = exchange(*rim)
-    field = sweep(field, rhs, weights[1], hot=hot)
+    field = sweep(field, rhs, weights[1])
     halo_next = exchange(*rims(field, halo, weights[1]))
-    field = sweep(field, rhs, weights[2], halo, weights[1], hot)
+    field = sweep(field, rhs, weights[2], halo, weights[1])
     field, chunks, *rim = call(
         functools.partial(finish_kernel, parts, brow, bcol, panel_dev, slot_rows, weights[2]),
         (field_shape, chunk_shape(used + LOAD_ROWS, 8), rim_shape, rim_shape),
@@ -677,20 +708,22 @@
 
     halo = exchange(*rim)
     chunks = swap_all(chunks)
-    field = sweep(field, *in_vmem(forcing_kept), weights[0], hot=hot)
+    field = sweep(field, *in_vmem(forcing_kept), weights[0])
     parts_out = call(
         functools.partial(potential_kernel, *sizes),
         parts_shape,
         2_000_000_000,
-        in_specs=[vmem] * 3,
+        limit=16 + tile_mib,
+        in_specs=[vmem, vmem, hbm],
         out_specs=vmem,
-    )(*in_vmem(row_map), chunks, *in_vmem(tiles))
+        scratch_shapes=[pltpu.VMEM(tile_shape, BF16), pltpu.SemaphoreType.DMA((bcol,))],
+    )(*in_vmem(row_map), chunks, *in_hbm(tiles))
     parts_in = swap_parts(parts_out)
     rhs, field, *rim = add_loads(chunks, field, halo, weights[0])
     halo = exchange(*rim)
-    field = sweep(field, rhs, weights[1], hot=hot)
+    field = sweep(field, rhs, weights[1])
     halo_next = exchange(*rims(field, halo, weights[1]))
-    field = sweep(field, rhs, weights[2], halo, weights[1], hot)
+    field = sweep(field, rhs, weights[2], halo, weights[1])
     return call(
         functools.partial(last_kernel, weights[2]),
         (field_shape, shape_of((columns, panel_dev), F32)),

time: 121 us -> 111 us (0.917)
  local copies, waits for them, and re-layouts: 13.7 us -> 0.01 us
  waiting for transfers between devices: 0.04 us -> 4.41 us
  Pallas kernels: 58.7 us -> 55.1 us
  starting transfers between devices: 46.9 us -> 49.1 us
    unnamed x12 -> x0, local copies, waits for them, and re-layouts: 13 us -> none
    pallas_call x7, Pallas kernels: 50 us -> 44.8 us  [the longest x6 34.9 us: sweep(): call(functools.partial(sweep_kernel, parts, weight, weight_before, keep),...]
    all_to_all x2, waiting for transfers between devices: 0.01 us -> 3.3 us  [swap_all(): return lax.all_to_all(chunks, AXES, split_axis=0, concat_axis=0, tiled=True)]
    pallas_call x1, Pallas kernels: 2.49 us -> 4 us  [per_device(): call(functools.partial(potential_kernel, *sizes), parts_shape, 2000000000...]
    all_to_all x2, starting transfers between devices: 6.97 us -> 8.29 us  [swap_parts(): lax.all_to_all(parts_out, 'brow', split_axis=0, concat_axis=0, tiled=True)]
  transfers between devices with their start and end apart: 16 -> 16, of which waited for: 0 -> 3; matrix products, arithmetic and copies ran while one was open for 1% -> 0% of each run, Pallas kernels for 44% -> 45%
where the time goes in v3:
time: 111 us; the launch traced here: 110 us
  Pallas kernels  55.1 us (50%)
  starting transfers between devices  49.1 us (44%)
  waiting for transfers between devices  4.41 us (4%)
    pallas_call x6, Pallas kernels, sweep(): call(functools.partial(sweep_kernel, parts, weight, weight_before, keep),...  34.9 us
    ppermute x6, starting transfers between devices, exchange(): lax.ppermute(second, AXES, odd_pairs)  31.2 us
    pallas_call x1, Pallas kernels, per_device(): call(functools.partial(tile_kernel, *sizes), (parts_shape, pltpu.HBM(tile...  9.95 us
    all_to_all x2, starting transfers between devices, swap_all(): return lax.all_to_all(chunks, AXES, split_axis=0, concat_axis=0, tiled=True)  8.75 us
    all_to_all x2, starting transfers between devices, swap_parts(): lax.all_to_all(parts_out, 'brow', split_axis=0, concat_axis=0, tiled=True)  8.29 us
    pallas_call x1, Pallas kernels, per_device(): call(functools.partial(potential_kernel, *sizes), parts_shape, 2000000000...  4 us
    all_to_all x2, waiting for transfers between devices, swap_all(): return lax.all_to_all(chunks, AXES, split_axis=0, concat_axis=0, tiled=True)  3.3 us
    pallas_call x1, Pallas kernels, per_device(): call(functools.partial(setup_kernel, parts, brow, bcol, panel_dev, slot_r...  3.29 us
  transfers between devices with their start and end apart: 16, of which 3 were waited for; matrix products, arithmetic and copies ran while one was open for 0% of the time, Pallas kernels for 45%

profile of v3, /device:TPU:4, one launch (start us, length us, event | category | flops | bytes accessed | tf_op | source)
XLA Modules:
  0.0 109.6 jit_solution(7605444655776027174)
XLA Ops:
  0.6 3.3 %shard_map.104 = (s32[8,512]{1,0:T(8,128)S(1)}, s32[8,512]{1,0:T(8,128)S(1)}, s32[3,1536]{1,0:T(4,128)S(1)}, s32[3,192]{1,0:T(4,128)S(1)}, s32[32,128]{1,0:T(8,1...) custom-call(s32[1]{0:T(128)} %bitcast.rank_ref, ...), custom_call_target="tpu_custom_call" | custom-call | flops 2000000000 | bytes 1048576 | tf_op jit(solution)/shard_map/pallas_call | solution.py:650
  3.9 6.1 %all-to-all-start = ((bf16[32,64,128]{2,1,0:T(8,128)(2,1)}), bf16[32,64,128]{2,1,0:T(8,128)(2,1)S(1)}, u32[]{:S(2)}, u32[]{:S(2)}) async-start(bf16[32,64,128]{2,1,0:T(8,128)(2,1)} %get-tuple-element.31), calls=%async_computation | async-start | bytes 1048576 | tf_op jit(solution)/shard_map/all_to_all | solution.py:602
  10.0 0.2 collective-permute-start
  10.2 6.1 %collective-permute-start.1 = (bf16[64,128]{1,0:T(8,128)(2,1)S(1)}, bf16[64,128]{1,0:T(8,128)(2,1)S(1)}, u32[]{:S(2)}, u32[]{:S(2)}) collective-permute-start(bf16[64,128]{1,0:T(8,128)(2,1)S(1)} %get-tuple-element.38), channel_id=1, source_target_pairs={{1,2},{2,1},{3,4},{4,3},{5,6},{6,5},{7,8},{8,7},{9,10},{10,9},{11,... | collective-permute-start | bytes 49160 | tf_op jit(solution)/shard_map/ppermute | solution.py:591
  16.3 6.2 %shard_map.105 = (f32[64,2048]{1,0:T(8,128)S(1)}, f32[64,2048]{1,0:T(8,128)S(1)}) custom-call(s32[1]{0:T(128)} %bitcast.rank_ref, f32[32]{0:T(128)} %coef_ref.11, f32[64,2048]{1,0:T(8,128)} %field_ref.3, f32[64,2048]{1,0:T(8,128)} %rhs_ref.1, f32[1,2048]{1,0:T(1,128)S(1)} %get-tuple-element.32.mass_ref, s32[32,128]{1,0:T(8,128)S(1)} %get-tuple-element.33.keys_ref, ...), custom_call_target="tpu_custom_call" | custom-call | flops 5000000000 | bytes 1048576 | tf_op jit(solution)/shard_map/pallas_call | solution.py:613
  22.6 0.0 collective-permute-done.first_ref
  22.6 1.1 collective-permute-done.1.second_ref
  23.7 1.7 %all-to-all-done.chunk_ref = bf16[32,64,128]{2,1,0:T(8,128)(2,1)S(1)} async-done(((bf16[32,64,128]{2,1,0:T(8,128)(2,1)}), bf16[32,64,128]{2,1,0:T(8,128)(2,1)S(1)}, u32[]{:S(2)}, u32[]{:S(2)}) %all-to-all-start) | async-done | bytes 524320 | tf_op jit(solution)/shard_map/all_to_all | solution.py:602
  25.3 0.4 shard_map.106
  25.7 0.2 collective-permute-start.2
  26.0 3.7 %collective-permute-start.3 = (bf16[64,128]{1,0:T(8,128)(2,1)S(1)}, bf16[64,128]{1,0:T(8,128)(2,1)S(1)}, u32[]{:S(2)}, u32[]{:S(2)}) collective-permute-start(bf16[64,128]{1,0:T(8,128)(2,1)S(1)} %get-tuple-element.42), channel_id=1, source_target_pairs={{1,2},{2,1},{3,4},{4,3},{5,6},{6,5},{7,8},{8,7},{9,10},{10,9},{11,... | collective-permute-start | bytes 49160 | tf_op jit(solution)/shard_map/ppermute | solution.py:591
  29.7 10.0 %shard_map.109 = (f32[4,64,192]{2,1,0:T(8,128)}, bf16[8,2,192,768]{3,2,1,0:T(8,128)(2,1)}) custom-call(s32[1]{0:T(128)} %bitcast.rank_ref, s32[3,1536]{1,0:T(4,128)S(1)} %get-tuple-element.43.map_ref, bf16[32,64,128]{2,1,0:T(8,128)(2,1)S(1)} %all-to-all-done.chunk_ref), custom_call_target="tpu_custom_call" | custom-call | flops 8000000000 | bytes 1048576 | tf_op jit(solution)/shard_map/pallas_call | solution.py:677
  39.7 3.6 %all-to-all-start.1 = ((f32[4,64,192]{2,1,0:T(8,128)}), f32[4,64,192]{2,1,0:T(8,128)S(1)}, u32[]{:S(2)}, u32[]{:S(2)}) async-start(f32[4,64,192]{2,1,0:T(8,128)} %get-tuple-element.44), calls=%async_computation.1 | async-start | bytes 524288 | tf_op jit(solution)/shard_map/all_to_all | solution.py:648
  43.3 5.7 %shard_map.107.field_ref = f32[64,2048]{1,0:T(8,128)S(1)} custom-call(s32[1]{0:T(128)} %bitcast.rank_ref, f32[32]{0:T(128)} %coef_ref.11, f32[64,2048]{1,0:T(8,128)S(1)} %get-tuple-element.39.field_ref, f32[64,2048]{1,0:T(8,128)S(1)} %get-tuple-element.40.rhs_ref, f32[1,2048]{1,0:T(1,128)S(1)} %get-tuple-element.32.mass_ref, ...), custom_call_target="tpu_custom_call" | custom-call | flops 5000000000 | bytes 1048576 | tf_op jit(solution)/shard_map/pallas_call | solution.py:613
  49.0 0.0 collective-permute-done.2.more_refs_0_
  49.0 0.0 collective-permute-done.3.more_refs_1_
  49.0 5.6 %collective-permute-start.5 = (bf16[64,128]{1,0:T(8,128)(2,1)S(1)}, bf16[64,128]{1,0:T(8,128)(2,1)S(1)}, u32[]{:S(2)}, u32[]{:S(2)}) collective-permute-start(bf16[64,128]{1,0:T(8,128)(2,1)S(1)} %get-tuple-element.56), channel_id=1, source_target_pairs={{1,2},{2,1},{3,4},{4,3},{5,6},{6,5},{7,8},{8,7},{9,10},{10,9},{11,... | collective-permute-start | bytes 49160 | tf_op jit(solution)/shard_map/ppermute | solution.py:591
  54.7 0.1 collective-permute-start.4
  54.8 5.8 %shard_map.108.field_ref = f32[64,2048]{1,0:T(8,128)S(1)} custom-call(s32[1]{0:T(128)} %bitcast.rank_ref, f32[32]{0:T(128)} %coef_ref.11, f32[64,2048]{1,0:T(8,128)S(1)} %shard_map.107.field_ref, f32[64,2048]{1,0:T(8,128)S(1)} %get-tuple-element.40.rhs_ref, f32[1,2048]{1,0:T(1,128)S(1)} %get-tuple-element.32.mass_ref, ...), custom_call_target="tpu_custom_call" | custom-call | flops 5000000000 | bytes 1048576 | tf_op jit(solution)/shard_map/pallas_call | solution.py:613
  60.5 0.0 collective-permute-done.5.second_ref
  60.5 0.0 collective-permute-done.4.first_ref
  60.5 0.0 all-to-all-done.1.parts_ref
  60.6 1.3 %shard_map.110 = (f32[64,2048]{1,0:T(8,128)S(1)}, bf16[32,56,128]{2,1,0:T(8,128)(2,1)}, bf16[64,128]{1,0:T(8,128)(2,1)S(1)}, bf16[64,128]{1,0:T(8,128)(2,1)S(1)}) custom-call(s32[1]{0:T(128)} %bitcast.rank_ref, s32[3,192]{1,0:T(4,128)S(1)} %get-tuple-element.29.own_map_ref, s32[8,512]{1,0:T(8,128)S(1)} %get-tuple-element.30.nodes_ref, ...), custom_call_target="tpu_custom_call" | custom-call | flops 1000000000 | bytes 1048576 | tf_op jit(solution)/shard_map/pallas_call | solution.py:701
  61.9 2.7 %all-to-all-start.2 = ((bf16[32,56,128]{2,1,0:T(8,128)(2,1)}), bf16[32,56,128]{2,1,0:T(8,128)(2,1)S(1)}, u32[]{:S(2)}, u32[]{:S(2)}) async-start(bf16[32,56,128]{2,1,0:T(8,128)(2,1)} %get-tuple-element.45), calls=%async_computation.2 | async-start | bytes 917504 | tf_op jit(solution)/shard_map/all_to_all | solution.py:602
  64.5 0.3 collective-permute-start.6
  64.8 6.3 %collective-permute-start.7 = (bf16[64,128]{1,0:T(8,128)(2,1)S(1)}, bf16[64,128]{1,0:T(8,128)(2,1)S(1)}, u32[]{:S(2)}, u32[]{:S(2)}) collective-permute-start(bf16[64,128]{1,0:T(8,128)(2,1)S(1)} %get-tuple-element.48), channel_id=1, source_target_pairs={{1,2},{2,1},{3,4},{4,3},{5,6},{6,5},{7,8},{8,7},{9,10},{10,9},{11,... | collective-permute-start | bytes 49160 | tf_op jit(solution)/shard_map/ppermute | solution.py:591
  71.1 5.7 %shard_map.111.field_ref = f32[64,2048]{1,0:T(8,128)S(1)} custom-call(s32[1]{0:T(128)} %bitcast.rank_ref, f32[32]{0:T(128)} %coef_ref.11, f32[64,2048]{1,0:T(8,128)S(1)} %get-tuple-element.46.field_ref, f32[64,2048]{1,0:T(8,128)S(1)} %get-tuple-element.35.forcing_ref.rhs_ref, f32[1,2048]{1,0:T(1,128)S(1)} %get-tuple-element.32.mass_ref, ...), custom_call_target="tpu_custom_call" | custom-call | flops 5000000000 | bytes 1048576 | tf_op jit(solution)/shard_map/pallas_call | solution.py:613
  76.8 1.6 %all-to-all-done.2.chunk_ref = bf16[32,56,128]{2,1,0:T(8,128)(2,1)S(1)} async-done(((bf16[32,56,128]{2,1,0:T(8,128)(2,1)}), bf16[32,56,128]{2,1,0:T(8,128)(2,1)S(1)}, u32[]{:S(2)}, u32[]{:S(2)}) %all-to-all-start.2) | async-done | bytes 458784 | tf_op jit(solution)/shard_map/all_to_all | solution.py:602
  78.4 4.0 %shard_map.115 = f32[4,64,192]{2,1,0:T(8,128)} custom-call(s32[3,1536]{1,0:T(4,128)S(1)} %get-tuple-element.43.map_ref, bf16[32,56,128]{2,1,0:T(8,128)(2,1)S(1)} %all-to-all-done.2.chunk_ref, bf16[8,2,192,768]{3,2,1,0:T(8,128)(2,1)} %get-tuple-element.53.tile_ref), custom_call_target="tpu_custom_call" | custom-call | flops 2000000000 | bytes 1048576 | tf_op jit(solution)/shard_map/pallas_call | solution.py:712
  82.4 4.7 %all-to-all-start.3 = ((f32[4,64,192]{2,1,0:T(8,128)}), f32[4,64,192]{2,1,0:T(8,128)S(1)}, u32[]{:S(2)}, u32[]{:S(2)}) async-start(f32[4,64,192]{2,1,0:T(8,128)} %shard_map.115), calls=%async_computation.3 | async-start | bytes 524288 | tf_op jit(solution)/shard_map/all_to_all | solution.py:648
  87.1 0.0 collective-permute-done.6.first_ref
  87.1 0.0 collective-permute-done.7.second_ref
  87.1 0.4 shard_map.112
  87.5 0.1 collective-permute-start.8
  87.6 3.4 %collective-permute-start.9 = (bf16[64,128]{1,0:T(8,128)(2,1)S(1)}, bf16[64,128]{1,0:T(8,128)(2,1)S(1)}, u32[]{:S(2)}, u32[]{:S(2)}) collective-permute-start(bf16[64,128]{1,0:T(8,128)(2,1)S(1)} %get-tuple-element.52), channel_id=1, source_target_pairs={{1,2},{2,1},{3,4},{4,3},{5,6},{6,5},{7,8},{8,7},{9,10},{10,9},{11,... | collective-permute-start | bytes 49160 | tf_op jit(solution)/shard_map/ppermute | solution.py:591
  91.0 5.7 %shard_map.113.field_ref = f32[64,2048]{1,0:T(8,128)S(1)} custom-call(s32[1]{0:T(128)} %bitcast.rank_ref, f32[32]{0:T(128)} %coef_ref.11, f32[64,2048]{1,0:T(8,128)S(1)} %get-tuple-element.49.field_ref, f32[64,2048]{1,0:T(8,128)S(1)} %get-tuple-element.50.rhs_ref, f32[1,2048]{1,0:T(1,128)S(1)} %get-tuple-element.32.mass_ref, ...), custom_call_target="tpu_custom_call" | custom-call | flops 5000000000 | bytes 1048576 | tf_op jit(solution)/shard_map/pallas_call | solution.py:613
  96.7 0.0 collective-permute-done.8.more_refs_0_
  96.8 0.0 collective-permute-done.9.more_refs_1_
  96.8 6.0 %collective-permute-start.11 = (bf16[64,128]{1,0:T(8,128)(2,1)S(1)}, bf16[64,128]{1,0:T(8,128)(2,1)S(1)}, u32[]{:S(2)}, u32[]{:S(2)}) collective-permute-start(bf16[64,128]{1,0:T(8,128)(2,1)S(1)} %get-tuple-element.54), channel_id=1, source_target_pairs={{1,2},{2,1},{3,4},{4,3},{5,6},{6,5},{7,8},{8,7},{9,10},{10,9},{11,... | collective-permute-start | bytes 49160 | tf_op jit(solution)/shard_map/ppermute | solution.py:591
  102.8 0.1 collective-permute-start.10
  102.9 5.8 %shard_map.114.field_ref = f32[64,2048]{1,0:T(8,128)S(1)} custom-call(s32[1]{0:T(128)} %bitcast.rank_ref, f32[32]{0:T(128)} %coef_ref.11, f32[64,2048]{1,0:T(8,128)S(1)} %shard_map.113.field_ref, f32[64,2048]{1,0:T(8,128)S(1)} %get-tuple-element.50.rhs_ref, f32[1,2048]{1,0:T(1,128)S(1)} %get-tuple-element.32.mass_ref, ...), custom_call_target="tpu_custom_call" | custom-call | flops 5000000000 | bytes 1048576 | tf_op jit(solution)/shard_map/pallas_call | solution.py:613
  108.7 0.0 collective-permute-done.11.second_ref
  108.7 0.0 collective-permute-done.10.first_ref
  108.7 0.0 all-to-all-done.3.parts_ref
  108.7 0.9 shard_map.116
  (3 shorter events, 0.0 us)
Async XLA Ops:
  3.9 21.4 %all-to-all-start = ((bf16[32,64,128]{2,1,0:T(8,128)(2,1)}), bf16[32,64,128]{2,1,0:T(8,128)(2,1)S(1)}, u32[]{:S(2)}, u32[]{:S(2)}) async-start(bf16[32,64,128]{2,1,0:T(8,128)(2,1)} %get-tuple-element.31), calls=%async_computation | async-start | bytes 1048576 | tf_op jit(solution)/shard_map/all_to_all | solution.py:602
  10.0 12.6 %collective-permute-start = (bf16[64,128]{1,0:T(8,128)(2,1)S(1)}, bf16[64,128]{1,0:T(8,128)(2,1)S(1)}, u32[]{:S(2)}, u32[]{:S(2)}) collective-permute-start(bf16[64,128]{1,0:T(8,128)(2,1)S(1)} %get-tuple-element.37), channel_id=1, source_target_pairs={{0,1},{1,0},{2,3},{3,2},{4,5},{5,4},{6,7},{7,6},{8,9},{9,8},{10,11... | collective-permute-start | bytes 49160 | tf_op jit(solution)/shard_map/ppermute | solution.py:591
  10.2 13.4 %collective-permute-start.1 = (bf16[64,128]{1,0:T(8,128)(2,1)S(1)}, bf16[64,128]{1,0:T(8,128)(2,1)S(1)}, u32[]{:S(2)}, u32[]{:S(2)}) collective-permute-start(bf16[64,128]{1,0:T(8,128)(2,1)S(1)} %get-tuple-element.38), channel_id=1, source_target_pairs={{1,2},{2,1},{3,4},{4,3},{5,6},{6,5},{7,8},{8,7},{9,10},{10,9},{11,... | collective-permute-start | bytes 49160 | tf_op jit(solution)/shard_map/ppermute | solution.py:591
  25.7 23.2 %collective-permute-start.2 = (bf16[64,128]{1,0:T(8,128)(2,1)S(1)}, bf16[64,128]{1,0:T(8,128)(2,1)S(1)}, u32[]{:S(2)}, u32[]{:S(2)}) collective-permute-start(bf16[64,128]{1,0:T(8,128)(2,1)S(1)} %get-tuple-element.41), channel_id=1, source_target_pairs={{0,1},{1,0},{2,3},{3,2},{4,5},{5,4},{6,7},{7,6},{8,9},{9,8},{10,11... | collective-permute-start | bytes 49160 | tf_op jit(solution)/shard_map/ppermute | solution.py:591
  26.0 23.0 %collective-permute-start.3 = (bf16[64,128]{1,0:T(8,128)(2,1)S(1)}, bf16[64,128]{1,0:T(8,128)(2,1)S(1)}, u32[]{:S(2)}, u32[]{:S(2)}) collective-permute-start(bf16[64,128]{1,0:T(8,128)(2,1)S(1)} %get-tuple-element.42), channel_id=1, source_target_pairs={{1,2},{2,1},{3,4},{4,3},{5,6},{6,5},{7,8},{8,7},{9,10},{10,9},{11,... | collective-permute-start | bytes 49160 | tf_op jit(solution)/shard_map/ppermute | solution.py:591
  39.7 20.9 %all-to-all-start.1 = ((f32[4,64,192]{2,1,0:T(8,128)}), f32[4,64,192]{2,1,0:T(8,128)S(1)}, u32[]{:S(2)}, u32[]{:S(2)}) async-start(f32[4,64,192]{2,1,0:T(8,128)} %get-tuple-element.44), calls=%async_computation.1 | async-start | bytes 524288 | tf_op jit(solution)/shard_map/all_to_all | solution.py:648
  49.0 11.5 %collective-permute-start.5 = (bf16[64,128]{1,0:T(8,128)(2,1)S(1)}, bf16[64,128]{1,0:T(8,128)(2,1)S(1)}, u32[]{:S(2)}, u32[]{:S(2)}) collective-permute-start(bf16[64,128]{1,0:T(8,128)(2,1)S(1)} %get-tuple-element.56), channel_id=1, source_target_pairs={{1,2},{2,1},{3,4},{4,3},{5,6},{6,5},{7,8},{8,7},{9,10},{10,9},{11,... | collective-permute-start | bytes 49160 | tf_op jit(solution)/shard_map/ppermute | solution.py:591
  54.7 5.9 %collective-permute-start.4 = (bf16[64,128]{1,0:T(8,128)(2,1)S(1)}, bf16[64,128]{1,0:T(8,128)(2,1)S(1)}, u32[]{:S(2)}, u32[]{:S(2)}) collective-permute-start(bf16[64,128]{1,0:T(8,128)(2,1)S(1)} %get-tuple-element.57), channel_id=1, source_target_pairs={{0,1},{1,0},{2,3},{3,2},{4,5},{5,4},{6,7},{7,6},{8,9},{9,8},{10,11... | collective-permute-start | bytes 49160 | tf_op jit(solution)/shard_map/ppermute | solution.py:591
  61.9 16.6 %all-to-all-start.2 = ((bf16[32,56,128]{2,1,0:T(8,128)(2,1)}), bf16[32,56,128]{2,1,0:T(8,128)(2,1)S(1)}, u32[]{:S(2)}, u32[]{:S(2)}) async-start(bf16[32,56,128]{2,1,0:T(8,128)(2,1)} %get-tuple-element.45), calls=%async_computation.2 | async-start | bytes 917504 | tf_op jit(solution)/shard_map/all_to_all | solution.py:602
  64.5 22.6 %collective-permute-start.6 = (bf16[64,128]{1,0:T(8,128)(2,1)S(1)}, bf16[64,128]{1,0:T(8,128)(2,1)S(1)}, u32[]{:S(2)}, u32[]{:S(2)}) collective-permute-start(bf16[64,128]{1,0:T(8,128)(2,1)S(1)} %get-tuple-element.47), channel_id=1, source_target_pairs={{0,1},{1,0},{2,3},{3,2},{4,5},{5,4},{6,7},{7,6},{8,9},{9,8},{10,11... | collective-permute-start | bytes 49160 | tf_op jit(solution)/shard_map/ppermute | solution.py:591
  64.8 22.3 %collective-permute-start.7 = (bf16[64,128]{1,0:T(8,128)(2,1)S(1)}, bf16[64,128]{1,0:T(8,128)(2,1)S(1)}, u32[]{:S(2)}, u32[]{:S(2)}) collective-permute-start(bf16[64,128]{1,0:T(8,128)(2,1)S(1)} %get-tuple-element.48), channel_id=1, source_target_pairs={{1,2},{2,1},{3,4},{4,3},{5,6},{6,5},{7,8},{8,7},{9,10},{10,9},{11,... | collective-permute-start | bytes 49160 | tf_op jit(solution)/shard_map/ppermute | solution.py:591
  82.4 26.3 %all-to-all-start.3 = ((f32[4,64,192]{2,1,0:T(8,128)}), f32[4,64,192]{2,1,0:T(8,128)S(1)}, u32[]{:S(2)}, u32[]{:S(2)}) async-start(f32[4,64,192]{2,1,0:T(8,128)} %shard_map.115), calls=%async_computation.3 | async-start | bytes 524288 | tf_op jit(solution)/shard_map/all_to_all | solution.py:648
  87.5 9.2 %collective-permute-start.8 = (bf16[64,128]{1,0:T(8,128)(2,1)S(1)}, bf16[64,128]{1,0:T(8,128)(2,1)S(1)}, u32[]{:S(2)}, u32[]{:S(2)}) collective-permute-start(bf16[64,128]{1,0:T(8,128)(2,1)S(1)} %get-tuple-element.51), channel_id=1, source_target_pairs={{0,1},{1,0},{2,3},{3,2},{4,5},{5,4},{6,7},{7,6},{8,9},{9,8},{10,11... | collective-permute-start | bytes 49160 | tf_op jit(solution)/shard_map/ppermute | solution.py:591
  87.6 9.1 %collective-permute-start.9 = (bf16[64,128]{1,0:T(8,128)(2,1)S(1)}, bf16[64,128]{1,0:T(8,128)(2,1)S(1)}, u32[]{:S(2)}, u32[]{:S(2)}) collective-permute-start(bf16[64,128]{1,0:T(8,128)(2,1)S(1)} %get-tuple-element.52), channel_id=1, source_target_pairs={{1,2},{2,1},{3,4},{4,3},{5,6},{6,5},{7,8},{8,7},{9,10},{10,9},{11,... | collective-permute-start | bytes 49160 | tf_op jit(solution)/shard_map/ppermute | solution.py:591
  96.8 11.9 %collective-permute-start.11 = (bf16[64,128]{1,0:T(8,128)(2,1)S(1)}, bf16[64,128]{1,0:T(8,128)(2,1)S(1)}, u32[]{:S(2)}, u32[]{:S(2)}) collective-permute-start(bf16[64,128]{1,0:T(8,128)(2,1)S(1)} %get-tuple-element.54), channel_id=1, source_target_pairs={{1,2},{2,1},{3,4},{4,3},{5,6},{6,5},{7,8},{8,7},{9,10},{10,9},{11,... | collective-permute-start | bytes 49160 | tf_op jit(solution)/shard_map/ppermute | solution.py:591
  102.8 5.8 %collective-permute-start.10 = (bf16[64,128]{1,0:T(8,128)(2,1)S(1)}, bf16[64,128]{1,0:T(8,128)(2,1)S(1)}, u32[]{:S(2)}, u32[]{:S(2)}) collective-permute-start(bf16[64,128]{1,0:T(8,128)(2,1)S(1)} %get-tuple-element.55), channel_id=1, source_target_pairs={{0,1},{1,0},{2,3},{3,2},{4,5},{5,4},{6,7},{7,6},{8,9},{9,8},{10,11... | collective-permute-start | bytes 49160 | tf_op jit(solution)/shard_map/ppermute | solution.py:591

commit v4 on v3

--- a/solution.py
+++ b/solution.py
@@ -25,7 +25,6 @@
 BF16 = jnp.bfloat16
 
 SIN_POLY = (3.14159264, -5.16771008, 2.55007752, -0.59829129, 0.07765766)
-COS_POLY = (0.99999995, -4.93479283, 4.05841135, -1.33187657, 0.21968961)
 
 ROUNDER = 1.5 * 2.0**23
 MIB = 1024 * 1024
@@ -123,15 +122,15 @@
     return half, slot - half * rows
 
 
-def trace_rows(field, nodes, parts, brow, used):
+def trace_rows(field, nodes, parts, groups, used):
     turned = jnp.transpose(gather_nodes(field, nodes, parts))
-    span = turned.shape[0] // brow
-    return [
-        jnp.concatenate(
-            [turned[r * span : r * span + used], turned[r * span + used : r * span + 2 * used]], axis=1
+    pieces = []
+    for group in range(groups):
+        base = group * HALVES * used
+        pieces.append(
+            jnp.concatenate([turned[base : base + used], turned[base + used : base + 2 * used]], axis=1)
         )
-        for r in range(brow)
-    ]
+    return pieces
 
 
 def own_panels(map_ref, rank, panel_dev):
@@ -151,25 +150,37 @@
     return jnp.concatenate([found[:rows], found[rows:]], axis=1).reshape(devices, LOAD_ROWS, LANES)
 
 
-def node_tables(map_ref, rank, brow, bcol, panel_dev, slot_rows, stride):
+def node_tables(map_ref, rank, brow, bcol, panel_dev, slot_rows):
     row_panels = bcol * panel_dev
-    row_slots = -(-HALVES * bcol * stride // LANES) * LANES
+    trace_slots, load_slots = table_lanes(brow, bcol, slot_rows)
     lane = lax.broadcasted_iota(jnp.int32, (1, row_panels), 1).astype(F32)
     block = jnp.floor((lane + 0.5) * (1.0 / panel_dev)).astype(jnp.int32)
     row_id = lax.broadcasted_iota(jnp.int32, (8, row_panels), 0)
-    tables = []
+    traces = None
+    loads = []
     for r in range(brow):
         span = slice(r * row_panels, (r + 1) * row_panels)
         owner, slot, node = map_ref[0:1, span], map_ref[1:2, span], map_ref[2:3, span]
         half, low = halves_of(slot, slot_rows)
-        key = jnp.where(owner == rank, half * (bcol * stride) + block * stride + low, -1)
+        own = owner == rank
         values = jnp.where(
             row_id == 0, high_part(node, 256), jnp.where(row_id == 1, low_part(node, 256), 1)
         ).astype(F32).astype(BF16)
-        found = dot_nt(values, one_hot_rows(key, row_slots))
+        key = ((block * HALVES + half) * brow + r) * slot_rows + low
+        found = dot_nt(values, one_hot_rows(jnp.where(own, key, -1), trace_slots))
+        traces = found if traces is None else traces + found
+        key = (half * bcol + block) * LOAD_ROWS + low
+        loads.append(dot_nt(values, one_hot_rows(jnp.where(own, key, -1), load_slots // brow)))
+    tables = []
+    for found in (traces, jnp.concatenate(loads, axis=1)):
         table = jnp.where(found[2:3] > 0.5, found[0:1] * 256.0 + found[1:2], -1.0)
         tables.append(table.astype(jnp.int32))
-    return jnp.concatenate(tables, axis=1)
+    return tables
+
+
+def table_lanes(brow, bcol, slot_rows):
+    trace_slots = -(-HALVES * brow * bcol * slot_rows // LANES) * LANES
+    return trace_slots, brow * (-(-HALVES * bcol * LOAD_ROWS // LANES) * LANES)
 
 
 def point_rows(points):
@@ -187,16 +198,14 @@
     return value
 
 
-def write_chunks(chunk_ref, pieces, loads, bcol, points=None):
+def write_chunks(chunk_ref, pieces, loads, points=None):
     used = pieces[0].shape[0]
-    for r, piece in enumerate(pieces):
-        for c in range(bcol):
-            device = r * bcol + c
-            rows = [piece, loads[device]] + ([] if points is None else [points])
-            left = chunk_ref.shape[1] - used - LOAD_ROWS - (0 if points is None else POINT_ROWS)
-            if left:
-                rows.append(jnp.zeros((left, LANES), F32))
-            chunk_ref[device] = jnp.concatenate(rows, axis=0).astype(BF16)
+    for device in range(chunk_ref.shape[0]):
+        rows = [pieces[device % len(pieces)], loads[device]] + ([] if points is None else [points])
+        left = chunk_ref.shape[1] - sum(piece.shape[0] for piece in rows)
+        if left:
+            rows.append(jnp.zeros((left, LANES), F32))
+        chunk_ref[device] = jnp.concatenate(rows, axis=0).astype(BF16)
 
 
 def write_rims(field, even, first_ref, second_ref):
@@ -209,13 +218,17 @@
 def setup_kernel(
     parts, brow, bcol, panel_dev, slot_rows, rank_ref, map_ref, field_ref, potential_ref, points_ref,
     element_nodes_ref, element_matrix_ref, node_mass_ref,
-    nodes_ref, load_nodes_ref, row_map_ref, own_map_ref, keys_ref, matrix_ref, mass_ref,
+    nodes_ref, load_nodes_ref, source_map_ref, own_map_ref, keys_ref, matrix_ref, mass_ref,
     chunk_ref, rim_first_ref, rim_second_ref,
 ):
     rank = rank_ref[0]
-    row_panels = bcol * panel_dev
-    base = pl.multiple_of(high_part(rank, bcol) * row_panels, LANES)
-    row_map_ref[...] = map_ref[:, pl.ds(base, row_panels)]
+    source_map_ref[...] = jnp.concatenate(
+        [
+            own_panels(map_ref, r * bcol + low_part(rank, bcol), panel_dev)
+            for r in range(brow)
+        ],
+        axis=1,
+    )
     own_map = own_panels(map_ref, rank, panel_dev)
     own_map_ref[...] = own_map
     keys_ref[...] = jnp.zeros_like(keys_ref)
@@ -223,15 +236,14 @@
     matrix_ref[...] = jnp.zeros_like(matrix_ref)
     matrix_ref[: element_matrix_ref.shape[0], : element_matrix_ref.shape[1]] = element_matrix_ref[...]
     mass_ref[...] = node_mass_ref[...]
-    tables = functools.partial(node_tables, map_ref, rank, brow, bcol, panel_dev, slot_rows)
-    nodes = tables(slot_rows)
+    nodes, load_nodes = node_tables(map_ref, rank, brow, bcol, panel_dev, slot_rows)
     nodes_ref[...] = jnp.broadcast_to(nodes, nodes_ref.shape)
-    load_nodes_ref[...] = jnp.broadcast_to(tables(LOAD_ROWS), load_nodes_ref.shape)
+    load_nodes_ref[...] = jnp.broadcast_to(load_nodes, load_nodes_ref.shape)
     field = field_ref[...]
     write_rims(field, low_part(rank, 2) == 0, rim_first_ref, rim_second_ref)
     loads = load_rows(potential_ref[...], own_map, brow * bcol, slot_rows)
-    pieces = trace_rows(field, nodes, parts, brow, bcol * slot_rows)
-    write_chunks(chunk_ref, pieces, loads, bcol, point_rows(points_ref[...].astype(F32)))
+    pieces = trace_rows(field, nodes, parts, bcol, brow * slot_rows)
+    write_chunks(chunk_ref, pieces, loads, point_rows(points_ref[...].astype(F32)))
 
 
 def rim_correction(value, even, first_ref, second_ref, mass, weight):
@@ -393,8 +405,8 @@
     out_ref[...] = field
     write_rims(field, even, rim_first_ref, rim_second_ref)
     loads = load_rows(total(parts_ref), own_map_ref[...], brow * bcol, slot_rows)
-    pieces = trace_rows(field, nodes_ref[0:1, :], parts, brow, bcol * slot_rows)
-    write_chunks(chunk_ref, pieces, loads, bcol)
+    pieces = trace_rows(field, nodes_ref[0:1, :], parts, bcol, brow * slot_rows)
+    write_chunks(chunk_ref, pieces, loads)
 
 
 def last_kernel(
@@ -413,7 +425,7 @@
     lane = lax.broadcasted_iota(jnp.int32, (1, panels), 1).astype(F32)
     block = jnp.floor((lane + 0.5) * (1.0 / panel_dev)).astype(jnp.int32)
     traces = chunk_ref[...].astype(F32)
-    for group in range(bcol // BLOCKS):
+    for group in range(brow // BLOCKS):
         span = slice(group * panels, (group + 1) * panels)
         owner, slot = map_ref[0:1, span], map_ref[1:2, span]
         half, low = halves_of(slot, slot_rows)
@@ -456,7 +468,7 @@
     soften = 0.5 * float(count_all) ** (-1.0 / 3.0)
     each = POINT_ROWS // 3
     row_index, col_index = high_part(rank_ref[0], bcol), low_part(rank_ref[0], bcol)
-    start = bcol * slot_rows + LOAD_ROWS
+    start = brow * slot_rows + LOAD_ROWS
     block = pl.program_id(0)
 
     def points_of(device):
@@ -467,7 +479,7 @@
 
     @pl.when(block == 0)
     def prepare():
-        near = [points_of(r * bcol + col_index) for r in range(brow)]
+        near = [points_of(row_index * bcol + c) for c in range(bcol)]
         axes = []
         for axis in range(3):
             rows = []
@@ -486,7 +498,7 @@
                 density_ref[group * BLOCKS + k] = density[:, span]
                 turned_ref[group * BLOCKS + k] = turned[:, span]
 
-    piece = points_of(row_index * bcol + block)
+    piece = points_of(block * bcol + col_index)
     axes = [
         jnp.concatenate([piece[axis * each + part : axis * each + part + 1] for part in range(each)], axis=1)
         for axis in range(3)
@@ -505,23 +517,21 @@
         for factor in SIN_POLY[-2::-1]:
             sine = sine * z + factor
         sine = sine * turns
-        cosine = jnp.full_like(z, COS_POLY[-1])
-        for factor in COS_POLY[-2::-1]:
-            cosine = cosine * z + factor
-        double = sine * (inverse * (2.0 / math.sqrt(float(count_all))))
-        built_ref[block, 0, top : top + step] = (
-            inverse * (1.0 / math.sqrt(float(count_all))) - sine * double
-        ).astype(BF16)
-        built_ref[block, 1, top : top + step] = (cosine * double).astype(BF16)
+        rest = 1.0 - sine * sine
+        safe = jnp.maximum(rest, 1e-12)
+        cosine = safe * lax.rsqrt(safe)
+        double = inverse * (2.0 / math.sqrt(float(count_all)))
+        built_ref[block, 0, top : top + step] = ((rest - 0.5) * double).astype(BF16)
+        built_ref[block, 1, top : top + step] = (sine * cosine * double).astype(BF16)
     copy_of(block).start()
     sum_ref[...] += dot(density_ref[block], built_ref[block, 0]) + dot(
         turned_ref[block], built_ref[block, 1]
     )
 
-    @pl.when(block == bcol - 1)
+    @pl.when(block == brow - 1)
     def end():
         write_parts(out_ref, sum_ref[...], panel_dev)
-        for index in range(bcol):
+        for index in range(brow):
             copy_of(index).wait()
 
 
@@ -530,7 +540,7 @@
 ):
     copies = [
         pltpu.make_async_copy(tile_ref.at[block], held_ref.at[block], sems.at[block])
-        for block in range(bcol)
+        for block in range(brow)
     ]
     for copy in copies:
         copy.start()
@@ -563,8 +573,8 @@
     devices = brow * bcol
     capacity = max(2, 2 * panel_dev // devices)
     slot_rows = -(-capacity // HALVES)
-    used = bcol * slot_rows
-    assert slot_rows <= LOAD_ROWS and columns * HALVES == LANES and bcol % BLOCKS == 0
+    used = brow * slot_rows
+    assert slot_rows <= LOAD_ROWS and columns * HALVES == LANES and brow % BLOCKS == 0
     parts = 256 // columns
     width = count // parts
     row_panels = bcol * panel_dev
@@ -584,9 +594,6 @@
     def chunk_shape(rows, unit):
         return shape_of((devices, -(-rows // unit) * unit, LANES), BF16)
 
-    def table_shape(stride):
-        return 8, brow * (-(-HALVES * bcol * stride // LANES) * LANES)
-
     def exchange(first, second):
         return lax.ppermute(first, AXES, even_pairs), lax.ppermute(second, AXES, odd_pairs)
 
@@ -603,7 +610,7 @@
 
     hbm = pl.BlockSpec(memory_space=pltpu.HBM)
     hot_shape = (elements // GROUP, width, GROUP * LANES)
-    tile_shape = (bcol, HALVES, panel_dev, brow * panel_dev)
+    tile_shape = (brow, HALVES, panel_dev, bcol * panel_dev)
 
     def sweep(field, rhs, weight, halo=(), weight_before=None, keep=False):
         rows = parts * columns
@@ -640,24 +647,25 @@
             out_specs=(vmem,) * 4,
         )(rank, *in_vmem(load_nodes), chunks, *in_vmem(forcing_kept), field, *halo, *in_vmem(mass))
 
-    parts_shape = shape_of((brow, columns, panel_dev), F32)
+    parts_shape = shape_of((bcol, columns, panel_dev), F32)
     sizes = (brow, bcol, panel_dev, slot_rows)
     tile_mib = -(-(2 * math.prod(tile_shape)) // MIB)
 
     def swap_parts(parts_out):
-        return lax.all_to_all(parts_out, "brow", split_axis=0, concat_axis=0, tiled=True)
-
-    (nodes, load_nodes, row_map, own_map, keys, matrix, mass, chunks, *rim) = call(
+        return lax.all_to_all(parts_out, "bcol", split_axis=0, concat_axis=0, tiled=True)
+
+    trace_slots, load_slots = table_lanes(brow, bcol, slot_rows)
+    (nodes, load_nodes, source_map, own_map, keys, matrix, mass, chunks, *rim) = call(
         functools.partial(setup_kernel, parts, brow, bcol, panel_dev, slot_rows),
         (
-            kept(table_shape(slot_rows), jnp.int32),
-            kept(table_shape(LOAD_ROWS), jnp.int32),
-            kept((3, row_panels), jnp.int32),
+            kept((8, trace_slots), jnp.int32),
+            kept((8, load_slots), jnp.int32),
+            kept((3, brow * panel_dev), jnp.int32),
             kept((3, panel_dev), jnp.int32),
             kept((elements, LANES), jnp.int32),
             kept((LANES, LANES), F32),
             kept((1, count), F32),
-            chunk_shape(used + LOAD_ROWS + POINT_ROWS, 16),
+            chunk_shape(used + LOAD_ROWS + POINT_ROWS, 8),
             kept(rim_shape.shape, BF16),
             kept(rim_shape.shape, BF16),
         ),
@@ -678,20 +686,20 @@
         functools.partial(tile_kernel, *sizes),
         (parts_shape, pltpu.HBM(tile_shape, BF16)),
         8_000_000_000,
-        grid=(bcol,),
+        grid=(brow,),
         limit=16 + tile_mib,
         in_specs=[smem, vmem, vmem],
         out_specs=(vmem, hbm),
         scratch_shapes=[
-            pltpu.VMEM((16, brow * panel_dev), BF16),
-            pltpu.VMEM((bcol, columns, panel_dev), BF16),
-            pltpu.VMEM((bcol, columns, panel_dev), BF16),
-            pltpu.VMEM((panel_dev, brow * panel_dev), F32),
+            pltpu.VMEM((16, bcol * panel_dev), BF16),
+            pltpu.VMEM((brow, columns, panel_dev), BF16),
+            pltpu.VMEM((brow, columns, panel_dev), BF16),
+            pltpu.VMEM((panel_dev, bcol * panel_dev), F32),
             pltpu.VMEM(tile_shape, BF16),
-            pltpu.VMEM((columns, brow * panel_dev), F32),
-            pltpu.SemaphoreType.DMA((bcol,)),
+            pltpu.VMEM((columns, bcol * panel_dev), F32),
+            pltpu.SemaphoreType.DMA((brow,)),
         ],
-    )(rank, *in_vmem(row_map), chunks)
+    )(rank, *in_vmem(source_map), chunks)
     parts_in = swap_parts(parts_out)
     rhs, field, *rim = add_loads(chunks, field, halo, weights[0])
     halo = exchange(*rim)
@@ -716,8 +724,8 @@
         limit=16 + tile_mib,
         in_specs=[vmem, vmem, hbm],
         out_specs=vmem,
-        scratch_shapes=[pltpu.VMEM(tile_shape, BF16), pltpu.SemaphoreType.DMA((bcol,))],
-    )(*in_vmem(row_map), chunks, *in_hbm(tiles))
+        scratch_shapes=[pltpu.VMEM(tile_shape, BF16), pltpu.SemaphoreType.DMA((brow,))],
+    )(*in_vmem(source_map), chunks, *in_hbm(tiles))
     parts_in = swap_parts(parts_out)
     rhs, field, *rim = add_loads(chunks, field, halo, weights[0])
     halo = exchange(*rim)

time: 111 us -> 107 us (0.964)
  waiting for transfers between devices: 4.41 us -> 1.41 us
    all_to_all x2, waiting for transfers between devices: 3.3 us -> 0.01 us  [swap_all(): return lax.all_to_all(chunks, AXES, split_axis=0, concat_axis=0, tiled=True)]
    pallas_call x1, Pallas kernels: 9.95 us -> 8.3 us  [per_device(): call(functools.partial(tile_kernel, *sizes), (parts_shape, pltpu.HBM(tile...]
  transfers between devices with their start and end apart: 16 -> 16, of which waited for: 3 -> 1; matrix products, arithmetic and copies ran while one was open for 0% -> 0% of each run, Pallas kernels for 45% -> 45%
where the time goes in v4:
time: 107 us; the launch traced here: 105 us
  Pallas kernels  54.1 us (51%)
  starting transfers between devices  48.8 us (46%)
  waiting for transfers between devices  1.41 us (1%)
    pallas_call x6, Pallas kernels, sweep(): call(functools.partial(sweep_kernel, parts, weight, weight_before, keep),...  34.9 us
    ppermute x6, starting transfers between devices, exchange(): lax.ppermute(second, AXES, odd_pairs)  31.7 us
    all_to_all x2, starting transfers between devices, swap_all(): return lax.all_to_all(chunks, AXES, split_axis=0, concat_axis=0, tiled=True)  8.43 us
    pallas_call x1, Pallas kernels, per_device(): call(functools.partial(tile_kernel, *sizes), (parts_shape, pltpu.HBM(tile...  8.3 us
    all_to_all x2, starting transfers between devices, swap_parts(): lax.all_to_all(parts_out, 'bcol', split_axis=0, concat_axis=0, tiled=True)  7.21 us
    pallas_call x1, Pallas kernels, per_device(): call(functools.partial(setup_kernel, parts, brow, bcol, panel_dev, slot_r...  4.18 us
    pallas_call x1, Pallas kernels, per_device(): call(functools.partial(potential_kernel, *sizes), parts_shape, 2000000000...  3.72 us
  transfers between devices with their start and end apart: 16, of which 1 were waited for; matrix products, arithmetic and copies ran while one was open for 0% of the time, Pallas kernels for 45%

profile of v4, /device:TPU:4, one launch (start us, length us, event | category | flops | bytes accessed | tf_op | source)
XLA Modules:
  0.0 105.3 jit_solution(18046907110452639454)
XLA Ops:
  0.6 4.2 %shard_map.104 = (s32[8,384]{1,0:T(8,128)S(1)}, s32[8,512]{1,0:T(8,128)S(1)}, s32[3,768]{1,0:T(4,128)S(1)}, s32[3,192]{1,0:T(4,128)S(1)}, s32[32,128]{1,0:T(8,12...) custom-call(s32[1]{0:T(128)} %bitcast.rank_ref, ...), custom_call_target="tpu_custom_call" | custom-call | flops 2000000000 | bytes 1048576 | tf_op jit(solution)/shard_map/pallas_call | solution.py:658
  4.8 6.1 %all-to-all-start = ((bf16[32,40,128]{2,1,0:T(8,128)(2,1)}), bf16[32,40,128]{2,1,0:T(8,128)(2,1)S(1)}, u32[]{:S(2)}, u32[]{:S(2)}) async-start(bf16[32,40,128]{2,1,0:T(8,128)(2,1)} %get-tuple-element.31), calls=%async_computation | async-start | bytes 655360 | tf_op jit(solution)/shard_map/all_to_all | solution.py:609
  10.9 0.2 collective-permute-start
  11.1 6.1 %collective-permute-start.1 = (bf16[64,128]{1,0:T(8,128)(2,1)S(1)}, bf16[64,128]{1,0:T(8,128)(2,1)S(1)}, u32[]{:S(2)}, u32[]{:S(2)}) collective-permute-start(bf16[64,128]{1,0:T(8,128)(2,1)S(1)} %get-tuple-element.38), channel_id=1, source_target_pairs={{1,2},{2,1},{3,4},{4,3},{5,6},{6,5},{7,8},{8,7},{9,10},{10,9},{11,... | collective-permute-start | bytes 49160 | tf_op jit(solution)/shard_map/ppermute | solution.py:598
  17.2 6.2 %shard_map.105 = (f32[64,2048]{1,0:T(8,128)S(1)}, f32[64,2048]{1,0:T(8,128)S(1)}) custom-call(s32[1]{0:T(128)} %bitcast.rank_ref, f32[32]{0:T(128)} %coef_ref.11, f32[64,2048]{1,0:T(8,128)} %field_ref.3, f32[64,2048]{1,0:T(8,128)} %rhs_ref.1, f32[1,2048]{1,0:T(1,128)S(1)} %get-tuple-element.32.mass_ref, s32[32,128]{1,0:T(8,128)S(1)} %get-tuple-element.33.keys_ref, ...), custom_call_target="tpu_custom_call" | custom-call | flops 5000000000 | bytes 1048576 | tf_op jit(solution)/shard_map/pallas_call | solution.py:620
  23.5 0.0 collective-permute-done.first_ref
  23.5 0.0 collective-permute-done.1.second_ref
  23.5 0.0 all-to-all-done.chunk_ref
  23.5 0.4 shard_map.106
  23.9 0.1 collective-permute-start.2
  24.0 3.1 %collective-permute-start.3 = (bf16[64,128]{1,0:T(8,128)(2,1)S(1)}, bf16[64,128]{1,0:T(8,128)(2,1)S(1)}, u32[]{:S(2)}, u32[]{:S(2)}) collective-permute-start(bf16[64,128]{1,0:T(8,128)(2,1)S(1)} %get-tuple-element.42), channel_id=1, source_target_pairs={{1,2},{2,1},{3,4},{4,3},{5,6},{6,5},{7,8},{8,7},{9,10},{10,9},{11,... | collective-permute-start | bytes 49160 | tf_op jit(solution)/shard_map/ppermute | solution.py:598
  27.1 8.3 %shard_map.109 = (f32[8,64,192]{2,1,0:T(8,128)}, bf16[4,2,192,1536]{3,2,1,0:T(8,128)(2,1)}) custom-call(s32[1]{0:T(128)} %bitcast.rank_ref, s32[3,768]{1,0:T(4,128)S(1)} %get-tuple-element.43.map_ref, bf16[32,40,128]{2,1,0:T(8,128)(2,1)S(1)} %all-to-all-done.chunk_ref), custom_call_target="tpu_custom_call" | custom-call | flops 8000000000 | bytes 1048576 | tf_op jit(solution)/shard_map/pallas_call | solution.py:685
  35.4 3.7 %all-to-all-start.1 = ((f32[8,64,192]{2,1,0:T(8,128)}), f32[8,64,192]{2,1,0:T(8,128)S(1)}, u32[]{:S(2)}, u32[]{:S(2)}) async-start(f32[8,64,192]{2,1,0:T(8,128)} %get-tuple-element.44), calls=%async_computation.1 | async-start | bytes 1048576 | tf_op jit(solution)/shard_map/all_to_all | solution.py:655
  39.1 5.7 %shard_map.107.field_ref = f32[64,2048]{1,0:T(8,128)S(1)} custom-call(s32[1]{0:T(128)} %bitcast.rank_ref, f32[32]{0:T(128)} %coef_ref.11, f32[64,2048]{1,0:T(8,128)S(1)} %get-tuple-element.39.field_ref, f32[64,2048]{1,0:T(8,128)S(1)} %get-tuple-element.40.rhs_ref, f32[1,2048]{1,0:T(1,128)S(1)} %get-tuple-element.32.mass_ref, ...), custom_call_target="tpu_custom_call" | custom-call | flops 5000000000 | bytes 1048576 | tf_op jit(solution)/shard_map/pallas_call | solution.py:620
  44.8 0.0 collective-permute-done.2.more_refs_0_
  44.8 0.0 collective-permute-done.3.more_refs_1_
  44.9 7.3 %collective-permute-start.5 = (bf16[64,128]{1,0:T(8,128)(2,1)S(1)}, bf16[64,128]{1,0:T(8,128)(2,1)S(1)}, u32[]{:S(2)}, u32[]{:S(2)}) collective-permute-start(bf16[64,128]{1,0:T(8,128)(2,1)S(1)} %get-tuple-element.56), channel_id=1, source_target_pairs={{1,2},{2,1},{3,4},{4,3},{5,6},{6,5},{7,8},{8,7},{9,10},{10,9},{11,... | collective-permute-start | bytes 49160 | tf_op jit(solution)/shard_map/ppermute | solution.py:598
  52.1 0.1 collective-permute-start.4
  52.2 5.7 %shard_map.108.field_ref = f32[64,2048]{1,0:T(8,128)S(1)} custom-call(s32[1]{0:T(128)} %bitcast.rank_ref, f32[32]{0:T(128)} %coef_ref.11, f32[64,2048]{1,0:T(8,128)S(1)} %shard_map.107.field_ref, f32[64,2048]{1,0:T(8,128)S(1)} %get-tuple-element.40.rhs_ref, f32[1,2048]{1,0:T(1,128)S(1)} %get-tuple-element.32.mass_ref, ...), custom_call_target="tpu_custom_call" | custom-call | flops 5000000000 | bytes 1048576 | tf_op jit(solution)/shard_map/pallas_call | solution.py:620
  58.0 0.0 collective-permute-done.5.second_ref
  58.0 0.0 collective-permute-done.4.first_ref
  58.0 0.0 all-to-all-done.1.parts_ref
  58.0 1.3 %shard_map.110 = (f32[64,2048]{1,0:T(8,128)S(1)}, bf16[32,32,128]{2,1,0:T(8,128)(2,1)}, bf16[64,128]{1,0:T(8,128)(2,1)S(1)}, bf16[64,128]{1,0:T(8,128)(2,1)S(1)}) custom-call(s32[1]{0:T(128)} %bitcast.rank_ref, s32[3,192]{1,0:T(4,128)S(1)} %get-tuple-element.29.own_map_ref, s32[8,384]{1,0:T(8,128)S(1)} %get-tuple-element.30.nodes_ref, ...), custom_call_target="tpu_custom_call" | custom-call | flops 1000000000 | bytes 1048576 | tf_op jit(solution)/shard_map/pallas_call | solution.py:709
  59.3 2.3 %all-to-all-start.2 = ((bf16[32,32,128]{2,1,0:T(8,128)(2,1)}), bf16[32,32,128]{2,1,0:T(8,128)(2,1)S(1)}, u32[]{:S(2)}, u32[]{:S(2)}) async-start(bf16[32,32,128]{2,1,0:T(8,128)(2,1)} %get-tuple-element.45), calls=%async_computation.2 | async-start | bytes 524288 | tf_op jit(solution)/shard_map/all_to_all | solution.py:609
  61.7 0.6 collective-permute-start.6
  62.2 5.9 %collective-permute-start.7 = (bf16[64,128]{1,0:T(8,128)(2,1)S(1)}, bf16[64,128]{1,0:T(8,128)(2,1)S(1)}, u32[]{:S(2)}, u32[]{:S(2)}) collective-permute-start(bf16[64,128]{1,0:T(8,128)(2,1)S(1)} %get-tuple-element.48), channel_id=1, source_target_pairs={{1,2},{2,1},{3,4},{4,3},{5,6},{6,5},{7,8},{8,7},{9,10},{10,9},{11,... | collective-permute-start | bytes 49160 | tf_op jit(solution)/shard_map/ppermute | solution.py:598
  68.1 5.7 %shard_map.111.field_ref = f32[64,2048]{1,0:T(8,128)S(1)} custom-call(s32[1]{0:T(128)} %bitcast.rank_ref, f32[32]{0:T(128)} %coef_ref.11, f32[64,2048]{1,0:T(8,128)S(1)} %get-tuple-element.46.field_ref, f32[64,2048]{1,0:T(8,128)S(1)} %get-tuple-element.35.forcing_ref.rhs_ref, f32[1,2048]{1,0:T(1,128)S(1)} %get-tuple-element.32.mass_ref, ...), custom_call_target="tpu_custom_call" | custom-call | flops 5000000000 | bytes 1048576 | tf_op jit(solution)/shard_map/pallas_call | solution.py:620
  73.8 0.0 all-to-all-done.2.chunk_ref
  73.8 3.7 %shard_map.115 = f32[8,64,192]{2,1,0:T(8,128)} custom-call(s32[3,768]{1,0:T(4,128)S(1)} %get-tuple-element.43.map_ref, bf16[32,32,128]{2,1,0:T(8,128)(2,1)S(1)} %all-to-all-done.2.chunk_ref, bf16[4,2,192,1536]{3,2,1,0:T(8,128)(2,1)} %get-tuple-element.53.tile_ref), custom_call_target="tpu_custom_call" | custom-call | flops 2000000000 | bytes 1048576 | tf_op jit(solution)/shard_map/pallas_call | solution.py:720
  77.5 3.5 %all-to-all-start.3 = ((f32[8,64,192]{2,1,0:T(8,128)}), f32[8,64,192]{2,1,0:T(8,128)S(1)}, u32[]{:S(2)}, u32[]{:S(2)}) async-start(f32[8,64,192]{2,1,0:T(8,128)} %shard_map.115), calls=%async_computation.3 | async-start | bytes 1048576 | tf_op jit(solution)/shard_map/all_to_all | solution.py:655
  81.1 0.0 collective-permute-done.6.first_ref
  81.1 0.0 collective-permute-done.7.second_ref
  81.1 0.4 shard_map.112
  81.5 0.5 collective-permute-start.8
  82.0 5.3 %collective-permute-start.9 = (bf16[64,128]{1,0:T(8,128)(2,1)S(1)}, bf16[64,128]{1,0:T(8,128)(2,1)S(1)}, u32[]{:S(2)}, u32[]{:S(2)}) collective-permute-start(bf16[64,128]{1,0:T(8,128)(2,1)S(1)} %get-tuple-element.52), channel_id=1, source_target_pairs={{1,2},{2,1},{3,4},{4,3},{5,6},{6,5},{7,8},{8,7},{9,10},{10,9},{11,... | collective-permute-start | bytes 49160 | tf_op jit(solution)/shard_map/ppermute | solution.py:598
  87.3 5.7 %shard_map.113.field_ref = f32[64,2048]{1,0:T(8,128)S(1)} custom-call(s32[1]{0:T(128)} %bitcast.rank_ref, f32[32]{0:T(128)} %coef_ref.11, f32[64,2048]{1,0:T(8,128)S(1)} %get-tuple-element.49.field_ref, f32[64,2048]{1,0:T(8,128)S(1)} %get-tuple-element.50.rhs_ref, f32[1,2048]{1,0:T(1,128)S(1)} %get-tuple-element.32.mass_ref, ...), custom_call_target="tpu_custom_call" | custom-call | flops 5000000000 | bytes 1048576 | tf_op jit(solution)/shard_map/pallas_call | solution.py:620
  93.0 0.0 collective-permute-done.8.more_refs_0_
  93.1 1.4 %collective-permute-done.9.more_refs_1_ = bf16[64,128]{1,0:T(8,128)(2,1)S(1)} collective-permute-done((bf16[64,128]{1,0:T(8,128)(2,1)S(1)}, bf16[64,128]{1,0:T(8,128)(2,1)S(1)}, u32[]{:S(2)}, u32[]{:S(2)}) %collective-permute-start.9) | collective-permute-done | bytes 16416 | tf_op jit(solution)/shard_map/ppermute | solution.py:598
  94.5 4.1 %collective-permute-start.11 = (bf16[64,128]{1,0:T(8,128)(2,1)S(1)}, bf16[64,128]{1,0:T(8,128)(2,1)S(1)}, u32[]{:S(2)}, u32[]{:S(2)}) collective-permute-start(bf16[64,128]{1,0:T(8,128)(2,1)S(1)} %get-tuple-element.54), channel_id=1, source_target_pairs={{1,2},{2,1},{3,4},{4,3},{5,6},{6,5},{7,8},{8,7},{9,10},{10,9},{11,... | collective-permute-start | bytes 49160 | tf_op jit(solution)/shard_map/ppermute | solution.py:598
  98.6 0.1 collective-permute-start.10
  98.7 5.8 %shard_map.114.field_ref = f32[64,2048]{1,0:T(8,128)S(1)} custom-call(s32[1]{0:T(128)} %bitcast.rank_ref, f32[32]{0:T(128)} %coef_ref.11, f32[64,2048]{1,0:T(8,128)S(1)} %shard_map.113.field_ref, f32[64,2048]{1,0:T(8,128)S(1)} %get-tuple-element.50.rhs_ref, f32[1,2048]{1,0:T(1,128)S(1)} %get-tuple-element.32.mass_ref, ...), custom_call_target="tpu_custom_call" | custom-call | flops 5000000000 | bytes 1048576 | tf_op jit(solution)/shard_map/pallas_call | solution.py:620
  104.4 0.0 collective-permute-done.11.second_ref
  104.4 0.0 collective-permute-done.10.first_ref
  104.5 0.0 all-to-all-done.3.parts_ref
  104.5 0.9 shard_map.116
  (3 shorter events, 0.0 us)
Async XLA Ops:
  4.8 18.7 %all-to-all-start = ((bf16[32,40,128]{2,1,0:T(8,128)(2,1)}), bf16[32,40,128]{2,1,0:T(8,128)(2,1)S(1)}, u32[]{:S(2)}, u32[]{:S(2)}) async-start(bf16[32,40,128]{2,1,0:T(8,128)(2,1)} %get-tuple-element.31), calls=%async_computation | async-start | bytes 655360 | tf_op jit(solution)/shard_map/all_to_all | solution.py:609
  10.9 12.6 %collective-permute-start = (bf16[64,128]{1,0:T(8,128)(2,1)S(1)}, bf16[64,128]{1,0:T(8,128)(2,1)S(1)}, u32[]{:S(2)}, u32[]{:S(2)}) collective-permute-start(bf16[64,128]{1,0:T(8,128)(2,1)S(1)} %get-tuple-element.37), channel_id=1, source_target_pairs={{0,1},{1,0},{2,3},{3,2},{4,5},{5,4},{6,7},{7,6},{8,9},{9,8},{10,11... | collective-permute-start | bytes 49160 | tf_op jit(solution)/shard_map/ppermute | solution.py:598
  11.1 12.4 %collective-permute-start.1 = (bf16[64,128]{1,0:T(8,128)(2,1)S(1)}, bf16[64,128]{1,0:T(8,128)(2,1)S(1)}, u32[]{:S(2)}, u32[]{:S(2)}) collective-permute-start(bf16[64,128]{1,0:T(8,128)(2,1)S(1)} %get-tuple-element.38), channel_id=1, source_target_pairs={{1,2},{2,1},{3,4},{4,3},{5,6},{6,5},{7,8},{8,7},{9,10},{10,9},{11,... | collective-permute-start | bytes 49160 | tf_op jit(solution)/shard_map/ppermute | solution.py:598
  23.9 20.9 %collective-permute-start.2 = (bf16[64,128]{1,0:T(8,128)(2,1)S(1)}, bf16[64,128]{1,0:T(8,128)(2,1)S(1)}, u32[]{:S(2)}, u32[]{:S(2)}) collective-permute-start(bf16[64,128]{1,0:T(8,128)(2,1)S(1)} %get-tuple-element.41), channel_id=1, source_target_pairs={{0,1},{1,0},{2,3},{3,2},{4,5},{5,4},{6,7},{7,6},{8,9},{9,8},{10,11... | collective-permute-start | bytes 49160 | tf_op jit(solution)/shard_map/ppermute | solution.py:598
  24.0 20.8 %collective-permute-start.3 = (bf16[64,128]{1,0:T(8,128)(2,1)S(1)}, bf16[64,128]{1,0:T(8,128)(2,1)S(1)}, u32[]{:S(2)}, u32[]{:S(2)}) collective-permute-start(bf16[64,128]{1,0:T(8,128)(2,1)S(1)} %get-tuple-element.42), channel_id=1, source_target_pairs={{1,2},{2,1},{3,4},{4,3},{5,6},{6,5},{7,8},{8,7},{9,10},{10,9},{11,... | collective-permute-start | bytes 49160 | tf_op jit(solution)/shard_map/ppermute | solution.py:598
  35.4 22.6 %all-to-all-start.1 = ((f32[8,64,192]{2,1,0:T(8,128)}), f32[8,64,192]{2,1,0:T(8,128)S(1)}, u32[]{:S(2)}, u32[]{:S(2)}) async-start(f32[8,64,192]{2,1,0:T(8,128)} %get-tuple-element.44), calls=%async_computation.1 | async-start | bytes 1048576 | tf_op jit(solution)/shard_map/all_to_all | solution.py:655
  44.9 13.1 %collective-permute-start.5 = (bf16[64,128]{1,0:T(8,128)(2,1)S(1)}, bf16[64,128]{1,0:T(8,128)(2,1)S(1)}, u32[]{:S(2)}, u32[]{:S(2)}) collective-permute-start(bf16[64,128]{1,0:T(8,128)(2,1)S(1)} %get-tuple-element.56), channel_id=1, source_target_pairs={{1,2},{2,1},{3,4},{4,3},{5,6},{6,5},{7,8},{8,7},{9,10},{10,9},{11,... | collective-permute-start | bytes 49160 | tf_op jit(solution)/shard_map/ppermute | solution.py:598
  52.1 5.8 %collective-permute-start.4 = (bf16[64,128]{1,0:T(8,128)(2,1)S(1)}, bf16[64,128]{1,0:T(8,128)(2,1)S(1)}, u32[]{:S(2)}, u32[]{:S(2)}) collective-permute-start(bf16[64,128]{1,0:T(8,128)(2,1)S(1)} %get-tuple-element.57), channel_id=1, source_target_pairs={{0,1},{1,0},{2,3},{3,2},{4,5},{5,4},{6,7},{7,6},{8,9},{9,8},{10,11... | collective-permute-start | bytes 49160 | tf_op jit(solution)/shard_map/ppermute | solution.py:598
  59.3 14.5 %all-to-all-start.2 = ((bf16[32,32,128]{2,1,0:T(8,128)(2,1)}), bf16[32,32,128]{2,1,0:T(8,128)(2,1)S(1)}, u32[]{:S(2)}, u32[]{:S(2)}) async-start(bf16[32,32,128]{2,1,0:T(8,128)(2,1)} %get-tuple-element.45), calls=%async_computation.2 | async-start | bytes 524288 | tf_op jit(solution)/shard_map/all_to_all | solution.py:609
  61.7 19.4 %collective-permute-start.6 = (bf16[64,128]{1,0:T(8,128)(2,1)S(1)}, bf16[64,128]{1,0:T(8,128)(2,1)S(1)}, u32[]{:S(2)}, u32[]{:S(2)}) collective-permute-start(bf16[64,128]{1,0:T(8,128)(2,1)S(1)} %get-tuple-element.47), channel_id=1, source_target_pairs={{0,1},{1,0},{2,3},{3,2},{4,5},{5,4},{6,7},{7,6},{8,9},{9,8},{10,11... | collective-permute-start | bytes 49160 | tf_op jit(solution)/shard_map/ppermute | solution.py:598
  62.2 18.9 %collective-permute-start.7 = (bf16[64,128]{1,0:T(8,128)(2,1)S(1)}, bf16[64,128]{1,0:T(8,128)(2,1)S(1)}, u32[]{:S(2)}, u32[]{:S(2)}) collective-permute-start(bf16[64,128]{1,0:T(8,128)(2,1)S(1)} %get-tuple-element.48), channel_id=1, source_target_pairs={{1,2},{2,1},{3,4},{4,3},{5,6},{6,5},{7,8},{8,7},{9,10},{10,9},{11,... | collective-permute-start | bytes 49160 | tf_op jit(solution)/shard_map/ppermute | solution.py:598
  77.5 26.9 %all-to-all-start.3 = ((f32[8,64,192]{2,1,0:T(8,128)}), f32[8,64,192]{2,1,0:T(8,128)S(1)}, u32[]{:S(2)}, u32[]{:S(2)}) async-start(f32[8,64,192]{2,1,0:T(8,128)} %shard_map.115), calls=%async_computation.3 | async-start | bytes 1048576 | tf_op jit(solution)/shard_map/all_to_all | solution.py:655
  81.5 11.5 %collective-permute-start.8 = (bf16[64,128]{1,0:T(8,128)(2,1)S(1)}, bf16[64,128]{1,0:T(8,128)(2,1)S(1)}, u32[]{:S(2)}, u32[]{:S(2)}) collective-permute-start(bf16[64,128]{1,0:T(8,128)(2,1)S(1)} %get-tuple-element.51), channel_id=1, source_target_pairs={{0,1},{1,0},{2,3},{3,2},{4,5},{5,4},{6,7},{7,6},{8,9},{9,8},{10,11... | collective-permute-start | bytes 49160 | tf_op jit(solution)/shard_map/ppermute | solution.py:598
  82.0 12.5 %collective-permute-start.9 = (bf16[64,128]{1,0:T(8,128)(2,1)S(1)}, bf16[64,128]{1,0:T(8,128)(2,1)S(1)}, u32[]{:S(2)}, u32[]{:S(2)}) collective-permute-start(bf16[64,128]{1,0:T(8,128)(2,1)S(1)} %get-tuple-element.52), channel_id=1, source_target_pairs={{1,2},{2,1},{3,4},{4,3},{5,6},{6,5},{7,8},{8,7},{9,10},{10,9},{11,... | collective-permute-start | bytes 49160 | tf_op jit(solution)/shard_map/ppermute | solution.py:598
  94.5 10.0 %collective-permute-start.11 = (bf16[64,128]{1,0:T(8,128)(2,1)S(1)}, bf16[64,128]{1,0:T(8,128)(2,1)S(1)}, u32[]{:S(2)}, u32[]{:S(2)}) collective-permute-start(bf16[64,128]{1,0:T(8,128)(2,1)S(1)} %get-tuple-element.54), channel_id=1, source_target_pairs={{1,2},{2,1},{3,4},{4,3},{5,6},{6,5},{7,8},{8,7},{9,10},{10,9},{11,... | collective-permute-start | bytes 49160 | tf_op jit(solution)/shard_map/ppermute | solution.py:598
  98.6 5.9 %collective-permute-start.10 = (bf16[64,128]{1,0:T(8,128)(2,1)S(1)}, bf16[64,128]{1,0:T(8,128)(2,1)S(1)}, u32[]{:S(2)}, u32[]{:S(2)}) collective-permute-start(bf16[64,128]{1,0:T(8,128)(2,1)S(1)} %get-tuple-element.55), channel_id=1, source_target_pairs={{0,1},{1,0},{2,3},{3,2},{4,5},{5,4},{6,7},{7,6},{8,9},{9,8},{10,11... | collective-permute-start | bytes 49160 | tf_op jit(solution)/shard_map/ppermute | solution.py:598
